TPU v7x, 128 devices: a whole 4x4x4 slice. The times are simulated.
128 devices in a mesh: row: 16 (over y, x_lo, core), col: 8 (over z, x_hi).
Axes of the slice: x: 4 (x_hi: 2, x_lo: 2; x = x_hi * 2 + x_lo), y: 4, z: 4, core: 2. Of those that a mesh axis runs over, the one named last changes fastest.
Arguments:
- eigenvectors: float32 [512, 65536], P(('row', 'col')), may hold values from -6 to 6
- reflectors: float32 [8, 256, 65536], P(None, 'col', 'row'), as said below
Outputs:
- backtransformed: float32 [512, 65536], P('col', 'row')
Inputs may be any that keep to these rules, and one draw needn't show every extreme that they name: Row j of reflectors[b] is zero at positions before b * 8192 + j and equals one at that position.
All inputs are finite; a program needn't handle non-finite values.
Results may differ from a plain program's by a relative error of at most 0.0003.
Values sent between devices are 32-bit elements; how exact they have to be, the bound alone decides.
No kernel may reach another device: no remote copies, remote signals or barrier semaphores. Data moves between devices by JAX's collectives and lax.ppermute only.
A program may use at most 128 MiB of HBM per device.

v0:
```python
import jax
import jax.numpy as jnp
from jax import lax
from jax.sharding import PartitionSpec as P

HIGHEST = lax.Precision.HIGHEST


def contract_rows(first_operand, second_operand):
    return lax.dot_general(
        first_operand,
        second_operand,
        (((1,), (1,)), ((), ())),
        precision=HIGHEST,
        preferred_element_type=jnp.float32,
    )


def upper_inverse(factor):
    width = factor.shape[-1]
    identity = jnp.eye(width, dtype=jnp.float32)
    diagonal = jnp.sum(factor * identity, axis=-1)
    strict = factor - factor * identity

    def back_step(count, inverse):
        index = (width - 1 - count).astype(jnp.int32)
        row_part = lax.dynamic_slice_in_dim(strict, index, 1, 1)
        unit_row = lax.dynamic_slice_in_dim(identity, index, 1, 0)
        pivot = lax.dynamic_slice_in_dim(diagonal, index, 1, 1)
        solved = jnp.einsum("bij,bjk->bik", row_part, inverse, precision=HIGHEST)
        value = (unit_row[None, :, :] - solved) / pivot[:, :, None]
        return lax.dynamic_update_slice_in_dim(inverse, value, index, 1)

    return lax.fori_loop(jnp.int32(0), jnp.int32(width), back_step, jnp.zeros_like(factor))


def apply_blocks(current, vectors, inverse, reduce_sum):
    for block_index in range(vectors.shape[0] - 1, -1, -1):
        partial_sum = contract_rows(current, vectors[block_index])
        projection = reduce_sum(partial_sum)
        coefficients = contract_rows(projection, inverse[block_index])
        current = current - jnp.dot(
            coefficients,
            vectors[block_index],
            precision=HIGHEST,
            preferred_element_type=jnp.float32,
        )
    return current


def on_device(eigenvectors, reflectors):
    row_count = lax.axis_size("row")
    column_count = lax.axis_size("col")
    devices = row_count * column_count
    ev_dev, matrix_order = eigenvectors.shape
    slice_rows = matrix_order // devices
    pieces = eigenvectors.reshape(1, ev_dev, devices, slice_rows)
    arrived = lax.all_to_all(pieces, ("row", "col"), split_axis=2, concat_axis=0, tiled=True)
    spread = arrived.reshape(devices * ev_dev, slice_rows)
    vectors = lax.all_to_all(reflectors, "col", split_axis=2, concat_axis=1, tiled=True)
    gram_part = jnp.einsum(
        "bjr,bkr->bjk", vectors, vectors, precision=HIGHEST, preferred_element_type=jnp.float32
    )
    gram_total = lax.psum(gram_part, ("row", "col"))
    width = gram_total.shape[1]
    factor = jnp.triu(gram_total, 1) + 0.5 * gram_total * jnp.eye(width, dtype=jnp.float32)
    inverse = upper_inverse(factor)

    def reduce_sum(partial_sum):
        return lax.psum(partial_sum, ("row", "col"))

    finished = apply_blocks(spread, vectors, inverse, reduce_sum)
    return lax.all_to_all(finished, "col", split_axis=0, concat_axis=1, tiled=True)


def solution(mesh):
    in_specs = (P(("row", "col"), None), P(None, "col", "row"))
    out_specs = P("col", "row")
    return jax.shard_map(
        on_device, mesh=mesh, in_specs=in_specs, out_specs=out_specs, check_vma=False
    )
```

profile of v0, /device:TPU:0, one launch (start us, length us, event | category | flops | bytes accessed | tf_op | source)
XLA Modules:
  0.0 1937.4 jit_solution(12541560706535362927)
XLA Ops:
  6.5 11.1 all-to-all-start
  17.7 10.6 copy.6
  28.3 12.8 reshape.63
  41.1 6.6 all-to-all-start.1
  48.1 50.9 %all-to-all-done.1 = f32[8,1,131072]{2,1,0:T(1,128)} async-done(((f32[8,1,131072]{2,1,0:T(1,128)}), f32[8,1,131072]{2,1,0:T(1,128)}, u32[]{:S(2)}, u32[]{:S(2)}) %all-to-all-start.1) | async-done | bytes 4194336 | tf_op jit(solution)/shard_map/all_to_all | solution.py:60
  99.6 13.7 reduce
  113.3 13.3 reshape.64
  126.6 11.5 copy.7
  138.2 4.2 fusion.32
  142.4 5.3 fusion.34
  149.7 149.1 %all-reduce.24.cloned.1.call-done = (f32[512,256]{1,0:T(8,128)}, f32[8,256,256]{2,1,0:T(8,128)}) async-done(((f32[512,256]{1,0:T(8,128)}, f32[8,256,256]{2,1,0:T(8,128)}), (f32[512,256]{1,0:T(8,128)}, f32[8,256,256]{2,1,0:T(8,128)})) %all-reduce.24.cloned.1.call-update) | async-done | bytes 2621456 | tf_op jit(solution)/shard_map/psum | solution.py:70
  298.8 3.5 multiply_reduce_fusion
  302.6 547.4 %while.12 = (s32[]{:T(128)}, f32[8,256,256]{2,1,0:T(8,128)S(1)}, f32[256,256]{1,0:T(8,128)S(1)}, f32[8,256,256]{2,1,0:T(8,128)}, f32[8,256]{0,1:T(8,128)S(1)}, /*index=5*/s32[]{:T(128)}, s32[]{:T(128)}, s32[]{:T(128)}, s32[]{:T(128)}) while((s32[]{:T(128)}, f32[8,256,256]{2,1,0:T(8,128)S(1)}, f32[256,256]{1,0:T(8,128)S(1)}, ...), condition=%wide.region_4.5_spmd, body=%wide.region_3.4_spmd.sunk | while | flops 6295558 | bytes 2166011 | solution.py:34
  850.6 2.4 convolution_subtract_fusion.7
  855.1 143.1 %all-reduce.10.cloned.1.call-done = f32[512,256]{1,0:T(8,128)} async-done(((f32[512,256]{1,0:T(8,128)}), f32[512,256]{1,0:T(8,128)}) %all-reduce.10.cloned.1.call-update) | async-done | bytes 524304 | tf_op jit(solution)/shard_map/psum | solution.py:70
  1004.9 143.9 %all-reduce.12.cloned.1.call-done = f32[512,256]{1,0:T(8,128)} async-done(((f32[512,256]{1,0:T(8,128)}), f32[512,256]{1,0:T(8,128)}) %all-reduce.12.cloned.1.call-update) | async-done | bytes 524304 | tf_op jit(solution)/shard_map/psum | solution.py:70
  1155.5 143.9 %all-reduce.14.cloned.1.call-done = f32[512,256]{1,0:T(8,128)} async-done(((f32[512,256]{1,0:T(8,128)}), f32[512,256]{1,0:T(8,128)}) %all-reduce.14.cloned.1.call-update) | async-done | bytes 524304 | tf_op jit(solution)/shard_map/psum | solution.py:70
  1301.2 2.1 convolution_subtract_fusion.4
  1306.1 143.9 %all-reduce.16.cloned.1.call-done = f32[512,256]{1,0:T(8,128)} async-done(((f32[512,256]{1,0:T(8,128)}), f32[512,256]{1,0:T(8,128)}) %all-reduce.16.cloned.1.call-update) | async-done | bytes 524304 | tf_op jit(solution)/shard_map/psum | solution.py:70
  1456.9 143.7 %all-reduce.18.cloned.1.call-done = f32[512,256]{1,0:T(8,128)} async-done(((f32[512,256]{1,0:T(8,128)}), f32[512,256]{1,0:T(8,128)}) %all-reduce.18.cloned.1.call-update) | async-done | bytes 524304 | tf_op jit(solution)/shard_map/psum | solution.py:70
  1607.3 143.9 %all-reduce.20.cloned.1.call-done = f32[512,256]{1,0:T(8,128)} async-done(((f32[512,256]{1,0:T(8,128)}), f32[512,256]{1,0:T(8,128)}) %all-reduce.20.cloned.1.call-update) | async-done | bytes 524304 | tf_op jit(solution)/shard_map/psum | solution.py:70
  1753.0 2.1 convolution_subtract_fusion.1
  1757.9 144.0 %all-reduce.22.cloned.1.call-done = f32[512,256]{1,0:T(8,128)} async-done(((f32[512,256]{1,0:T(8,128)}), f32[512,256]{1,0:T(8,128)}) %all-reduce.22.cloned.1.call-update) | async-done | bytes 524304 | tf_op jit(solution)/shard_map/psum | solution.py:70
  1905.6 23.5 %all_to_all.52 = f32[8,64,512]{2,1,0:T(8,128)S(1)} all-to-all(f32[8,64,512]{2,1,0:T(8,128)S(1)} %bitcast.131), channel_id=1, replica_groups=mesh['row'=16,'col'=8] {'col'}, dimensions={0} | all-to-all | bytes 2097152 | tf_op jit(solution)/shard_map/all_to_all | solution.py:73
  (1627 shorter events, 584.1 us)
Async XLA Ops:
  6.5 34.6 %all-to-all-start = ((f32[1,4,128,512]{3,1,0,2:T(4,128)}), f32[1,4,128,512]{3,1,0,2:T(4,128)S(1)}, u32[]{:S(2)}, u32[]{:S(2)}) async-start(f32[1,4,128,512]{3,1,0,2:T(4,128)} %bitcast.134), calls=%async_computation | async-start | bytes 2097152 | tf_op jit(solution)/shard_map/all_to_all | solution.py:58
  41.1 57.9 %all-to-all-start.1 = ((f32[8,1,131072]{2,1,0:T(1,128)}), f32[8,1,131072]{2,1,0:T(1,128)}, u32[]{:S(2)}, u32[]{:S(2)}) async-start(f32[8,1,131072]{2,1,0:T(1,128)} %reshape.63), calls=%async_computation.1 | async-start | bytes 8388608 | tf_op jit(solution)/shard_map/all_to_all | solution.py:60
  47.7 251.1 %all-reduce.24.cloned.1.call-start = ((), (), s32[]{:S(2)}) async-start(), calls=%async_computation.10 | async-start | bytes 5242880 | tf_op jit(solution)/shard_map/psum | solution.py:70
  48.1 99.6 %copy-start.13 = (f32[512,512]{1,0:T(8,128)}, f32[512,512]{1,0:T(8,128)S(1)}, u32[]{:S(2)}) copy-start(f32[512,512]{1,0:T(8,128)S(1)} %reshape.59) | copy-start | bytes 3145732
  142.3 5.4 copy-start.21
  149.5 848.7 %all-reduce.10.cloned.1.call-start = ((), (), s32[]{:S(2)}) async-start(), calls=%async_computation.3 | async-start | bytes 1048576 | tf_op jit(solution)/shard_map/psum | solution.py:70
  302.6 547.4 %copy-start.22 = (f32[512,256]{1,0:T(8,128)S(1)}, f32[512,256]{1,0:T(8,128)}, u32[]{:S(2)}) copy-start(f32[512,256]{1,0:T(8,128)} %get-tuple-element.86) | copy-start | bytes 1572868
  854.8 294.0 %all-reduce.12.cloned.1.call-start = ((), (), s32[]{:S(2)}) async-start(), calls=%async_computation.4 | async-start | bytes 1048576 | tf_op jit(solution)/shard_map/psum | solution.py:70
  1004.8 145.7 %copy-start.2 = (f32[512,512]{1,0:T(8,128)S(1)}, f32[512,512]{1,0:T(8,128)}, u32[]{:S(2)}) copy-start(f32[512,512]{1,0:T(8,128)} %copy-done.1) | copy-start | bytes 3145732
  1004.8 294.6 %all-reduce.14.cloned.1.call-start = ((), (), s32[]{:S(2)}) async-start(), calls=%async_computation.5 | async-start | bytes 1048576 | tf_op jit(solution)/shard_map/psum | solution.py:70
  1148.8 4.8 copy-start.18
  1155.4 145.7 %copy-start.4 = (f32[512,512]{1,0:T(8,128)S(1)}, f32[512,512]{1,0:T(8,128)}, u32[]{:S(2)}) copy-start(f32[512,512]{1,0:T(8,128)} %copy-done.3) | copy-start | bytes 3145732
  1155.4 294.6 %all-reduce.16.cloned.1.call-start = ((), (), s32[]{:S(2)}) async-start(), calls=%async_computation.6 | async-start | bytes 1048576 | tf_op jit(solution)/shard_map/psum | solution.py:70
  1299.4 4.8 copy-start.17
  1306.0 145.7 %copy-start.6 = (f32[512,512]{1,0:T(8,128)S(1)}, f32[512,512]{1,0:T(8,128)}, u32[]{:S(2)}) copy-start(f32[512,512]{1,0:T(8,128)} %copy-done.5) | copy-start | bytes 3145732
  1306.1 294.6 %all-reduce.18.cloned.1.call-start = ((), (), s32[]{:S(2)}) async-start(), calls=%async_computation.7 | async-start | bytes 1048576 | tf_op jit(solution)/shard_map/psum | solution.py:70
  1450.0 4.8 copy-start.16
  1456.6 145.7 %copy-start.8 = (f32[512,512]{1,0:T(8,128)S(1)}, f32[512,512]{1,0:T(8,128)}, u32[]{:S(2)}) copy-start(f32[512,512]{1,0:T(8,128)} %copy-done.7) | copy-start | bytes 3145732
  1456.6 294.6 %all-reduce.20.cloned.1.call-start = ((), (), s32[]{:S(2)}) async-start(), calls=%async_computation.8 | async-start | bytes 1048576 | tf_op jit(solution)/shard_map/psum | solution.py:70
  1600.6 4.8 copy-start.15
  1607.2 145.7 %copy-start.10 = (f32[512,512]{1,0:T(8,128)S(1)}, f32[512,512]{1,0:T(8,128)}, u32[]{:S(2)}) copy-start(f32[512,512]{1,0:T(8,128)} %copy-done.9) | copy-start | bytes 3145732
  1607.3 294.6 %all-reduce.22.cloned.1.call-start = ((), (), s32[]{:S(2)}) async-start(), calls=%async_computation.9 | async-start | bytes 1048576 | tf_op jit(solution)/shard_map/psum | solution.py:70
  1751.2 4.8 copy-start.14
  1757.8 145.7 %copy-start.12 = (f32[512,512]{1,0:T(8,128)S(1)}, f32[512,512]{1,0:T(8,128)}, u32[]{:S(2)}) copy-start(f32[512,512]{1,0:T(8,128)} %copy-done.11) | copy-start | bytes 3145732
  (9 other events, 17.8 us)
Sparse Core Ops, SparseCore 0:
  149.7 149.0 all-reduce.23
  855.0 143.2 all-reduce.9
  1005.0 143.8 all-reduce.11
  1155.6 143.8 all-reduce.13
  1306.2 143.7 all-reduce.15
  1456.8 143.8 all-reduce.17
  1607.4 143.7 all-reduce.19
  1758.0 143.8 all-reduce.21
where the time goes:
time: 1960 us; the launch traced here: 1940 us
  waiting for transfers between devices  1210 us (62%)
  matrix products  549 us (28%)
  local copies, waits for them, and re-layouts  80.3 us (4%)
  other arithmetic  35.8 us (2%)
  blocking collectives  23.5 us (1%)
    psum x8, waiting for transfers between devices, reduce_sum(): return lax.psum(partial_sum, ('row', 'col'))  1160 us
    dot_general x256, matrix products, back_step(): solved = jnp.einsum('bij,bjk->bik', row_part, inverse, precision=HIGHEST)  499 us
    all_to_all x1, waiting for transfers between devices, on_device(): lax.all_to_all(reflectors, 'col', split_axis=2, concat_axis=1, tiled=True)  50.9 us
    unnamed x49, local copies, waits for them, and re-layouts  42.6 us
  transfers between devices with their start and end apart: 10, of which 9 were waited for; matrix products, arithmetic and copies ran while one was open for 1% of the time, Pallas kernels for 0%

commit v1 on v0

v1 whole, which is shorter than its diff:
```python
import jax
import jax.numpy as jnp
from jax import lax
from jax.experimental import pallas as pl
from jax.experimental.pallas import tpu as pltpu
from jax.sharding import Mesh, PartitionSpec as P

AXES = ("y", "xl", "core", "z", "xh")
SIZES = (4, 2, 2, 4, 2)
CHIPS = ("y", "xl", "z", "xh")
COLS = ("z", "xh")
CORE_COLS = ("core", "z", "xh")
SWAP = ((0, 1), (1, 0))

NCHIP = 64
NCOL = 8
NB = 256
GROUP = 4
PAIRS = [(i, j) for i in range(GROUP) for j in range(i, GROUP)]


def place_pieces():
    at, pieces = 0, {}
    for i, j in PAIRS:
        for half in range(2):
            rows = NB // 2 if i == j and half == 0 else NB
            pieces[i, j, half] = (at, rows)
            at += rows
    return at, pieces


ALLROWS, PIECES = place_pieces()
GROWS = ALLROWS // NCHIP
PROWS = 32
ANY = pl.BlockSpec(memory_space=pl.ANY)
F32 = jnp.float32
BF16 = jnp.bfloat16
NT = (((1,), (1,)), ((), ()))
NN = (((1,), (0,)), ((), ()))


def bf16(*shape):
    return jax.ShapeDtypeStruct(shape, BF16)


def f32(*shape):
    return jax.ShapeDtypeStruct(shape, F32)


def split(value):
    high = value.astype(BF16)
    return high, (value - high.astype(F32)).astype(BF16)


def dot3(a, b, dims):
    def one(x, y):
        return lax.dot_general(x, y, dims, preferred_element_type=F32)

    return one(a[0], b[0]) + (one(a[0], b[1]) + one(a[1], b[0]))


def cut_eigenvectors(after_ref, e_ref, out_ref):
    for core in range(2):
        for c in range(NCOL):
            for t in range(4):
                for k in range(8):
                    at = (((k * 2 + core) * NCOL + c) * 4 + t) * 128
                    out_ref[k * NCOL + c, core, t * 4 : t * 4 + 4, :] = e_ref[:, at : at + 128]


def cut_vectors(w_ref, out_ref, done):
    copies = [
        pltpu.make_async_copy(w_ref.at[:, :, c * 512 : c * 512 + 512], out_ref.at[c], done.at[c])
        for c in range(NCOL)
    ]
    for copy in copies:
        copy.start()
    for copy in copies:
        copy.wait()


def split_block(own_ref, sib_ref):
    high, low = [], []
    for ref in (own_ref, sib_ref):
        pair = split(ref[...].reshape(NB, 512))
        high.append(pair[0])
        low.append(pair[1])
    return jnp.concatenate(high, axis=1), jnp.concatenate(low, axis=1)


def inner_products(core_ref, own_ref, sib_ref, buf_ref, high_ref, low_ref):
    def block(j):
        high_ref[j], low_ref[j] = split_block(own_ref, sib_ref)
        for i in range(j + 1):
            value = dot3((high_ref[i], low_ref[i]), (high_ref[j], low_ref[j]), NT)
            for half in range(2):
                at, rows = PIECES[i, j, half]
                buf_ref[at : at + rows, :] = value[:rows, half * 128 : half * 128 + 128]

    for j in range(GROUP):
        pl.when(pl.program_id(0) == j)(lambda j=j: block(j))


def gather_rows(ref, step, first, high_ref, low_ref, value_ref=None, columns=8):
    for t in range(columns):
        for i in range(4):
            value = ref[pl.ds(first + t * 4 + i, NCHIP, stride=step), :]
            high, low = split(value)
            high_ref[i * 64 : i * 64 + 64, t * 128 : t * 128 + 128] = high
            low_ref[i * 64 : i * 64 + 64, t * 128 : t * 128 + 128] = low
            if value_ref is not None:
                value_ref[i * 64 : i * 64 + 64, t * 128 : t * 128 + 128] = value


def scatter_rows(value, block, buf_ref):
    for half in range(2):
        for i in range(4):
            start = (block * 2 + half) * 4 + i
            buf_ref[pl.ds(start, NCHIP, stride=PROWS), :] = value[
                i * 64 : i * 64 + 64, half * 128 : half * 128 + 128
            ]


def local_products(
    core_ref, own_ref, sib_ref, e_ref,
    high_ref, low_ref, x_ref, buf_ref, first_ref, ch_ref, cl_ref,
    eh_ref, el_ref, bh_ref, bl_ref,
):
    core, n = core_ref[0], pl.program_id(0)

    @pl.when(n == 0)
    def _():
        for part in range(2):
            held = core if part == 0 else 1 - core
            at = pl.ds(part * 512, 512)
            gather_rows(
                e_ref, 32, held * 16, eh_ref.at[:, at], el_ref.at[:, at], x_ref.at[:, at], columns=4
            )

    high, low = split_block(own_ref, sib_ref)
    high_ref[0], low_ref[0] = high, low
    value = dot3((eh_ref[...], el_ref[...]), (high, low), NT)

    @pl.when(n < GROUP)
    def _():
        bh_ref[pl.ds(n * NB, NB), :] = high
        bl_ref[pl.ds(n * NB, NB), :] = low
        scatter_rows(value, n, buf_ref)

    @pl.when(n >= GROUP)
    def _():
        first_ref[...] = value
        for j in range(GROUP):
            rows = slice(j * NB, j * NB + NB)
            ch_ref[rows, :], cl_ref[rows, :] = split(
                dot3((bh_ref[rows, :], bl_ref[rows, :]), (high, low), NT)
            )


def sum_chips(buf_ref, rows):
    def add(q, total):
        return total + buf_ref[q]

    return lax.fori_loop(0, NCHIP, add, jnp.zeros((rows, 128), F32), unroll=8)


def spread_to_chips(part, out_ref):
    def spread(q, carry):
        out_ref[q] = part
        return carry

    lax.fori_loop(0, NCHIP, spread, 0, unroll=8)


def sum_products(buf_ref, out_ref):
    spread_to_chips(sum_chips(buf_ref, GROWS), out_ref)


def block_of(g_ref, i, j):
    halves = []
    for half in range(2):
        at, rows = PIECES[i, j, half]
        value = g_ref[at : at + rows, :]
        if rows < NB:
            value = jnp.concatenate([value, jnp.zeros((NB - rows, 128), F32)], axis=0)
        halves.append(value)
    return jnp.concatenate(halves, axis=1)


def invert(g_ref, out_ref):
    row = lax.broadcasted_iota(jnp.int32, (NB, NB), 0)
    col = lax.broadcasted_iota(jnp.int32, (NB, NB), 1)
    apart = row ^ col
    for index, (i, j) in enumerate(PAIRS):
        value = block_of(g_ref, i, j)
        if i == j:
            diagonal = jnp.where(row == col, 0.5 * value, 0.0)
            down = 1.0 / jnp.sum(diagonal, axis=1, keepdims=True)
            across = 1.0 / jnp.sum(diagonal, axis=0, keepdims=True)
            beside = jnp.where((apart == 1) & (row < col), value, 0.0)
            value = jnp.where(row == col, down, 0.0) - down * beside * across
        out_ref[index] = value
    size = 2
    while size < NB:
        for i in range(GROUP):
            index = PAIRS.index((i, i))
            beside = jnp.where((apart >= size) & (apart < 2 * size) & (row < col), block_of(g_ref, i, i), 0.0)
            value = out_ref[index]
            halves = split(value)
            product = dot3(split(dot3(halves, split(beside), NN)), halves, NN)
            out_ref[index] = value - product
        size *= 2


def split_factors(core_ref, own_ref, sib_ref, bh_ref, bl_ref, ah_ref, al_ref):
    mine = core_ref[0] == 0
    bh_ref[...], bl_ref[...] = split(jnp.where(mine, own_ref[...], sib_ref[...]))
    ah_ref[...], al_ref[...] = split(jnp.where(mine, sib_ref[...], own_ref[...]))


def solve(buf_ref, high_ref, low_ref, out_ref, c_ref):
    c_ref[...] = sum_chips(buf_ref, PROWS)

    def factor(i, j):
        index = PAIRS.index((i, j))
        return high_ref[index], low_ref[index]

    found = {}
    for b in range(GROUP - 1, -1, -1):
        rest = jnp.concatenate([c_ref[b * 8 : b * 8 + 4, :], c_ref[b * 8 + 4 : b * 8 + 8, :]], axis=1)
        rest = jnp.concatenate([rest, rest], axis=0)
        for later in range(GROUP - 1, b, -1):
            rest = rest - dot3(found[later], factor(b, later), NT)
        value = dot3(split(rest), factor(b, b), NT)
        found[b] = split(value)
        for half in range(2):
            c_ref[b * 8 + half * 4 : b * 8 + half * 4 + 4, :] = value[0:4, half * 128 : half * 128 + 128]
    spread_to_chips(c_ref[...], out_ref)


def correct_projection(c_ref, gh_ref, gl_ref, first_ref, buf_ref, ch_ref, cl_ref):
    n = pl.program_id(0)

    @pl.when(n == 0)
    def _():
        gather_rows(c_ref, PROWS, 0, ch_ref, cl_ref)

    value = first_ref[...] - dot3((ch_ref[...], cl_ref[...]), (gh_ref[...], gl_ref[...]), NN)
    scatter_rows(value, n, buf_ref)


def updated(c_ref, high_ref, low_ref, x_ref, ch_ref, cl_ref):
    @pl.when(pl.program_id(0) == 0)
    def _():
        gather_rows(c_ref, PROWS, 0, ch_ref, cl_ref)

    vectors = (high_ref[...].reshape(1024, 256), low_ref[...].reshape(1024, 256))
    return x_ref[...] - dot3((ch_ref[...], cl_ref[...]), vectors, NN)


def update(c_ref, high_ref, low_ref, x_ref, out_ref, ch_ref, cl_ref):
    out_ref[...] = updated(c_ref, high_ref, low_ref, x_ref, ch_ref, cl_ref)


def update_last(core_ref, c_ref, high_ref, low_ref, x_ref, out_ref, ch_ref, cl_ref):
    value = updated(c_ref, high_ref, low_ref, x_ref, ch_ref, cl_ref)
    for c in range(NCOL):
        for i in range(4):
            out_ref[c, i * 8 : i * 8 + 8, :] = value[i * 64 + c * 8 : i * 64 + c * 8 + 8, :]


def pass_on(after_ref, in_ref, out_ref):
    pass


def place_rows(in_ref, out_ref, held_ref):
    for c in range(NCOL):
        for t in range(4):
            at = c * 512 + t * 128
            for core in range(2):
                for i in range(4):
                    held_ref[pl.ds((c * 4 + t) * 64 + core * 32 + i, 8, stride=4), :] = in_ref[
                        core * NCOL + c, i * 8 : i * 8 + 8, t * 128 : t * 128 + 128
                    ]
            out_ref[:, at : at + 128] = held_ref[(c * 4 + t) * 64 : (c * 4 + t) * 64 + 64, :]


def whole(*shape):
    return pl.BlockSpec(shape, lambda *_: (0,) * len(shape))


def run(kernel, out_shape, out_specs, in_specs, operands, grid=(1,), scratch=(), core=None, flops=0, size=0, **options):
    spec = pltpu.PrefetchScalarGridSpec(
        num_scalar_prefetch=0 if core is None else 1,
        grid=grid,
        in_specs=in_specs,
        out_specs=out_specs,
        scratch_shapes=list(scratch),
    )
    built = pl.pallas_call(
        kernel,
        out_shape=out_shape,
        grid_spec=spec,
        compiler_params=pltpu.CompilerParams(vmem_limit_bytes=48 * 1024 * 1024),
        cost_estimate=pl.CostEstimate(flops=flops, bytes_accessed=size, transcendentals=0),
        **options,
    )
    return built(*operands) if core is None else built(core, *operands)


def exchange(value, axes):
    return lax.all_to_all(value, axes, 0, 0, tiled=True)


def on_device(eigenvectors, reflectors):
    core = lax.axis_index("core").astype(jnp.int32).reshape(1)
    mega = 2**20
    rows_pair = [pltpu.VMEM((256, 1024), BF16)] * 2

    vectors = run(
        cut_vectors,
        f32(NCOL, 8, 32, 512),
        ANY,
        [ANY],
        (reflectors,),
        scratch=[pltpu.SemaphoreType.DMA((NCOL,))],
        size=8 * mega,
    )
    own = exchange(vectors, COLS)
    sib = lax.ppermute(own, "core", SWAP)
    pieces = run(
        cut_eigenvectors,
        f32(NCHIP, 2, 16, 128),
        whole(NCHIP, 2, 16, 128),
        [ANY, whole(4, 65536)],
        (own, eigenvectors),
        size=2 * mega,
    )
    spread = exchange(pieces, CHIPS).reshape(NCHIP * 32, 128)

    picked = pl.BlockSpec((NCOL, 1, 32, 512), lambda b, core: (0, (1 - core[0]) * GROUP + b, 0, 0))
    buf = run(
        inner_products,
        f32(ALLROWS, 128),
        whole(ALLROWS, 128),
        [picked, picked],
        (own, sib),
        grid=(GROUP,),
        scratch=[pltpu.VMEM((GROUP, NB, 1024), BF16)] * 2,
        core=core,
        flops=4 * 10**9,
        size=6 * mega,
    )

    def after(earlier, value):
        return run(
            pass_on, jax.ShapeDtypeStruct(value.shape, F32), ANY, [ANY, ANY], (earlier, value), input_output_aliases={1: 0}
        )

    buf = after(spread, buf)
    arrived = exchange(buf.reshape(NCHIP, GROWS, 128), CHIPS)

    block = pl.BlockSpec((NCOL, 1, 32, 512), lambda n, core: (0, lax.rem(n + GROUP, 8), 0, 0))
    halves = pl.BlockSpec((1, NB, 1024), lambda n, core: (lax.rem(n + GROUP, 8), 0, 0))
    column = pl.BlockSpec((1024, NB), lambda n, core: (0, jnp.maximum(n - GROUP, 0)))
    high, low, start, buf, first, cross_high, cross_low = run(
        local_products,
        (
            bf16(8, NB, 1024), bf16(8, NB, 1024), f32(256, 1024), f32(NCHIP * PROWS, 128),
            f32(256, 1024), bf16(1024, 1024), bf16(1024, 1024),
        ),
        (
            halves, halves, whole(256, 1024), whole(NCHIP * PROWS, 128),
            pl.BlockSpec((256, NB), lambda n, core: (0, jnp.maximum(n - GROUP, 0))), column, column,
        ),
        [block, block, whole(NCHIP * 32, 128)],
        (own, sib, spread),
        grid=(8,),
        scratch=rows_pair + [pltpu.VMEM((1024, 1024), BF16)] * 2,
        core=core,
        flops=10**10,
        size=24 * mega,
    )
    part = run(
        sum_products,
        f32(NCHIP, GROWS, 128),
        whole(NCHIP, GROWS, 128),
        [whole(NCHIP, GROWS, 128)],
        (arrived,),
        size=5 * mega,
    )
    part = after(first, part)
    gram = exchange(part, CHIPS).reshape(ALLROWS, 128)

    buf = after(gram, buf)
    arrived = exchange(buf.reshape(NCHIP, PROWS, 128), CHIPS)
    count = len(PAIRS)
    factors = run(
        invert,
        f32(count, NB, NB),
        whole(count, NB, NB),
        [whole(ALLROWS, 128)],
        (gram,),
    )
    factors_sib = lax.ppermute(factors, "core", SWAP)
    square = pl.BlockSpec((2, NB, NB), lambda n, core: (n, 0, 0))
    last_high, last_low, first_high, first_low = run(
        split_factors,
        (bf16(count, NB, NB),) * 4,
        (square,) * 4,
        [square, square],
        (factors, factors_sib),
        grid=(count // 2,),
        core=core,
    )

    def coefficients_of(arrived, high, low):
        rows = run(
            solve,
            f32(NCHIP, PROWS, 128),
            whole(NCHIP, PROWS, 128),
            [whole(NCHIP, PROWS, 128), whole(count, NB, NB), whole(count, NB, NB)],
            (arrived, high, low),
            scratch=[pltpu.VMEM((PROWS, 128), F32)],
            flops=10**8,
            size=5 * mega,
        )
        return exchange(rows, CHIPS).reshape(NCHIP * PROWS, 128)

    coefficients = coefficients_of(arrived, last_high, last_low)
    buf = run(
        correct_projection,
        f32(NCHIP * PROWS, 128),
        whole(NCHIP * PROWS, 128),
        [
            whole(NCHIP * PROWS, 128),
            pl.BlockSpec((1024, NB), lambda n: (0, n)),
            pl.BlockSpec((1024, NB), lambda n: (0, n)),
            pl.BlockSpec((256, NB), lambda n: (0, n)),
        ],
        (coefficients, cross_high, cross_low, first),
        grid=(GROUP,),
        scratch=rows_pair,
        flops=2 * 10**9,
        size=7 * mega,
    )
    arrived = exchange(buf.reshape(NCHIP, PROWS, 128), CHIPS)

    def group(which):
        return pl.BlockSpec((GROUP, NB, NB), lambda n, *_: (which, 0, n))

    slab = pl.BlockSpec((256, NB), lambda n, *_: (0, n))
    middle = run(
        update,
        f32(256, 1024),
        slab,
        [whole(NCHIP * PROWS, 128), group(1), group(1), slab],
        (coefficients, high, low, start),
        grid=(4,),
        scratch=rows_pair,
        flops=2 * 10**9,
        size=7 * mega,
    )
    coefficients = coefficients_of(arrived, first_high, first_low)
    finished = run(
        update_last,
        f32(2 * NCOL, 32, 512),
        pl.BlockSpec((NCOL, 32, NB), lambda n, core: (jnp.where(n < 2, core[0], 1 - core[0]), 0, lax.rem(n, 2))),
        [whole(NCHIP * PROWS, 128), group(0), group(0), slab],
        (coefficients, high, low, middle),
        grid=(4,),
        scratch=rows_pair,
        core=core,
        flops=2 * 10**9,
        size=7 * mega,
    )
    return run(
        place_rows,
        f32(64, 4096),
        whole(64, 4096),
        [whole(2 * NCOL, 32, 512)],
        (exchange(finished, CORE_COLS),),
        scratch=[pltpu.VMEM((2048, 128), F32)],
        size=2 * mega,
    )


def solution(mesh):
    fine = Mesh(mesh.devices.reshape(SIZES), AXES)
    in_specs = (P(AXES, None), P(None, COLS, ("y", "xl", "core")))
    out_specs = P(COLS, ("y", "xl", "core"))
    return jax.shard_map(on_device, mesh=fine, in_specs=in_specs, out_specs=out_specs, check_vma=False)
```

time: 1960 us -> 302 us (0.15); the launches traced: 1940 us -> 300 us
  waiting for transfers between devices: 1210 us -> 42.6 us
  matrix products: 549 us -> 0 us
  blocking collectives: 23.5 us -> 160 us
  local copies, waits for them, and re-layouts: 80.3 us -> 11.8 us
  Pallas kernels: 0 us -> 62.3 us
  other arithmetic: 35.8 us -> 0 us
    psum x8 -> x0, waiting for transfers between devices: 1160 us -> none  [reduce_sum(): return lax.psum(partial_sum, ('row', 'col'))]
    dot_general x281 -> x0, matrix products: 549 us -> none  [the longest x256 499 us: back_step(): solved = jnp.einsum('bij,bjk->bik', row_part, inverse, precision=HIGHEST)]
    all_to_all x1 -> x5, blocking collectives: 23.5 us -> 160 us  [exchange(): return lax.all_to_all(value, axes, 0, 0, tiled=True)]
    pallas_call x0 -> x16, Pallas kernels: none -> 62.3 us  [run(): return built(*operands) if core is None else built(core, *operands)]
    unnamed x49 -> x32, local copies, waits for them, and re-layouts: 42.6 us -> 11.8 us
    all_to_all x2 -> x4, waiting for transfers between devices: 50.9 us -> 42.6 us  [exchange(): return lax.all_to_all(value, axes, 0, 0, tiled=True)]
  transfers between devices with their start and end apart: 10 -> 6, of which waited for: 9 -> 4; matrix products, arithmetic and copies ran while one was open for 1% -> 0% of each run, Pallas kernels for 0% -> 12%
where the time goes in v1:
time: 302 us; the launch traced here: 300 us
  blocking collectives  160 us (53%)
  Pallas kernels  62.3 us (21%)
  waiting for transfers between devices  42.6 us (14%)
  starting transfers between devices  23.2 us (8%)
  local copies, waits for them, and re-layouts  11.8 us (4%)
    all_to_all x5, blocking collectives, exchange(): return lax.all_to_all(value, axes, 0, 0, tiled=True)  160 us
    pallas_call x16, Pallas kernels, run(): return built(*operands) if core is None else built(core, *operands)  62.3 us
    all_to_all x4, waiting for transfers between devices, exchange(): return lax.all_to_all(value, axes, 0, 0, tiled=True)  42.6 us
    all_to_all x4, starting transfers between devices, exchange(): return lax.all_to_all(value, axes, 0, 0, tiled=True)  23.1 us
    unnamed x32, local copies, waits for them, and re-layouts  11.8 us
  transfers between devices with their start and end apart: 6, of which 4 were waited for; matrix products, arithmetic and copies ran while one was open for 0% of the time, Pallas kernels for 12%

profile of v1, /device:TPU:0, one launch (start us, length us, event | category | flops | bytes accessed | tf_op | source)
XLA Modules:
  0.0 300.3 jit_solution(14163908357565460034)
XLA Ops:
  0.0 2.2 shard_map.28
  2.2 58.8 %all_to_all.45.after_ref.own_ref = f32[8,8,32,512]{3,2,1,0:T(8,128)} all-to-all(f32[8,8,32,512]{3,2,1,0:T(8,128)S(1)} %shard_map.28), channel_id=1, replica_groups=mesh['y'=4,'xl'=2,'core'=2,'z'=4,'xh'=2] {'z','xh'}, dimensions={0} | all-to-all | bytes 8388608 | tf_op jit(solution)/shard_map/all_to_all | solution.py:312
  62.1 6.7 %all-to-all-start.1 = ((f32[64,2,16,128]{3,2,1,0:T(8,128)}), f32[64,2,16,128]{3,2,1,0:T(8,128)S(1)}, u32[]{:S(2)}, u32[]{:S(2)}) async-start(f32[64,2,16,128]{3,2,1,0:T(8,128)} %shard_map.29), calls=%async_computation.1 | async-start | bytes 2097152 | tf_op jit(solution)/shard_map/all_to_all | solution.py:312
  68.8 6.4 %shard_map.31.in_ref = f32[4608,128]{1,0:T(8,128)S(1)} custom-call(s32[1]{0:T(128)} %bitcast.core_ref, f32[8,8,32,512]{3,2,1,0:T(8,128)} %all_to_all.45.after_ref.own_ref, f32[8,8,32,512]{3,2,1,0:T(8,128)} %collective-permute-done.sib_ref), custom_call_target="tpu_custom_call" | custom-call | flops 4000000000 | bytes 6291456 | tf_op jit(solution)/shard_map/pallas_call | solution.py:308
  75.2 12.6 %all-to-all-done.1 = f32[64,2,16,128]{3,2,1,0:T(8,128)S(1)} async-done(((f32[64,2,16,128]{3,2,1,0:T(8,128)}), f32[64,2,16,128]{3,2,1,0:T(8,128)S(1)}, u32[]{:S(2)}, u32[]{:S(2)}) %all-to-all-start.1) | async-done | bytes 1048608 | tf_op jit(solution)/shard_map/all_to_all | solution.py:312
  87.9 1.4 copy-done.1
  89.3 5.4 %all-to-all-start.2 = ((f32[64,72,128]{2,1,0:T(8,128)}), f32[64,72,128]{2,1,0:T(8,128)S(1)}, u32[]{:S(2)}, u32[]{:S(2)}) async-start(f32[64,72,128]{2,1,0:T(8,128)} %bitcast.10), calls=%async_computation.2 | async-start | bytes 4718592 | tf_op jit(solution)/shard_map/all_to_all | solution.py:312
  94.8 18.7 %shard_map.30 = (bf16[8,256,1024]{2,1,0:T(8,128)(2,1)}, bf16[8,256,1024]{2,1,0:T(8,128)(2,1)}, f32[256,1024]{1,0:T(8,128)S(1)}, f32[2048,128]{1,0:T(8,128)S(1)},...) custom-call(s32[1]{0:T(128)} %bitcast.core_ref, ...), custom_call_target="tpu_custom_call" | custom-call | flops 10000000000 | bytes 25165824 | tf_op jit(solution)/shard_map/pallas_call | solution.py:308
  116.4 9.8 %all-to-all-done.2.buf_ref = f32[64,72,128]{2,1,0:T(8,128)S(1)} async-done(((f32[64,72,128]{2,1,0:T(8,128)}), f32[64,72,128]{2,1,0:T(8,128)S(1)}, u32[]{:S(2)}, u32[]{:S(2)}) %all-to-all-start.2) | async-done | bytes 2359328 | tf_op jit(solution)/shard_map/all_to_all | solution.py:312
  127.4 36.8 %all_to_all.46 = f32[64,72,128]{2,1,0:T(8,128)S(1)} all-to-all(f32[64,72,128]{2,1,0:T(8,128)S(1)} %shard_map.34), channel_id=1, replica_groups=mesh['y'=4,'xl'=2,'core'=2,'z'=4,'xh'=2] {'y','xl','z','xh'}, dimensions={0} | all-to-all | bytes 4718592 | tf_op jit(solution)/shard_map/all_to_all | solution.py:312
  164.3 6.4 %shard_map.36.own_ref = f32[10,256,256]{2,1,0:T(8,128)S(1)} custom-call(f32[4608,128]{1,0:T(8,128)S(1)} %bitcast.8), custom_call_target="tpu_custom_call" | custom-call | tf_op jit(solution)/shard_map/pallas_call | solution.py:308
  172.6 5.5 %all-to-all-start.4 = ((f32[64,32,128]{2,1,0:T(8,128)}), f32[64,32,128]{2,1,0:T(8,128)}, u32[]{:S(2)}, u32[]{:S(2)}) async-start(f32[64,32,128]{2,1,0:T(8,128)} %bitcast.11), calls=%async_computation.4 | async-start | bytes 2097152 | tf_op jit(solution)/shard_map/all_to_all | solution.py:312
  178.2 4.3 %shard_map.37 = (bf16[10,256,256]{2,1,0:T(8,128)(2,1)S(1)}, bf16[10,256,256]{2,1,0:T(8,128)(2,1)S(1)}, bf16[10,256,256]{2,1,0:T(8,128)(2,1)S(1)}, bf16[10,256,256]{2,1,0:T(8,128)(2,1)S(1)}) custom-call(s32[1]{0:T(128)} %bitcast.core_ref, f32[10,256,256]{2,1,0:T(8,128)} %copy-done, f32[10,256,256]{2,1,0:T(8,128)} %collective-permute-done.1.sib_ref), custom_call_target="tpu_custom_call" | custom-call | tf_op jit(solution)/shard_map/pallas_call | solution.py:308
  184.6 11.9 %all-to-all-done.4.buf_ref = f32[64,32,128]{2,1,0:T(8,128)} async-done(((f32[64,32,128]{2,1,0:T(8,128)}), f32[64,32,128]{2,1,0:T(8,128)}, u32[]{:S(2)}, u32[]{:S(2)}) %all-to-all-start.4) | async-done | bytes 1048608 | tf_op jit(solution)/shard_map/all_to_all | solution.py:312
  197.8 3.4 %shard_map.38 = f32[64,32,128]{2,1,0:T(8,128)S(1)} custom-call(f32[64,32,128]{2,1,0:T(8,128)} %all-to-all-done.4.buf_ref, bf16[10,256,256]{2,1,0:T(8,128)(2,1)S(1)} %get-tuple-element.18.high_ref, bf16[10,256,256]{2,1,0:T(8,128)(2,1)S(1)} %copy-done.8), custom_call_target="tpu_custom_call" | custom-call | flops 100000000 | bytes 5242880 | tf_op jit(solution)/shard_map/pallas_call | solution.py:308
  201.2 22.4 %all_to_all.47 = f32[64,32,128]{2,1,0:T(8,128)S(1)} all-to-all(f32[64,32,128]{2,1,0:T(8,128)S(1)} %shard_map.38), channel_id=1, replica_groups=mesh['y'=4,'xl'=2,'core'=2,'z'=4,'xh'=2] {'y','xl','z','xh'}, dimensions={0} | all-to-all | bytes 2097152 | tf_op jit(solution)/shard_map/all_to_all | solution.py:312
  223.6 5.2 %shard_map.39 = f32[2048,128]{1,0:T(8,128)S(1)} custom-call(f32[2048,128]{1,0:T(8,128)S(1)} %bitcast.15, bf16[1024,1024]{1,0:T(8,128)(2,1)S(1)} %copy-done.15, bf16[1024,1024]{1,0:T(8,128)(2,1)} %get-tuple-element.21.gl_ref, f32[256,1024]{1,0:T(8,128)S(1)} %copy-done.12), custom_call_target="tpu_custom_call" | custom-call | flops 2000000000 | bytes 7340032 | tf_op jit(solution)/shard_map/pallas_call | solution.py:308
  228.9 21.3 %all_to_all.48.buf_ref = f32[64,32,128]{2,1,0:T(8,128)S(1)} all-to-all(f32[64,32,128]{2,1,0:T(8,128)S(1)} %bitcast.17), channel_id=1, replica_groups=mesh['y'=4,'xl'=2,'core'=2,'z'=4,'xh'=2] {'y','xl','z','xh'}, dimensions={0} | all-to-all | bytes 2097152 | tf_op jit(solution)/shard_map/all_to_all | solution.py:312
  250.2 3.0 shard_map.40
  253.1 5.4 %all-to-all-start.7 = ((f32[64,32,128]{2,1,0:T(8,128)}), f32[64,32,128]{2,1,0:T(8,128)S(1)}, u32[]{:S(2)}, u32[]{:S(2)}) async-start(f32[64,32,128]{2,1,0:T(8,128)} %shard_map.40), calls=%async_computation.7 | async-start | bytes 2097152 | tf_op jit(solution)/shard_map/all_to_all | solution.py:312
  259.8 5.0 %shard_map.41.x_ref = f32[256,1024]{1,0:T(8,128)S(1)} custom-call(f32[2048,128]{1,0:T(8,128)S(1)} %bitcast.16, bf16[8,256,1024]{2,1,0:T(8,128)(2,1)} %get-tuple-element.24.high_ref, bf16[8,256,1024]{2,1,0:T(8,128)(2,1)} %get-tuple-element.25.low_ref, f32[256,1024]{1,0:T(8,128)S(1)} %copy-done.14), custom_call_target="tpu_custom_call" | custom-call | flops 2000000000 | bytes 7340032 | tf_op jit(solution)/shard_map/pallas_call | solution.py:308
  264.9 8.3 %all-to-all-done.7 = f32[64,32,128]{2,1,0:T(8,128)S(1)} async-done(((f32[64,32,128]{2,1,0:T(8,128)}), f32[64,32,128]{2,1,0:T(8,128)S(1)}, u32[]{:S(2)}, u32[]{:S(2)}) %all-to-all-start.7) | async-done | bytes 1048608 | tf_op jit(solution)/shard_map/all_to_all | solution.py:312
  273.2 5.1 %shard_map.42 = f32[16,32,512]{2,1,0:T(8,128)S(1)} custom-call(s32[1]{0:T(128)} %bitcast.core_ref, f32[2048,128]{1,0:T(8,128)S(1)} %bitcast.12, bf16[8,256,1024]{2,1,0:T(8,128)(2,1)} %get-tuple-element.24.high_ref, bf16[8,256,1024]{2,1,0:T(8,128)(2,1)} %get-tuple-element.25.low_ref, f32[256,1024]{1,0:T(8,128)S(1)} %shard_map.41.x_ref), custom_call_target="tpu_custom_call" | custom-call | flops 2000000000 | bytes 7340032 | tf_op jit(solution)/shard_map/pallas_call | solution.py:308
  278.3 20.9 %all_to_all.49.in_ref = f32[16,32,512]{2,1,0:T(8,128)S(1)} all-to-all(f32[16,32,512]{2,1,0:T(8,128)S(1)} %shard_map.42), channel_id=1, replica_groups=mesh['y'=4,'xl'=2,'core'=2,'z'=4,'xh'=2] {'core','z','xh'}, dimensions={0} | all-to-all | bytes 2097152 | tf_op jit(solution)/shard_map/all_to_all | solution.py:312
  (41 shorter events, 13.0 us)
Async XLA Ops:
  2.2 58.8 %copy-start.9 = (f32[4,65536]{1,0:T(4,128)S(1)}, f32[4,65536]{1,0:T(4,128)}, u32[]{:S(2)}) copy-start(f32[4,65536]{1,0:T(4,128)} %e_ref.1) | copy-start | bytes 3145732
  61.0 7.8 %collective-permute-start = (f32[8,8,32,512]{3,2,1,0:T(8,128)}, f32[8,8,32,512]{3,2,1,0:T(8,128)}, u32[]{:S(2)}, u32[]{:S(2)}) collective-permute-start(f32[8,8,32,512]{3,2,1,0:T(8,128)} %all_to_all.45.after_ref.own_ref), channel_id=1, source_target_pairs={{0,8},{8,0},{1,9},{9,1},{2,10},{10,2},{3,11},{11,3},{4,12},{12,4},... | collective-permute-start | bytes 12582920 | tf_op jit(solution)/shard_map/ppermute | solution.py:330
  62.1 25.8 %all-to-all-start.1 = ((f32[64,2,16,128]{3,2,1,0:T(8,128)}), f32[64,2,16,128]{3,2,1,0:T(8,128)S(1)}, u32[]{:S(2)}, u32[]{:S(2)}) async-start(f32[64,2,16,128]{3,2,1,0:T(8,128)} %shard_map.29), calls=%async_computation.1 | async-start | bytes 2097152 | tf_op jit(solution)/shard_map/all_to_all | solution.py:312
  87.9 1.4 copy-start.1
  89.3 36.9 %all-to-all-start.2 = ((f32[64,72,128]{2,1,0:T(8,128)}), f32[64,72,128]{2,1,0:T(8,128)S(1)}, u32[]{:S(2)}, u32[]{:S(2)}) async-start(f32[64,72,128]{2,1,0:T(8,128)} %bitcast.10), calls=%async_computation.2 | async-start | bytes 4718592 | tf_op jit(solution)/shard_map/all_to_all | solution.py:312
  113.4 1.0 copy-start.2
  114.5 1.0 copy-start.10
  115.4 1.0 copy-start.13
  126.2 1.2 copy-start.11
  164.3 6.5 %copy-start.3 = (f32[2048,128]{1,0:T(8,128)S(1)}, f32[2048,128]{1,0:T(8,128)}, u32[]{:S(2)}) copy-start(f32[2048,128]{1,0:T(8,128)} %copy-done.2) | copy-start | bytes 3145732
  170.7 1.9 copy-start
  170.7 7.4 %collective-permute-start.1 = (f32[10,256,256]{2,1,0:T(8,128)S(1)}, f32[10,256,256]{2,1,0:T(8,128)}, u32[]{:S(2)}, u32[]{:S(2)}) collective-permute-start(f32[10,256,256]{2,1,0:T(8,128)S(1)} %shard_map.36.own_ref), channel_id=1, source_target_pairs={{0,8},{8,0},{1,9},{9,1},{2,10},{10,2},{3,11},{11,3},{4,12},{12,4},... | collective-permute-start | bytes 7864328 | tf_op jit(solution)/shard_map/ppermute | solution.py:405
  170.8 1.2 copy-start.4
  172.6 23.9 %all-to-all-start.4 = ((f32[64,32,128]{2,1,0:T(8,128)}), f32[64,32,128]{2,1,0:T(8,128)}, u32[]{:S(2)}, u32[]{:S(2)}) async-start(f32[64,32,128]{2,1,0:T(8,128)} %bitcast.11), calls=%async_computation.4 | async-start | bytes 2097152 | tf_op jit(solution)/shard_map/all_to_all | solution.py:312
  182.5 1.1 copy-start.5
  183.6 1.1 copy-start.7
  196.5 1.3 copy-start.8
  197.8 25.8 %copy-start.12 = (f32[256,1024]{1,0:T(8,128)S(1)}, f32[256,1024]{1,0:T(8,128)}, u32[]{:S(2)}) copy-start(f32[256,1024]{1,0:T(8,128)} %copy-done.10) | copy-start | bytes 3145732
  197.8 25.8 %copy-start.15 = (bf16[1024,1024]{1,0:T(8,128)(2,1)S(1)}, bf16[1024,1024]{1,0:T(8,128)(2,1)}, u32[]{:S(2)}) copy-start(bf16[1024,1024]{1,0:T(8,128)(2,1)} %get-tuple-element.20.gh_ref) | copy-start | bytes 6291460
  228.8 21.3 %copy-start.6 = (bf16[10,256,256]{2,1,0:T(8,128)(2,1)S(1)}, bf16[10,256,256]{2,1,0:T(8,128)(2,1)}, u32[]{:S(2)}) copy-start(bf16[10,256,256]{2,1,0:T(8,128)(2,1)} %copy-done.5) | copy-start | bytes 3932164
  253.1 20.0 %all-to-all-start.7 = ((f32[64,32,128]{2,1,0:T(8,128)}), f32[64,32,128]{2,1,0:T(8,128)S(1)}, u32[]{:S(2)}, u32[]{:S(2)}) async-start(f32[64,32,128]{2,1,0:T(8,128)} %shard_map.40), calls=%async_computation.7 | async-start | bytes 2097152 | tf_op jit(solution)/shard_map/all_to_all | solution.py:312
  258.6 1.2 copy-start.14

commit v2 on v1

v2 whole, which is shorter than its diff:
```python
import jax
import jax.numpy as jnp
from jax import lax
from jax.experimental import pallas as pl
from jax.experimental.pallas import tpu as pltpu
from jax.sharding import Mesh, PartitionSpec as P

AXES = ("y", "xl", "core", "z", "xh")
SIZES = (4, 2, 2, 4, 2)
CHIPS = ("y", "xl", "z", "xh")
COLS = ("z", "xh")
CORE_COLS = ("core", "z", "xh")
SWAP = ((0, 1), (1, 0))

NCHIP = 64
NCOL = 8
NB = 256
GROUP = 4
PAIRS = [(i, j) for i in range(GROUP) for j in range(i, GROUP)]


def place_pieces():
    at, pieces = 0, {}
    for i, j in PAIRS:
        for half in range(2):
            rows = NB // 2 if i == j and half == 0 else NB
            pieces[i, j, half] = (at, rows)
            at += rows
    return at, pieces


ALLROWS, PIECES = place_pieces()
GROWS = ALLROWS // NCHIP
EROWS = 32
STEP = GROWS + EROWS
PROWS = 32
ANY = pl.BlockSpec(memory_space=pl.ANY)
HBM = pl.BlockSpec(memory_space=pltpu.HBM)
F32 = jnp.float32
BF16 = jnp.bfloat16
NT = (((1,), (1,)), ((), ()))
NN = (((1,), (0,)), ((), ()))


def bf16(*shape):
    return jax.ShapeDtypeStruct(shape, BF16)


def f32(*shape):
    return jax.ShapeDtypeStruct(shape, F32)


def hbm(dtype, *shape):
    return pltpu.HBM(shape, dtype)


def split(value):
    high = value.astype(BF16)
    return high, (value - high.astype(F32)).astype(BF16)


def dot3(a, b, dims):
    def one(x, y):
        return lax.dot_general(x, y, dims, preferred_element_type=F32)

    return one(a[0], b[0]) + (one(a[0], b[1]) + one(a[1], b[0]))


def cut_eigenvectors(e_ref, out_ref):
    for core in range(2):
        for c in range(NCOL):
            for t in range(4):
                for k in range(8):
                    at = (((k * 2 + core) * NCOL + c) * 4 + t) * 128
                    out_ref[k * NCOL + c, core * 16 + t * 4 : core * 16 + t * 4 + 4, :] = e_ref[:, at : at + 128]


def cut_vectors(w_ref, out_ref, done):
    copies = []
    for core in range(2):
        for c in range(NCOL):
            to = core * NCOL + c
            first = (1 - core) * GROUP
            copies.append(
                pltpu.make_async_copy(
                    w_ref.at[first : first + GROUP, :, c * 512 : c * 512 + 512], out_ref.at[to], done.at[to]
                )
            )
    for copy in copies:
        copy.start()
    for copy in copies:
        copy.wait()


def whole_block(value):
    return jnp.concatenate([value[:NCOL].reshape(NB, 512), value[NCOL:].reshape(NB, 512)], axis=1)


def inner_products(w_ref, e_ref, buf_ref, high_ref, low_ref):
    def block(j):
        high_ref[j], low_ref[j] = split(whole_block(w_ref[:, 0]))
        for i in range(j + 1):
            value = dot3((high_ref[i], low_ref[i]), (high_ref[j], low_ref[j]), NT)
            for half in range(2):
                at, rows = PIECES[i, j, half]
                done = 0
                while done < rows:
                    chip, offset = divmod(at + done, GROWS)
                    take = min(rows - done, GROWS - offset)
                    start = chip * STEP + offset
                    buf_ref[start : start + take, :] = value[done : done + take, half * 128 : half * 128 + 128]
                    done += take

    for j in range(GROUP):
        pl.when(pl.program_id(0) == j)(lambda j=j: block(j))

    @pl.when(pl.program_id(0) == 0)
    def _():
        for q in range(NCHIP):
            buf_ref[q * STEP + GROWS : q * STEP + STEP, :] = e_ref[q]


def gather_rows(ref, step, first, high_ref, low_ref, value_ref=None, columns=8):
    for t in range(columns):
        for i in range(4):
            value = ref[pl.ds(first + t * 4 + i, NCHIP, stride=step), :]
            high, low = split(value)
            high_ref[i * 64 : i * 64 + 64, t * 128 : t * 128 + 128] = high
            low_ref[i * 64 : i * 64 + 64, t * 128 : t * 128 + 128] = low
            if value_ref is not None:
                value_ref[i * 64 : i * 64 + 64, t * 128 : t * 128 + 128] = value


def scatter_rows(value, block, buf_ref):
    for half in range(2):
        for i in range(4):
            start = (block * 2 + half) * 4 + i
            buf_ref[pl.ds(start, NCHIP, stride=PROWS), :] = value[
                i * 64 : i * 64 + 64, half * 128 : half * 128 + 128
            ]


def local_products(
    core_ref, mine_ref, other_ref, e_ref,
    high_ref, low_ref, x_ref, buf_ref, first_ref, ch_ref, cl_ref,
    eh_ref, el_ref, bh_ref, bl_ref,
):
    core, n = core_ref[0], pl.program_id(0)

    @pl.when(n == 0)
    def _():
        for part in range(2):
            at = pl.ds(part * 512, 512)
            gather_rows(
                e_ref, EROWS, part * 16, eh_ref.at[:, at], el_ref.at[:, at], x_ref.at[:, at], columns=4
            )

    held = (core == 0) == (n < GROUP)
    high, low = split(jnp.where(held, whole_block(mine_ref[:, 0]), whole_block(other_ref[:, 0])))
    high_ref[0], low_ref[0] = high, low
    value = dot3((eh_ref[...], el_ref[...]), (high, low), NT)

    @pl.when(n < GROUP)
    def _():
        bh_ref[pl.ds(n * NB, NB), :] = high
        bl_ref[pl.ds(n * NB, NB), :] = low
        scatter_rows(value, n, buf_ref)

    @pl.when(n >= GROUP)
    def _():
        first_ref[...] = value
        for j in range(GROUP):
            rows = slice(j * NB, j * NB + NB)
            ch_ref[rows, :], cl_ref[rows, :] = split(
                dot3((bh_ref[rows, :], bl_ref[rows, :]), (high, low), NT)
            )


def sum_chips(buf_ref, rows):
    def add(q, total):
        return total + buf_ref[q, :rows, :]

    return lax.fori_loop(0, NCHIP, add, jnp.zeros((rows, 128), F32), unroll=8)


def sum_projection(buf_ref, out_ref):
    out_ref[...] = sum_chips(buf_ref, PROWS)


def spread_to_chips(part_ref, out_ref, done, beside=None):
    copies = [pltpu.make_async_copy(part_ref, out_ref.at[q], done.at[q]) for q in range(NCHIP)]
    for copy in copies:
        copy.start()
    if beside is not None:
        beside()
    for copy in copies:
        copy.wait()


def spread_rows(part, out_ref):
    def spread(q, carry):
        out_ref[q] = part
        return carry

    lax.fori_loop(0, NCHIP, spread, 0, unroll=8)


def sum_products(buf_ref, out_ref, e_ref, part_ref, done):
    part_ref[...] = sum_chips(buf_ref, GROWS)

    def keep_eigenvectors():
        e_ref[...] = buf_ref[:, GROWS:, :]

    spread_to_chips(part_ref, out_ref, done, keep_eigenvectors)


def spread_found(core_ref, own_ref, sib_ref, out_ref):
    spread_rows(jnp.where(core_ref[0] == 0, own_ref[...], sib_ref[...]), out_ref)


def block_of(g_ref, i, j):
    halves = []
    for half in range(2):
        at, rows = PIECES[i, j, half]
        value = g_ref[at : at + rows, :]
        if rows < NB:
            value = jnp.concatenate([value, jnp.zeros((NB - rows, 128), F32)], axis=0)
        halves.append(value)
    return jnp.concatenate(halves, axis=1)


def invert(g_ref, out_ref, high_ref, low_ref):
    row = lax.broadcasted_iota(jnp.int32, (NB, NB), 0)
    col = lax.broadcasted_iota(jnp.int32, (NB, NB), 1)
    apart = row ^ col
    for index, (i, j) in enumerate(PAIRS):
        value = block_of(g_ref, i, j)
        if i == j:
            diagonal = jnp.where(row == col, 0.5 * value, 0.0)
            down = 1.0 / jnp.sum(diagonal, axis=1, keepdims=True)
            across = 1.0 / jnp.sum(diagonal, axis=0, keepdims=True)
            beside = jnp.where((apart == 1) & (row < col), value, 0.0)
            value = jnp.where(row == col, down, 0.0) - down * beside * across
        out_ref[index] = value
    size = 2
    while size < NB:
        for i in range(GROUP):
            index = PAIRS.index((i, i))
            beside = jnp.where((apart >= size) & (apart < 2 * size) & (row < col), block_of(g_ref, i, i), 0.0)
            value = out_ref[index]
            halves = split(value)
            product = dot3(split(dot3(halves, split(beside), NN)), halves, NN)
            out_ref[index] = value - product
        size *= 2
    for index in range(len(PAIRS)):
        high_ref[index], low_ref[index] = split(out_ref[index])


def pick_factors(core_ref, own_ref, sib_ref, high_ref, low_ref):
    high_ref[...], low_ref[...] = split(jnp.where(core_ref[0] == 1, own_ref[...], sib_ref[...]))


def solve(rows_of, high_ref, low_ref, keep):
    def factor(i, j):
        index = PAIRS.index((i, j))
        return high_ref[index], low_ref[index]

    found = {}
    for b in range(GROUP - 1, -1, -1):
        rest = jnp.concatenate([rows_of(b * 2), rows_of(b * 2 + 1)], axis=1)
        for later in range(GROUP - 1, b, -1):
            rest = rest - dot3(found[later], factor(b, later), NT)
        value = dot3(split(rest), factor(b, b), NT)
        found[b] = split(value)
        for half in range(2):
            keep(b * 2 + half, value[:, half * 128 : half * 128 + 128])


def solve_both(own_ref, sib_ref, high_ref, low_ref, c_own_ref, c_sib_ref):
    def rows_of(t):
        return jnp.concatenate([own_ref[t * 4 : t * 4 + 4, :], sib_ref[t * 4 : t * 4 + 4, :]], axis=0)

    def keep(t, value):
        c_own_ref[t * 4 : t * 4 + 4, :] = value[0:4]
        c_sib_ref[t * 4 : t * 4 + 4, :] = value[4:8]

    solve(rows_of, high_ref, low_ref, keep)


def solve_own(buf_ref, high_ref, low_ref, out_ref, c_ref):
    c_ref[...] = sum_chips(buf_ref, PROWS)

    def rows_of(t):
        return jnp.concatenate([c_ref[t * 4 : t * 4 + 4, :]] * 2, axis=0)

    def keep(t, value):
        c_ref[t * 4 : t * 4 + 4, :] = value[0:4]

    solve(rows_of, high_ref, low_ref, keep)
    spread_rows(c_ref[...], out_ref)


def correct_projection(c_ref, gh_ref, gl_ref, first_ref, buf_ref, ch_ref, cl_ref):
    n = pl.program_id(0)

    @pl.when(n == 0)
    def _():
        gather_rows(c_ref, PROWS, 0, ch_ref, cl_ref)

    value = first_ref[...] - dot3((ch_ref[...], cl_ref[...]), (gh_ref[...], gl_ref[...]), NN)
    scatter_rows(value, n, buf_ref)


def updated(c_ref, high_ref, low_ref, x_ref, ch_ref, cl_ref):
    @pl.when(pl.program_id(0) == 0)
    def _():
        gather_rows(c_ref, PROWS, 0, ch_ref, cl_ref)

    vectors = (high_ref[...].reshape(1024, 256), low_ref[...].reshape(1024, 256))
    return x_ref[...] - dot3((ch_ref[...], cl_ref[...]), vectors, NN)


def update(c_ref, high_ref, low_ref, x_ref, out_ref, ch_ref, cl_ref):
    out_ref[...] = updated(c_ref, high_ref, low_ref, x_ref, ch_ref, cl_ref)


def update_last(c_ref, high_ref, low_ref, x_ref, out_ref, ch_ref, cl_ref):
    value = updated(c_ref, high_ref, low_ref, x_ref, ch_ref, cl_ref)
    for c in range(NCOL):
        for i in range(4):
            out_ref[c, i * 8 : i * 8 + 8, :] = value[i * 64 + c * 8 : i * 64 + c * 8 + 8, :]


def pass_on(after_ref, in_ref, out_ref):
    pass


def place_rows(in_ref, out_ref, held_ref):
    for c in range(NCOL):
        for t in range(4):
            at = c * 512 + t * 128
            for core in range(2):
                for i in range(4):
                    held_ref[pl.ds((c * 4 + t) * 64 + core * 32 + i, 8, stride=4), :] = in_ref[
                        core * NCOL + c, i * 8 : i * 8 + 8, t * 128 : t * 128 + 128
                    ]
            out_ref[:, at : at + 128] = held_ref[(c * 4 + t) * 64 : (c * 4 + t) * 64 + 64, :]


def whole(*shape):
    return pl.BlockSpec(shape, lambda *_: (0,) * len(shape))


def run(kernel, out_shape, out_specs, in_specs, operands, grid=(1,), scratch=(), core=None, flops=0, size=0, limit=40, pin=(), **options):
    operands = [in_hbm(value) if at in pin else value for at, value in enumerate(operands)]
    spec = pltpu.PrefetchScalarGridSpec(
        num_scalar_prefetch=0 if core is None else 1,
        grid=grid,
        in_specs=in_specs,
        out_specs=out_specs,
        scratch_shapes=list(scratch),
    )
    built = pl.pallas_call(
        kernel,
        out_shape=out_shape,
        grid_spec=spec,
        compiler_params=pltpu.CompilerParams(vmem_limit_bytes=limit * 2**20),
        cost_estimate=pl.CostEstimate(flops=flops, bytes_accessed=size, transcendentals=0),
        **options,
    )
    return built(*operands) if core is None else built(core, *operands)


def in_hbm(value):
    return pltpu.with_memory_space_constraint(value, pltpu.HBM)


def exchange(value, axes):
    return lax.all_to_all(value, axes, 0, 0, tiled=True)


def on_device(eigenvectors, reflectors):
    core = lax.axis_index("core").astype(jnp.int32).reshape(1)
    mega = 2**20
    rows_pair = [pltpu.VMEM((256, 1024), BF16)] * 2

    def after(earlier, value, pin=(0,)):
        return run(
            pass_on, jax.ShapeDtypeStruct(value.shape, F32), ANY, [ANY, ANY], (earlier, value), pin=pin, input_output_aliases={1: 0}
        )

    vectors = run(
        cut_vectors,
        f32(2 * NCOL, GROUP, 32, 512),
        whole(2 * NCOL, GROUP, 32, 512),
        [HBM],
        (reflectors,),
        pin=(0,),
        scratch=[pltpu.SemaphoreType.DMA((2 * NCOL,))],
        size=8 * mega,
    )
    mine = exchange(vectors, CORE_COLS)
    other = lax.ppermute(mine, "core", SWAP)
    pieces = run(
        cut_eigenvectors, f32(NCHIP, EROWS, 128), whole(NCHIP, EROWS, 128), [whole(4, 65536)], (eigenvectors,), size=2 * mega
    )
    buf = run(
        inner_products,
        f32(NCHIP * STEP, 128),
        whole(NCHIP * STEP, 128),
        [pl.BlockSpec((2 * NCOL, 1, 32, 512), lambda b: (0, b, 0, 0)), whole(NCHIP, EROWS, 128)],
        (mine, pieces),
        grid=(GROUP,),
        scratch=[pltpu.VMEM((GROUP, NB, 1024), BF16)] * 2,
        flops=4 * 10**9,
        size=6 * mega,
    )
    arrived = exchange(after(other, buf).reshape(NCHIP, STEP, 128), CHIPS)

    part, spread = run(
        sum_products,
        (hbm(F32, NCHIP, GROWS, 128), f32(NCHIP, EROWS, 128)),
        (HBM, whole(NCHIP, EROWS, 128)),
        [whole(NCHIP, STEP, 128)],
        (arrived,),
        scratch=[pltpu.VMEM((GROWS, 128), F32), pltpu.SemaphoreType.DMA((NCHIP,))],
        size=5 * mega,
    )

    block = pl.BlockSpec((2 * NCOL, 1, 32, 512), lambda n, core: (0, lax.rem(n, GROUP), 0, 0))
    halves = pl.BlockSpec((1, NB, 1024), lambda n, core: (lax.rem(n + GROUP, 8), 0, 0))
    column = pl.BlockSpec((1024, NB), lambda n, core: (0, jnp.maximum(n - GROUP, 0)))
    high, low, start, buf, first, cross_high, cross_low = run(
        local_products,
        (
            hbm(BF16, 8, NB, 1024), hbm(BF16, 8, NB, 1024), hbm(F32, 256, 1024), hbm(F32, NCHIP * PROWS, 128),
            hbm(F32, 256, 1024), hbm(BF16, 1024, 1024), hbm(BF16, 1024, 1024),
        ),
        (
            halves, halves, whole(256, 1024), whole(NCHIP * PROWS, 128),
            pl.BlockSpec((256, NB), lambda n, core: (0, jnp.maximum(n - GROUP, 0))), column, column,
        ),
        [block, block, whole(NCHIP * EROWS, 128)],
        (mine, other, spread.reshape(NCHIP * EROWS, 128)),
        pin=(0, 1),
        grid=(8,),
        scratch=rows_pair + [pltpu.VMEM((1024, 1024), BF16)] * 2,
        core=core,
        flops=10**10,
        size=24 * mega,
    )
    gram = after(first, exchange(part, CHIPS)).reshape(ALLROWS, 128)

    count = len(PAIRS)
    factors, own_high, own_low = run(
        invert,
        (hbm(F32, count, NB, NB), bf16(count, NB, NB), bf16(count, NB, NB)),
        (whole(count, NB, NB),) * 3,
        [whole(ALLROWS, 128)],
        (gram,),
    )
    arrived = after(factors, exchange(after(gram, buf, (1,)).reshape(NCHIP, PROWS, 128), CHIPS))
    rows = f32(PROWS, 128)
    projection = run(sum_projection, rows, whole(PROWS, 128), [whole(NCHIP, PROWS, 128)], (arrived,), size=mega)
    found, found_sib = run(
        solve_both,
        (rows, rows),
        (whole(PROWS, 128),) * 2,
        [whole(PROWS, 128), whole(PROWS, 128), whole(count, NB, NB), whole(count, NB, NB)],
        (projection, lax.ppermute(projection, "core", SWAP), own_high, own_low),
        flops=10**8,
        size=3 * mega,
    )
    found = run(
        spread_found,
        f32(NCHIP, PROWS, 128),
        whole(NCHIP, PROWS, 128),
        [whole(PROWS, 128), whole(PROWS, 128)],
        (found, lax.ppermute(found_sib, "core", SWAP)),
        core=core,
        size=mega,
    )
    coefficients = exchange(found, CHIPS)
    factors = after(coefficients, factors, (1,))
    coefficients = coefficients.reshape(NCHIP * PROWS, 128)
    square = pl.BlockSpec((2, NB, NB), lambda n, core: (n, 0, 0))
    first_high, first_low = run(
        pick_factors,
        (hbm(BF16, count, NB, NB),) * 2,
        (square,) * 2,
        [square, square],
        (factors, lax.ppermute(factors, "core", SWAP)),
        grid=(count // 2,),
        core=core,
        size=8 * mega,
    )
    buf = run(
        correct_projection,
        f32(NCHIP * PROWS, 128),
        whole(NCHIP * PROWS, 128),
        [
            whole(NCHIP * PROWS, 128),
            pl.BlockSpec((1024, NB), lambda n: (0, n)),
            pl.BlockSpec((1024, NB), lambda n: (0, n)),
            pl.BlockSpec((256, NB), lambda n: (0, n)),
        ],
        (coefficients, cross_high, cross_low, first),
        pin=(1, 2, 3),
        grid=(GROUP,),
        scratch=rows_pair,
        flops=2 * 10**9,
        size=7 * mega,
    )

    def group(which):
        return pl.BlockSpec((GROUP, NB, NB), lambda n, *_: (which, 0, n))

    slab = pl.BlockSpec((256, NB), lambda n, *_: (0, n))
    middle = run(
        update,
        f32(256, 1024),
        slab,
        [whole(NCHIP * PROWS, 128), group(1), group(1), slab],
        (coefficients, high, low, start),
        pin=(1, 2, 3),
        grid=(4,),
        scratch=rows_pair,
        flops=2 * 10**9,
        size=7 * mega,
    )
    arrived = after(middle, after(first_high, exchange(buf.reshape(NCHIP, PROWS, 128), CHIPS)), ())
    found = run(
        solve_own,
        f32(NCHIP, PROWS, 128),
        whole(NCHIP, PROWS, 128),
        [whole(NCHIP, PROWS, 128), whole(count, NB, NB), whole(count, NB, NB)],
        (arrived, first_high, first_low),
        scratch=[pltpu.VMEM((PROWS, 128), F32)],
        flops=10**8,
        size=5 * mega,
    )
    coefficients = exchange(found, CHIPS).reshape(NCHIP * PROWS, 128)
    finished = run(
        update_last,
        f32(2 * NCOL, 32, 512),
        pl.BlockSpec((NCOL, 32, NB), lambda n: (n // 2, 0, lax.rem(n, 2))),
        [whole(NCHIP * PROWS, 128), group(0), group(0), slab],
        (coefficients, high, low, middle),
        pin=(1, 2),
        grid=(4,),
        scratch=rows_pair,
        flops=2 * 10**9,
        size=7 * mega,
    )
    return run(
        place_rows,
        f32(64, 4096),
        whole(64, 4096),
        [whole(2 * NCOL, 32, 512)],
        (exchange(finished, CORE_COLS),),
        scratch=[pltpu.VMEM((2048, 128), F32)],
        size=2 * mega,
    )


def solution(mesh):
    fine = Mesh(mesh.devices.reshape(SIZES), AXES)
    in_specs = (P(AXES, None), P(None, COLS, ("y", "xl", "core")))
    out_specs = P(COLS, ("y", "xl", "core"))
    return jax.shard_map(on_device, mesh=fine, in_specs=in_specs, out_specs=out_specs, check_vma=False)
```

time: 302 us -> 297 us (0.983)
  blocking collectives: 160 us -> 177 us
  waiting for transfers between devices: 42.6 us -> 29.9 us
  starting transfers between devices: 23.2 us -> 16.9 us
  local copies, waits for them, and re-layouts: 11.8 us -> 6.2 us
  Pallas kernels: 62.3 us -> 65.4 us
    all_to_all x5, blocking collectives: 160 us -> 177 us  [exchange(): return lax.all_to_all(value, axes, 0, 0, tiled=True)]
    all_to_all x4 -> x3, waiting for transfers between devices: 42.6 us -> 25.9 us  [exchange(): return lax.all_to_all(value, axes, 0, 0, tiled=True)]
    all_to_all x4 -> x3, starting transfers between devices: 23.1 us -> 16.8 us  [exchange(): return lax.all_to_all(value, axes, 0, 0, tiled=True)]
    unnamed x32 -> x20, local copies, waits for them, and re-layouts: 11.8 us -> 6.2 us
    ppermute x2 -> x4, waiting for transfers between devices: 0.01 us -> 4.01 us  [the longest x1 1.62 us: on_device(): other = lax.ppermute(mine, 'core', SWAP)]
    pallas_call x16 -> x22, Pallas kernels: 62.3 us -> 65.4 us  [run(): return built(*operands) if core is None else built(core, *operands)]
  transfers between devices with their start and end apart: 6 -> 7, of which waited for: 4 -> 6; matrix products, arithmetic and copies ran while one was open for 0% -> 0% of each run, Pallas kernels for 12% -> 17%
where the time goes in v2:
time: 297 us; the launch traced here: 296 us
  blocking collectives  177 us (60%)
  Pallas kernels  65.4 us (22%)
  waiting for transfers between devices  29.9 us (10%)
  starting transfers between devices  16.9 us (6%)
  local copies, waits for them, and re-layouts  6.2 us (2%)
    all_to_all x5, blocking collectives, exchange(): return lax.all_to_all(value, axes, 0, 0, tiled=True)  177 us
    pallas_call x22, Pallas kernels, run(): return built(*operands) if core is None else built(core, *operands)  65.4 us
    all_to_all x3, waiting for transfers between devices, exchange(): return lax.all_to_all(value, axes, 0, 0, tiled=True)  25.9 us
    all_to_all x3, starting transfers between devices, exchange(): return lax.all_to_all(value, axes, 0, 0, tiled=True)  16.8 us
    unnamed x20, local copies, waits for them, and re-layouts  6.2 us
  transfers between devices with their start and end apart: 7, of which 6 were waited for; matrix products, arithmetic and copies ran while one was open for 0% of the time, Pallas kernels for 17%

profile of v2, /device:TPU:0, one launch (start us, length us, event | category | flops | bytes accessed | tf_op | source)
XLA Modules:
  0.0 295.9 jit_solution(14279960096769103426)
XLA Ops:
  0.0 2.3 shard_map.28
  2.3 58.9 %all_to_all.40.w_ref.mine_ref = f32[16,4,32,512]{3,2,1,0:T(8,128)S(1)} all-to-all(f32[16,4,32,512]{3,2,1,0:T(8,128)S(1)} %shard_map.28), channel_id=1, replica_groups=mesh['y'=4,'xl'=2,'core'=2,'z'=4,'xh'=2] {'core','z','xh'}, dimensions={0} | all-to-all | bytes 8388608 | tf_op jit(solution)/shard_map/all_to_all | solution.py:379
  61.3 5.4 %shard_map.30.in_ref = f32[6656,128]{1,0:T(8,128)S(1)} custom-call(f32[16,4,32,512]{3,2,1,0:T(8,128)S(1)} %all_to_all.40.w_ref.mine_ref, f32[64,32,128]{2,1,0:T(8,128)S(1)} %shard_map.29.e_ref), custom_call_target="tpu_custom_call" | custom-call | flops 4000000000 | bytes 6291456 | tf_op jit(solution)/shard_map/pallas_call | solution.py:371
  66.8 1.6 collective-permute-done.after_ref.other_ref
  68.4 1.9 copy-done.9
  70.4 50.7 %all_to_all.41.buf_ref = f32[64,104,128]{2,1,0:T(8,128)S(1)} all-to-all(f32[64,104,128]{2,1,0:T(8,128)S(1)} %bitcast.10), channel_id=1, replica_groups=mesh['y'=4,'xl'=2,'core'=2,'z'=4,'xh'=2] {'y','xl','z','xh'}, dimensions={0} | all-to-all | bytes 6815744 | tf_op jit(solution)/shard_map/all_to_all | solution.py:379
  121.1 2.1 shard_map.32
  123.2 5.5 %all-to-all-start.2 = ((f32[64,72,128]{2,1,0:T(8,128)}), f32[64,72,128]{2,1,0:T(8,128)S(1)}, u32[]{:S(2)}, u32[]{:S(2)}) async-start(f32[64,72,128]{2,1,0:T(8,128)} %get-tuple-element.23), calls=%async_computation.2 | async-start | bytes 4718592 | tf_op jit(solution)/shard_map/all_to_all | solution.py:379
  128.7 20.5 %shard_map.33 = (bf16[8,256,1024]{2,1,0:T(8,128)(2,1)}, bf16[8,256,1024]{2,1,0:T(8,128)(2,1)}, f32[256,1024]{1,0:T(8,128)}, f32[2048,128]{1,0:T(8,128)}, f32[256...) custom-call(s32[1]{0:T(128)} %bitcast.core_ref, f32[16,4,32,512]{3,2,1,0:T(8,128)} %copy-done.2, ...), custom_call_target="tpu_custom_call" | custom-call | flops 10000000000 | bytes 25165824 | tf_op jit(solution)/shard_map/pallas_call | solution.py:371
  149.2 10.5 %all-to-all-done.2.in_ref = f32[64,72,128]{2,1,0:T(8,128)S(1)} async-done(((f32[64,72,128]{2,1,0:T(8,128)}), f32[64,72,128]{2,1,0:T(8,128)S(1)}, u32[]{:S(2)}, u32[]{:S(2)}) %all-to-all-start.2) | async-done | bytes 2359328 | tf_op jit(solution)/shard_map/all_to_all | solution.py:379
  159.8 5.6 %all-to-all-start.3 = ((f32[64,32,128]{2,1,0:T(8,128)}), f32[64,32,128]{2,1,0:T(8,128)S(1)}, u32[]{:S(2)}, u32[]{:S(2)}) async-start(f32[64,32,128]{2,1,0:T(8,128)} %bitcast.15), calls=%async_computation.3 | async-start | bytes 2097152 | tf_op jit(solution)/shard_map/all_to_all | solution.py:379
  165.4 8.0 %shard_map.35 = (f32[10,256,256]{2,1,0:T(8,128)}, bf16[10,256,256]{2,1,0:T(8,128)(2,1)S(1)}, bf16[10,256,256]{2,1,0:T(8,128)(2,1)S(1)}) custom-call(f32[4608,128]{1,0:T(8,128)S(1)} %bitcast.9), custom_call_target="tpu_custom_call" | custom-call | tf_op jit(solution)/shard_map/pallas_call | solution.py:371
  175.6 6.7 %all-to-all-done.3.in_ref = f32[64,32,128]{2,1,0:T(8,128)S(1)} async-done(((f32[64,32,128]{2,1,0:T(8,128)}), f32[64,32,128]{2,1,0:T(8,128)S(1)}, u32[]{:S(2)}, u32[]{:S(2)}) %all-to-all-start.3) | async-done | bytes 1048608 | tf_op jit(solution)/shard_map/all_to_all | solution.py:379
  184.0 1.8 shard_map.39
  187.1 24.0 %all_to_all.42.after_ref = f32[64,32,128]{2,1,0:T(8,128)S(1)} all-to-all(f32[64,32,128]{2,1,0:T(8,128)S(1)} %shard_map.40), channel_id=1, replica_groups=mesh['y'=4,'xl'=2,'core'=2,'z'=4,'xh'=2] {'y','xl','z','xh'}, dimensions={0} | all-to-all | bytes 2097152 | tf_op jit(solution)/shard_map/all_to_all | solution.py:379
  211.1 6.5 %shard_map.44 = f32[2048,128]{1,0:T(8,128)} custom-call(f32[2048,128]{1,0:T(8,128)S(1)} %bitcast.11, bf16[1024,1024]{1,0:T(8,128)(2,1)} %get-tuple-element.34.gh_ref, bf16[1024,1024]{1,0:T(8,128)(2,1)} %get-tuple-element.35.gl_ref, f32[256,1024]{1,0:T(8,128)} %get-tuple-element.22.after_ref.first_ref), custom_call_target="tpu_custom_call" | custom-call | flops 2000000000 | bytes 7340032 | tf_op jit(solution)/shard_map/pallas_call | solution.py:371
  217.6 5.7 %all-to-all-start.5 = ((f32[64,32,128]{2,1,0:T(8,128)}), f32[64,32,128]{2,1,0:T(8,128)S(1)}, u32[]{:S(2)}, u32[]{:S(2)}) async-start(f32[64,32,128]{2,1,0:T(8,128)} %bitcast.6), calls=%async_computation.5 | async-start | bytes 2097152 | tf_op jit(solution)/shard_map/all_to_all | solution.py:379
  223.3 5.4 %shard_map.41.after_ref.x_ref = f32[256,1024]{1,0:T(8,128)S(1)} custom-call(f32[2048,128]{1,0:T(8,128)S(1)} %bitcast.12, bf16[8,256,1024]{2,1,0:T(8,128)(2,1)} %get-tuple-element.30.high_ref, bf16[8,256,1024]{2,1,0:T(8,128)(2,1)} %get-tuple-element.31.low_ref, f32[256,1024]{1,0:T(8,128)} %get-tuple-element.32.x_ref), custom_call_target="tpu_custom_call" | custom-call | flops 2000000000 | bytes 7340032 | tf_op jit(solution)/shard_map/pallas_call | solution.py:371
  228.7 4.8 %shard_map.43 = (bf16[10,256,256]{2,1,0:T(8,128)(2,1)}, bf16[10,256,256]{2,1,0:T(8,128)(2,1)}) custom-call(s32[1]{0:T(128)} %bitcast.core_ref, f32[10,256,256]{2,1,0:T(8,128)S(1)} %copy-done, f32[10,256,256]{2,1,0:T(8,128)} %collective-permute-done.3.sib_ref), custom_call_target="tpu_custom_call" | custom-call | bytes 8388608 | tf_op jit(solution)/shard_map/pallas_call | solution.py:371
  233.5 8.7 %all-to-all-done.5.in_ref = f32[64,32,128]{2,1,0:T(8,128)S(1)} async-done(((f32[64,32,128]{2,1,0:T(8,128)}), f32[64,32,128]{2,1,0:T(8,128)S(1)}, u32[]{:S(2)}, u32[]{:S(2)}) %all-to-all-start.5) | async-done | bytes 1048608 | tf_op jit(solution)/shard_map/all_to_all | solution.py:379
  243.9 2.0 shard_map.47
  245.9 22.8 %all_to_all.43 = f32[64,32,128]{2,1,0:T(8,128)S(1)} all-to-all(f32[64,32,128]{2,1,0:T(8,128)S(1)} %shard_map.47), channel_id=1, replica_groups=mesh['y'=4,'xl'=2,'core'=2,'z'=4,'xh'=2] {'y','xl','z','xh'}, dimensions={0} | all-to-all | bytes 2097152 | tf_op jit(solution)/shard_map/all_to_all | solution.py:379
  268.7 5.1 %shard_map.48 = f32[16,32,512]{2,1,0:T(8,128)S(1)} custom-call(f32[2048,128]{1,0:T(8,128)S(1)} %bitcast.13, bf16[8,256,1024]{2,1,0:T(8,128)(2,1)} %get-tuple-element.30.high_ref, bf16[8,256,1024]{2,1,0:T(8,128)(2,1)} %get-tuple-element.31.low_ref, f32[256,1024]{1,0:T(8,128)S(1)} %shard_map.41.after_ref.x_ref), custom_call_target="tpu_custom_call" | custom-call | flops 2000000000 | bytes 7340032 | tf_op jit(solution)/shard_map/pallas_call | solution.py:371
  273.8 20.9 %all_to_all.44.in_ref = f32[16,32,512]{2,1,0:T(8,128)S(1)} all-to-all(f32[16,32,512]{2,1,0:T(8,128)S(1)} %shard_map.48), channel_id=1, replica_groups=mesh['y'=4,'xl'=2,'core'=2,'z'=4,'xh'=2] {'core','z','xh'}, dimensions={0} | all-to-all | bytes 2097152 | tf_op jit(solution)/shard_map/all_to_all | solution.py:379
  (37 shorter events, 8.2 us)
Async XLA Ops:
  2.3 59.0 %copy-start.8 = (f32[4,65536]{1,0:T(4,128)S(1)}, f32[4,65536]{1,0:T(4,128)}, u32[]{:S(2)}) copy-start(f32[4,65536]{1,0:T(4,128)} %e_ref.1) | copy-start | bytes 3145732
  61.2 5.5 %copy-start.2 = (f32[16,4,32,512]{3,2,1,0:T(8,128)}, f32[16,4,32,512]{3,2,1,0:T(8,128)S(1)}, u32[]{:S(2)}) copy-start(f32[16,4,32,512]{3,2,1,0:T(8,128)S(1)} %all_to_all.40.w_ref.mine_ref) | copy-start | bytes 12582916
  61.2 7.2 %collective-permute-start = (f32[16,4,32,512]{3,2,1,0:T(8,128)S(1)}, f32[16,4,32,512]{3,2,1,0:T(8,128)S(1)}, u32[]{:S(2)}, u32[]{:S(2)}) collective-permute-start(f32[16,4,32,512]{3,2,1,0:T(8,128)S(1)} %all_to_all.40.w_ref.mine_ref), channel_id=1, source_target_pairs={{0,8},{8,0},{1,9},{9,1},{2,10},{10,2},{3,11},{11,3},{4,12},{12,4},... | collective-permute-start | bytes 12582920 | tf_op jit(solution)/shard_map/ppermute | solution.py:403
  68.4 1.9 copy-start.9
  123.2 36.6 %all-to-all-start.2 = ((f32[64,72,128]{2,1,0:T(8,128)}), f32[64,72,128]{2,1,0:T(8,128)S(1)}, u32[]{:S(2)}, u32[]{:S(2)}) async-start(f32[64,72,128]{2,1,0:T(8,128)} %get-tuple-element.23), calls=%async_computation.2 | async-start | bytes 4718592 | tf_op jit(solution)/shard_map/all_to_all | solution.py:379
  159.8 22.5 %all-to-all-start.3 = ((f32[64,32,128]{2,1,0:T(8,128)}), f32[64,32,128]{2,1,0:T(8,128)S(1)}, u32[]{:S(2)}, u32[]{:S(2)}) async-start(f32[64,32,128]{2,1,0:T(8,128)} %bitcast.15), calls=%async_computation.3 | async-start | bytes 2097152 | tf_op jit(solution)/shard_map/all_to_all | solution.py:379
  173.4 1.1 copy-start.4
  174.5 1.1 copy-start.6
  182.3 1.4 copy-start.5
  182.3 1.7 copy-start.7
  182.4 1.3 collective-permute-start.1
  185.8 1.2 collective-permute-start.2
  211.1 17.6 %collective-permute-start.3 = (f32[10,256,256]{2,1,0:T(8,128)}, f32[10,256,256]{2,1,0:T(8,128)}, u32[]{:S(2)}, u32[]{:S(2)}) collective-permute-start(f32[10,256,256]{2,1,0:T(8,128)} %shard_map.42.own_ref), channel_id=1, source_target_pairs={{0,8},{8,0},{1,9},{9,1},{2,10},{10,2},{3,11},{11,3},{4,12},{12,4},... | collective-permute-start | bytes 7864328 | tf_op jit(solution)/shard_map/ppermute | solution.py:492
  217.6 24.6 %all-to-all-start.5 = ((f32[64,32,128]{2,1,0:T(8,128)}), f32[64,32,128]{2,1,0:T(8,128)S(1)}, u32[]{:S(2)}, u32[]{:S(2)}) async-start(f32[64,32,128]{2,1,0:T(8,128)} %bitcast.6), calls=%async_computation.5 | async-start | bytes 2097152 | tf_op jit(solution)/shard_map/all_to_all | solution.py:379
  223.3 5.4 %copy-start = (f32[10,256,256]{2,1,0:T(8,128)S(1)}, f32[10,256,256]{2,1,0:T(8,128)}, u32[]{:S(2)}) copy-start(f32[10,256,256]{2,1,0:T(8,128)} %shard_map.42.own_ref) | copy-start | bytes 7864324
  242.1 1.3 copy-start.1
  242.1 1.7 copy-start.3

commit v3 on v2

--- a/solution.py
+++ b/solution.py
@@ -36,6 +36,7 @@
 PROWS = 32
 ANY = pl.BlockSpec(memory_space=pl.ANY)
 HBM = pl.BlockSpec(memory_space=pltpu.HBM)
+VMEM = pl.BlockSpec(memory_space=pltpu.VMEM)
 F32 = jnp.float32
 BF16 = jnp.bfloat16
 NT = (((1,), (1,)), ((), ()))
@@ -66,7 +67,7 @@
     return one(a[0], b[0]) + (one(a[0], b[1]) + one(a[1], b[0]))
 
 
-def cut_eigenvectors(e_ref, out_ref):
+def cut_eigenvectors(after_ref, e_ref, out_ref):
     for core in range(2):
         for c in range(NCOL):
             for t in range(4):
@@ -96,9 +97,11 @@
     return jnp.concatenate([value[:NCOL].reshape(NB, 512), value[NCOL:].reshape(NB, 512)], axis=1)
 
 
-def inner_products(w_ref, e_ref, buf_ref, high_ref, low_ref):
-    def block(j):
-        high_ref[j], low_ref[j] = split(whole_block(w_ref[:, 0]))
+def inner_products(w_ref, e_ref, buf_ref, kept_ref, high_ref, low_ref, done):
+    keep = pltpu.make_async_copy(w_ref, kept_ref, done)
+    keep.start()
+    for j in range(GROUP):
+        high_ref[j], low_ref[j] = split(whole_block(w_ref[:, j]))
         for i in range(j + 1):
             value = dot3((high_ref[i], low_ref[i]), (high_ref[j], low_ref[j]), NT)
             for half in range(2):
@@ -110,14 +113,9 @@
                     start = chip * STEP + offset
                     buf_ref[start : start + take, :] = value[done : done + take, half * 128 : half * 128 + 128]
                     done += take
-
-    for j in range(GROUP):
-        pl.when(pl.program_id(0) == j)(lambda j=j: block(j))
-
-    @pl.when(pl.program_id(0) == 0)
-    def _():
-        for q in range(NCHIP):
-            buf_ref[q * STEP + GROWS : q * STEP + STEP, :] = e_ref[q]
+    for q in range(NCHIP):
+        buf_ref[q * STEP + GROWS : q * STEP + STEP, :] = e_ref[q]
+    keep.wait()
 
 
 def gather_rows(ref, step, first, high_ref, low_ref, value_ref=None, columns=8):
@@ -142,7 +140,7 @@
 
 def local_products(
     core_ref, mine_ref, other_ref, e_ref,
-    high_ref, low_ref, x_ref, buf_ref, first_ref, ch_ref, cl_ref,
+    high_b_ref, low_b_ref, high_a_ref, low_a_ref, x_ref, buf_ref, first_ref, ch_ref, cl_ref,
     eh_ref, el_ref, bh_ref, bl_ref,
 ):
     core, n = core_ref[0], pl.program_id(0)
@@ -157,17 +155,18 @@
 
     held = (core == 0) == (n < GROUP)
     high, low = split(jnp.where(held, whole_block(mine_ref[:, 0]), whole_block(other_ref[:, 0])))
-    high_ref[0], low_ref[0] = high, low
     value = dot3((eh_ref[...], el_ref[...]), (high, low), NT)
 
     @pl.when(n < GROUP)
     def _():
+        high_b_ref[0], low_b_ref[0] = high, low
         bh_ref[pl.ds(n * NB, NB), :] = high
         bl_ref[pl.ds(n * NB, NB), :] = low
         scatter_rows(value, n, buf_ref)
 
     @pl.when(n >= GROUP)
     def _():
+        high_a_ref[0], low_a_ref[0] = high, low
         first_ref[...] = value
         for j in range(GROUP):
             rows = slice(j * NB, j * NB + NB)
@@ -301,34 +300,34 @@
 
 
 def correct_projection(c_ref, gh_ref, gl_ref, first_ref, buf_ref, ch_ref, cl_ref):
-    n = pl.program_id(0)
-
-    @pl.when(n == 0)
-    def _():
-        gather_rows(c_ref, PROWS, 0, ch_ref, cl_ref)
-
-    value = first_ref[...] - dot3((ch_ref[...], cl_ref[...]), (gh_ref[...], gl_ref[...]), NN)
-    scatter_rows(value, n, buf_ref)
-
-
-def updated(c_ref, high_ref, low_ref, x_ref, ch_ref, cl_ref):
-    @pl.when(pl.program_id(0) == 0)
-    def _():
-        gather_rows(c_ref, PROWS, 0, ch_ref, cl_ref)
-
-    vectors = (high_ref[...].reshape(1024, 256), low_ref[...].reshape(1024, 256))
-    return x_ref[...] - dot3((ch_ref[...], cl_ref[...]), vectors, NN)
+    gather_rows(c_ref, PROWS, 0, ch_ref, cl_ref)
+    for n in range(GROUP):
+        at = slice(n * NB, n * NB + NB)
+        value = first_ref[:, at] - dot3((ch_ref[...], cl_ref[...]), (gh_ref[:, at], gl_ref[:, at]), NN)
+        scatter_rows(value, n, buf_ref)
+
+
+def updated(n, high_ref, low_ref, x_ref, ch_ref, cl_ref):
+    at = slice(n * NB, n * NB + NB)
+    vectors = (high_ref[:, :, at].reshape(1024, NB), low_ref[:, :, at].reshape(1024, NB))
+    return x_ref[:, at] - dot3((ch_ref[...], cl_ref[...]), vectors, NN)
 
 
 def update(c_ref, high_ref, low_ref, x_ref, out_ref, ch_ref, cl_ref):
-    out_ref[...] = updated(c_ref, high_ref, low_ref, x_ref, ch_ref, cl_ref)
+    gather_rows(c_ref, PROWS, 0, ch_ref, cl_ref)
+    for n in range(4):
+        out_ref[:, n * NB : n * NB + NB] = updated(n, high_ref, low_ref, x_ref, ch_ref, cl_ref)
 
 
 def update_last(c_ref, high_ref, low_ref, x_ref, out_ref, ch_ref, cl_ref):
-    value = updated(c_ref, high_ref, low_ref, x_ref, ch_ref, cl_ref)
-    for c in range(NCOL):
-        for i in range(4):
-            out_ref[c, i * 8 : i * 8 + 8, :] = value[i * 64 + c * 8 : i * 64 + c * 8 + 8, :]
+    gather_rows(c_ref, PROWS, 0, ch_ref, cl_ref)
+    for n in range(4):
+        value = updated(n, high_ref, low_ref, x_ref, ch_ref, cl_ref)
+        at = n % 2 * NB
+        for c in range(NCOL):
+            for i in range(4):
+                rows = slice(i * 64 + c * 8, i * 64 + c * 8 + 8)
+                out_ref[n // 2 * NCOL + c, i * 8 : i * 8 + 8, at : at + NB] = value[rows, :]
 
 
 def pass_on(after_ref, in_ref, out_ref):
@@ -351,7 +350,7 @@
     return pl.BlockSpec(shape, lambda *_: (0,) * len(shape))
 
 
-def run(kernel, out_shape, out_specs, in_specs, operands, grid=(1,), scratch=(), core=None, flops=0, size=0, limit=40, pin=(), **options):
+def run(kernel, out_shape, out_specs, in_specs, operands, grid=(1,), scratch=(), core=None, flops=0, size=0, limit=32, pin=(), **options):
     operands = [in_hbm(value) if at in pin else value for at, value in enumerate(operands)]
     spec = pltpu.PrefetchScalarGridSpec(
         num_scalar_prefetch=0 if core is None else 1,
@@ -371,6 +370,18 @@
     return built(*operands) if core is None else built(core, *operands)
 
 
+def direct(kernel, out_shape, operands, scratch=(), out_specs=None, flops=0, size=0, limit=32):
+    return pl.pallas_call(
+        kernel,
+        out_shape=out_shape,
+        in_specs=[VMEM] * len(operands),
+        out_specs=jax.tree.map(lambda _: VMEM, out_shape) if out_specs is None else out_specs,
+        scratch_shapes=list(scratch),
+        compiler_params=pltpu.CompilerParams(vmem_limit_bytes=limit * 2**20),
+        cost_estimate=pl.CostEstimate(flops=flops, bytes_accessed=size, transcendentals=0),
+    )(*operands)
+
+
 def in_hbm(value):
     return pltpu.with_memory_space_constraint(value, pltpu.HBM)
 
@@ -386,7 +397,7 @@
 
     def after(earlier, value, pin=(0,)):
         return run(
-            pass_on, jax.ShapeDtypeStruct(value.shape, F32), ANY, [ANY, ANY], (earlier, value), pin=pin, input_output_aliases={1: 0}
+            pass_on, jax.ShapeDtypeStruct(value.shape, F32), ANY, [ANY, ANY], (earlier, value), pin=pin, size=1024, input_output_aliases={1: 0}
         )
 
     vectors = run(
@@ -400,22 +411,25 @@
         size=8 * mega,
     )
     mine = exchange(vectors, CORE_COLS)
-    other = lax.ppermute(mine, "core", SWAP)
     pieces = run(
-        cut_eigenvectors, f32(NCHIP, EROWS, 128), whole(NCHIP, EROWS, 128), [whole(4, 65536)], (eigenvectors,), size=2 * mega
-    )
-    buf = run(
+        cut_eigenvectors,
+        f32(NCHIP, EROWS, 128),
+        whole(NCHIP, EROWS, 128),
+        [ANY, whole(4, 65536)],
+        (mine, eigenvectors),
+        size=2 * mega,
+    )
+    buf, kept = direct(
         inner_products,
-        f32(NCHIP * STEP, 128),
-        whole(NCHIP * STEP, 128),
-        [pl.BlockSpec((2 * NCOL, 1, 32, 512), lambda b: (0, b, 0, 0)), whole(NCHIP, EROWS, 128)],
+        (f32(NCHIP * STEP, 128), hbm(F32, 2 * NCOL, GROUP, 32, 512)),
         (mine, pieces),
-        grid=(GROUP,),
-        scratch=[pltpu.VMEM((GROUP, NB, 1024), BF16)] * 2,
+        scratch=[pltpu.VMEM((GROUP, NB, 1024), BF16)] * 2 + [pltpu.SemaphoreType.DMA(())],
+        out_specs=(VMEM, HBM),
         flops=4 * 10**9,
         size=6 * mega,
     )
-    arrived = exchange(after(other, buf).reshape(NCHIP, STEP, 128), CHIPS)
+    other = lax.ppermute(kept, "core", SWAP)
+    arrived = exchange(buf.reshape(NCHIP, STEP, 128), CHIPS)
 
     part, spread = run(
         sum_products,
@@ -428,20 +442,22 @@
     )
 
     block = pl.BlockSpec((2 * NCOL, 1, 32, 512), lambda n, core: (0, lax.rem(n, GROUP), 0, 0))
-    halves = pl.BlockSpec((1, NB, 1024), lambda n, core: (lax.rem(n + GROUP, 8), 0, 0))
+    early = pl.BlockSpec((1, NB, 1024), lambda n, core: (jnp.minimum(n, GROUP - 1), 0, 0))
+    late = pl.BlockSpec((1, NB, 1024), lambda n, core: (jnp.maximum(n - GROUP, 0), 0, 0))
     column = pl.BlockSpec((1024, NB), lambda n, core: (0, jnp.maximum(n - GROUP, 0)))
-    high, low, start, buf, first, cross_high, cross_low = run(
+    split_vectors = hbm(BF16, GROUP, NB, 1024)
+    high_b, low_b, high_a, low_a, start, buf, first, cross_high, cross_low = run(
         local_products,
         (
-            hbm(BF16, 8, NB, 1024), hbm(BF16, 8, NB, 1024), hbm(F32, 256, 1024), hbm(F32, NCHIP * PROWS, 128),
-            hbm(F32, 256, 1024), hbm(BF16, 1024, 1024), hbm(BF16, 1024, 1024),
+            split_vectors, split_vectors, split_vectors, split_vectors, hbm(F32, 256, 1024),
+            hbm(F32, NCHIP * PROWS, 128), hbm(F32, 256, 1024), hbm(BF16, 1024, 1024), hbm(BF16, 1024, 1024),
         ),
         (
-            halves, halves, whole(256, 1024), whole(NCHIP * PROWS, 128),
+            early, early, late, late, whole(256, 1024), whole(NCHIP * PROWS, 128),
             pl.BlockSpec((256, NB), lambda n, core: (0, jnp.maximum(n - GROUP, 0))), column, column,
         ),
         [block, block, whole(NCHIP * EROWS, 128)],
-        (mine, other, spread.reshape(NCHIP * EROWS, 128)),
+        (kept, other, spread.reshape(NCHIP * EROWS, 128)),
         pin=(0, 1),
         grid=(8,),
         scratch=rows_pair + [pltpu.VMEM((1024, 1024), BF16)] * 2,
@@ -449,7 +465,7 @@
         flops=10**10,
         size=24 * mega,
     )
-    gram = after(first, exchange(part, CHIPS)).reshape(ALLROWS, 128)
+    gram = after(buf, exchange(part, CHIPS)).reshape(ALLROWS, 128)
 
     count = len(PAIRS)
     factors, own_high, own_low = run(
@@ -462,11 +478,9 @@
     arrived = after(factors, exchange(after(gram, buf, (1,)).reshape(NCHIP, PROWS, 128), CHIPS))
     rows = f32(PROWS, 128)
     projection = run(sum_projection, rows, whole(PROWS, 128), [whole(NCHIP, PROWS, 128)], (arrived,), size=mega)
-    found, found_sib = run(
+    found, found_sib = direct(
         solve_both,
         (rows, rows),
-        (whole(PROWS, 128),) * 2,
-        [whole(PROWS, 128), whole(PROWS, 128), whole(count, NB, NB), whole(count, NB, NB)],
         (projection, lax.ppermute(projection, "core", SWAP), own_high, own_low),
         flops=10**8,
         size=3 * mega,
@@ -486,7 +500,7 @@
     square = pl.BlockSpec((2, NB, NB), lambda n, core: (n, 0, 0))
     first_high, first_low = run(
         pick_factors,
-        (hbm(BF16, count, NB, NB),) * 2,
+        (bf16(count, NB, NB),) * 2,
         (square,) * 2,
         [square, square],
         (factors, lax.ppermute(factors, "core", SWAP)),
@@ -494,60 +508,36 @@
         core=core,
         size=8 * mega,
     )
-    buf = run(
+    buf = direct(
         correct_projection,
         f32(NCHIP * PROWS, 128),
-        whole(NCHIP * PROWS, 128),
-        [
-            whole(NCHIP * PROWS, 128),
-            pl.BlockSpec((1024, NB), lambda n: (0, n)),
-            pl.BlockSpec((1024, NB), lambda n: (0, n)),
-            pl.BlockSpec((256, NB), lambda n: (0, n)),
-        ],
         (coefficients, cross_high, cross_low, first),
-        pin=(1, 2, 3),
-        grid=(GROUP,),
         scratch=rows_pair,
         flops=2 * 10**9,
         size=7 * mega,
     )
-
-    def group(which):
-        return pl.BlockSpec((GROUP, NB, NB), lambda n, *_: (which, 0, n))
-
-    slab = pl.BlockSpec((256, NB), lambda n, *_: (0, n))
-    middle = run(
+    middle = direct(
         update,
         f32(256, 1024),
-        slab,
-        [whole(NCHIP * PROWS, 128), group(1), group(1), slab],
-        (coefficients, high, low, start),
-        pin=(1, 2, 3),
-        grid=(4,),
+        (coefficients, high_b, low_b, start),
         scratch=rows_pair,
         flops=2 * 10**9,
         size=7 * mega,
     )
-    arrived = after(middle, after(first_high, exchange(buf.reshape(NCHIP, PROWS, 128), CHIPS)), ())
-    found = run(
+    arrived = after(middle, after(first_high, exchange(buf.reshape(NCHIP, PROWS, 128), CHIPS), ()), ())
+    found = direct(
         solve_own,
         f32(NCHIP, PROWS, 128),
-        whole(NCHIP, PROWS, 128),
-        [whole(NCHIP, PROWS, 128), whole(count, NB, NB), whole(count, NB, NB)],
         (arrived, first_high, first_low),
         scratch=[pltpu.VMEM((PROWS, 128), F32)],
         flops=10**8,
         size=5 * mega,
     )
     coefficients = exchange(found, CHIPS).reshape(NCHIP * PROWS, 128)
-    finished = run(
+    finished = direct(
         update_last,
         f32(2 * NCOL, 32, 512),
-        pl.BlockSpec((NCOL, 32, NB), lambda n: (n // 2, 0, lax.rem(n, 2))),
-        [whole(NCHIP * PROWS, 128), group(0), group(0), slab],
-        (coefficients, high, low, middle),
-        pin=(1, 2),
-        grid=(4,),
+        (coefficients, high_a, low_a, middle),
         scratch=rows_pair,
         flops=2 * 10**9,
         size=7 * mega,

time: 297 us -> 291 us (0.980)
  blocking collectives: 177 us -> 126 us
  waiting for transfers between devices: 29.9 us -> 70.2 us
  Pallas kernels: 65.4 us -> 55.1 us
  local copies, waits for them, and re-layouts: 6.2 us -> 14.1 us
  starting transfers between devices: 16.9 us -> 24.4 us
    all_to_all x5 -> x4, blocking collectives: 177 us -> 126 us  [exchange(): return lax.all_to_all(value, axes, 0, 0, tiled=True)]
    all_to_all x3 -> x4, waiting for transfers between devices: 25.9 us -> 67.8 us  [exchange(): return lax.all_to_all(value, axes, 0, 0, tiled=True)]
    pallas_call x22 -> x15, Pallas kernels: 65.4 us -> 38.6 us  [run(): return built(*operands) if core is None else built(core, *operands)]
    pallas_call x0 -> x6, Pallas kernels: none -> 16.5 us  [direct(): pl.pallas_call(kernel, out_shape=out_shape, in_specs=[VMEM] * len(operand...]
    unnamed x20 -> x42, local copies, waits for them, and re-layouts: 6.2 us -> 14.1 us
    all_to_all x3 -> x4, starting transfers between devices: 16.8 us -> 24.1 us  [exchange(): return lax.all_to_all(value, axes, 0, 0, tiled=True)]
  transfers between devices with their start and end apart: 7 -> 8, of which waited for: 6 -> 6; matrix products, arithmetic and copies ran while one was open for 0% -> 0% of each run, Pallas kernels for 17% -> 14%
where the time goes in v3:
time: 291 us; the launch traced here: 290 us
  blocking collectives  126 us (43%)
  waiting for transfers between devices  70.2 us (24%)
  Pallas kernels  55.1 us (19%)
  starting transfers between devices  24.4 us (8%)
  local copies, waits for them, and re-layouts  14.1 us (5%)
    all_to_all x4, blocking collectives, exchange(): return lax.all_to_all(value, axes, 0, 0, tiled=True)  126 us
    all_to_all x4, waiting for transfers between devices, exchange(): return lax.all_to_all(value, axes, 0, 0, tiled=True)  67.8 us
    pallas_call x15, Pallas kernels, run(): return built(*operands) if core is None else built(core, *operands)  38.6 us
    all_to_all x4, starting transfers between devices, exchange(): return lax.all_to_all(value, axes, 0, 0, tiled=True)  24.1 us
    pallas_call x6, Pallas kernels, direct(): pl.pallas_call(kernel, out_shape=out_shape, in_specs=[VMEM] * len(operand...  16.5 us
    unnamed x42, local copies, waits for them, and re-layouts  14.1 us
  transfers between devices with their start and end apart: 8, of which 6 were waited for; matrix products, arithmetic and copies ran while one was open for 0% of the time, Pallas kernels for 14%

profile of v3, /device:TPU:0, one launch (start us, length us, event | category | flops | bytes accessed | tf_op | source)
XLA Modules:
  0.0 289.6 jit_solution(3769812063961926121)
XLA Ops:
  0.0 2.3 shard_map.28
  2.3 58.9 %all_to_all.40.after_ref.w_ref = f32[16,4,32,512]{3,2,1,0:T(8,128)S(1)} all-to-all(f32[16,4,32,512]{3,2,1,0:T(8,128)S(1)} %shard_map.28), channel_id=1, replica_groups=mesh['y'=4,'xl'=2,'core'=2,'z'=4,'xh'=2] {'core','z','xh'}, dimensions={0} | all-to-all | bytes 8388608 | tf_op jit(solution)/shard_map/all_to_all | solution.py:390
  61.3 4.3 %shard_map.30 = (f32[6656,128]{1,0:T(8,128)S(1)}, f32[16,4,32,512]{3,2,1,0:T(8,128)}) custom-call(f32[16,4,32,512]{3,2,1,0:T(8,128)S(1)} %all_to_all.40.after_ref.w_ref, f32[64,32,128]{2,1,0:T(8,128)S(1)} %shard_map.29.e_ref), custom_call_target="tpu_custom_call" | custom-call | flops 4000000000 | bytes 6291456 | tf_op jit(solution)/shard_map/pallas_call | solution.py:374
  65.6 1.7 copy-done.1
  67.3 7.0 %all-to-all-start.1 = ((f32[64,104,128]{2,1,0:T(8,128)}), f32[64,104,128]{2,1,0:T(8,128)S(1)}, u32[]{:S(2)}, u32[]{:S(2)}) async-start(f32[64,104,128]{2,1,0:T(8,128)} %bitcast.12), calls=%async_computation.1 | async-start | bytes 6815744 | tf_op jit(solution)/shard_map/all_to_all | solution.py:390
  74.4 42.8 %all-to-all-done.1.buf_ref = f32[64,104,128]{2,1,0:T(8,128)S(1)} async-done(((f32[64,104,128]{2,1,0:T(8,128)}), f32[64,104,128]{2,1,0:T(8,128)S(1)}, u32[]{:S(2)}, u32[]{:S(2)}) %all-to-all-start.1) | async-done | bytes 3407904 | tf_op jit(solution)/shard_map/all_to_all | solution.py:390
  117.3 2.2 shard_map.31
  120.4 6.0 %all-to-all-start.2 = ((f32[64,72,128]{2,1,0:T(8,128)}), f32[64,72,128]{2,1,0:T(8,128)S(1)}, u32[]{:S(2)}, u32[]{:S(2)}) async-start(f32[64,72,128]{2,1,0:T(8,128)} %get-tuple-element.29), calls=%async_computation.2 | async-start | bytes 4718592 | tf_op jit(solution)/shard_map/all_to_all | solution.py:390
  126.5 21.3 %shard_map.32 = (bf16[4,256,1024]{2,1,0:T(8,128)(2,1)}, bf16[4,256,1024]{2,1,0:T(8,128)(2,1)}, bf16[4,256,1024]{2,1,0:T(8,128)(2,1)}, bf16[4,256,1024]{2,1,0:T(8...) custom-call(s32[1]{0:T(128)} %bitcast.core_ref, ...), custom_call_target="tpu_custom_call" | custom-call | flops 10000000000 | bytes 25165824 | tf_op jit(solution)/shard_map/pallas_call | solution.py:370
  147.8 11.1 %all-to-all-done.2.in_ref = f32[64,72,128]{2,1,0:T(8,128)S(1)} async-done(((f32[64,72,128]{2,1,0:T(8,128)}), f32[64,72,128]{2,1,0:T(8,128)S(1)}, u32[]{:S(2)}, u32[]{:S(2)}) %all-to-all-start.2) | async-done | bytes 2359328 | tf_op jit(solution)/shard_map/all_to_all | solution.py:390
  158.8 5.6 %all-to-all-start.3 = ((f32[64,32,128]{2,1,0:T(8,128)}), f32[64,32,128]{2,1,0:T(8,128)S(1)}, u32[]{:S(2)}, u32[]{:S(2)}) async-start(f32[64,32,128]{2,1,0:T(8,128)} %bitcast.15), calls=%async_computation.3 | async-start | bytes 2097152 | tf_op jit(solution)/shard_map/all_to_all | solution.py:390
  164.5 7.9 %shard_map.34 = (f32[10,256,256]{2,1,0:T(8,128)}, bf16[10,256,256]{2,1,0:T(8,128)(2,1)S(1)}, bf16[10,256,256]{2,1,0:T(8,128)(2,1)S(1)}) custom-call(f32[4608,128]{1,0:T(8,128)S(1)} %bitcast.9), custom_call_target="tpu_custom_call" | custom-call | tf_op jit(solution)/shard_map/pallas_call | solution.py:370
  174.5 7.8 %all-to-all-done.3.in_ref = f32[64,32,128]{2,1,0:T(8,128)S(1)} async-done(((f32[64,32,128]{2,1,0:T(8,128)}), f32[64,32,128]{2,1,0:T(8,128)S(1)}, u32[]{:S(2)}, u32[]{:S(2)}) %all-to-all-start.3) | async-done | bytes 1048608 | tf_op jit(solution)/shard_map/all_to_all | solution.py:390
  184.1 1.8 shard_map.38
  187.2 24.0 %all_to_all.41.after_ref = f32[64,32,128]{2,1,0:T(8,128)S(1)} all-to-all(f32[64,32,128]{2,1,0:T(8,128)S(1)} %shard_map.39), channel_id=1, replica_groups=mesh['y'=4,'xl'=2,'core'=2,'z'=4,'xh'=2] {'y','xl','z','xh'}, dimensions={0} | all-to-all | bytes 2097152 | tf_op jit(solution)/shard_map/all_to_all | solution.py:390
  213.7 3.9 %shard_map.43 = f32[2048,128]{1,0:T(8,128)} custom-call(f32[2048,128]{1,0:T(8,128)S(1)} %bitcast.10, bf16[1024,1024]{1,0:T(8,128)(2,1)S(1)} %copy-done.17, bf16[1024,1024]{1,0:T(8,128)(2,1)S(1)} %copy-done.18, f32[256,1024]{1,0:T(8,128)S(1)} %copy-done.20), custom_call_target="tpu_custom_call" | custom-call | flops 2000000000 | bytes 7340032 | tf_op jit(solution)/shard_map/pallas_call | solution.py:374
  217.5 5.4 %all-to-all-start.5 = ((f32[64,32,128]{2,1,0:T(8,128)}), f32[64,32,128]{2,1,0:T(8,128)S(1)}, u32[]{:S(2)}, u32[]{:S(2)}) async-start(f32[64,32,128]{2,1,0:T(8,128)} %bitcast.6), calls=%async_computation.5 | async-start | bytes 2097152 | tf_op jit(solution)/shard_map/all_to_all | solution.py:390
  226.2 2.3 shard_map.40.after_ref.x_ref
  229.5 3.5 %shard_map.42 = (bf16[10,256,256]{2,1,0:T(8,128)(2,1)S(1)}, bf16[10,256,256]{2,1,0:T(8,128)(2,1)S(1)}) custom-call(s32[1]{0:T(128)} %bitcast.core_ref, f32[10,256,256]{2,1,0:T(8,128)S(1)} %copy-done, f32[10,256,256]{2,1,0:T(8,128)} %collective-permute-done.3.sib_ref), custom_call_target="tpu_custom_call" | custom-call | bytes 8388608 | tf_op jit(solution)/shard_map/pallas_call | solution.py:370
  234.0 6.1 %all-to-all-done.5.in_ref = f32[64,32,128]{2,1,0:T(8,128)S(1)} async-done(((f32[64,32,128]{2,1,0:T(8,128)}), f32[64,32,128]{2,1,0:T(8,128)S(1)}, u32[]{:S(2)}, u32[]{:S(2)}) %all-to-all-start.5) | async-done | bytes 1048608 | tf_op jit(solution)/shard_map/all_to_all | solution.py:390
  241.5 2.0 shard_map.46
  243.5 21.8 %all_to_all.42 = f32[64,32,128]{2,1,0:T(8,128)S(1)} all-to-all(f32[64,32,128]{2,1,0:T(8,128)S(1)} %shard_map.46), channel_id=1, replica_groups=mesh['y'=4,'xl'=2,'core'=2,'z'=4,'xh'=2] {'y','xl','z','xh'}, dimensions={0} | all-to-all | bytes 2097152 | tf_op jit(solution)/shard_map/all_to_all | solution.py:390
  265.3 2.3 shard_map.47
  267.6 20.9 %all_to_all.43.in_ref = f32[16,32,512]{2,1,0:T(8,128)S(1)} all-to-all(f32[16,32,512]{2,1,0:T(8,128)S(1)} %shard_map.47), channel_id=1, replica_groups=mesh['y'=4,'xl'=2,'core'=2,'z'=4,'xh'=2] {'core','z','xh'}, dimensions={0} | all-to-all | bytes 2097152 | tf_op jit(solution)/shard_map/all_to_all | solution.py:390
  (59 shorter events, 16.5 us)
Async XLA Ops:
  2.3 59.0 %copy-start.10 = (f32[4,65536]{1,0:T(4,128)S(1)}, f32[4,65536]{1,0:T(4,128)}, u32[]{:S(2)}) copy-start(f32[4,65536]{1,0:T(4,128)} %e_ref.1) | copy-start | bytes 3145732
  65.6 1.7 copy-start.1
  67.3 49.9 %all-to-all-start.1 = ((f32[64,104,128]{2,1,0:T(8,128)}), f32[64,104,128]{2,1,0:T(8,128)S(1)}, u32[]{:S(2)}, u32[]{:S(2)}) async-start(f32[64,104,128]{2,1,0:T(8,128)} %bitcast.12), calls=%async_computation.1 | async-start | bytes 6815744 | tf_op jit(solution)/shard_map/all_to_all | solution.py:390
  74.3 52.1 %collective-permute-start = (f32[16,4,32,512]{3,2,1,0:T(8,128)}, f32[16,4,32,512]{3,2,1,0:T(8,128)}, u32[]{:S(2)}, u32[]{:S(2)}) collective-permute-start(f32[16,4,32,512]{3,2,1,0:T(8,128)} %get-tuple-element.25.mine_ref), channel_id=1, source_target_pairs={{0,8},{8,0},{1,9},{9,1},{2,10},{10,2},{3,11},{11,3},{4,12},{12,4},... | collective-permute-start | bytes 12582920 | tf_op jit(solution)/shard_map/ppermute | solution.py:431
  120.4 6.1 %copy-start.12 = (f32[64,32,128]{2,1,0:T(8,128)S(1)}, f32[64,32,128]{2,1,0:T(8,128)}, u32[]{:S(2)}) copy-start(f32[64,32,128]{2,1,0:T(8,128)} %copy-done.11) | copy-start | bytes 3145732
  120.4 38.4 %all-to-all-start.2 = ((f32[64,72,128]{2,1,0:T(8,128)}), f32[64,72,128]{2,1,0:T(8,128)S(1)}, u32[]{:S(2)}, u32[]{:S(2)}) async-start(f32[64,72,128]{2,1,0:T(8,128)} %get-tuple-element.29), calls=%async_computation.2 | async-start | bytes 4718592 | tf_op jit(solution)/shard_map/all_to_all | solution.py:390
  158.8 23.5 %all-to-all-start.3 = ((f32[64,32,128]{2,1,0:T(8,128)}), f32[64,32,128]{2,1,0:T(8,128)S(1)}, u32[]{:S(2)}, u32[]{:S(2)}) async-start(f32[64,32,128]{2,1,0:T(8,128)} %bitcast.15), calls=%async_computation.3 | async-start | bytes 2097152 | tf_op jit(solution)/shard_map/all_to_all | solution.py:390
  182.4 1.4 copy-start.5
  182.4 1.7 copy-start.7
  182.5 1.3 collective-permute-start.1
  185.9 1.2 collective-permute-start.2
  211.2 1.6 copy-start.17
  211.2 2.2 copy-start.18
  211.2 2.5 copy-start.20
  211.2 18.3 %collective-permute-start.3 = (f32[10,256,256]{2,1,0:T(8,128)}, f32[10,256,256]{2,1,0:T(8,128)}, u32[]{:S(2)}, u32[]{:S(2)}) collective-permute-start(f32[10,256,256]{2,1,0:T(8,128)} %shard_map.41.own_ref), channel_id=1, source_target_pairs={{0,8},{8,0},{1,9},{9,1},{2,10},{10,2},{3,11},{11,3},{4,12},{12,4},... | collective-permute-start | bytes 7864328 | tf_op jit(solution)/shard_map/ppermute | solution.py:506
  213.7 9.3 %copy-start.19 = (f32[256,1024]{1,0:T(8,128)S(1)}, f32[256,1024]{1,0:T(8,128)}, u32[]{:S(2)}) copy-start(f32[256,1024]{1,0:T(8,128)} %get-tuple-element.37.x_ref) | copy-start | bytes 3145732
  217.5 22.6 %all-to-all-start.5 = ((f32[64,32,128]{2,1,0:T(8,128)}), f32[64,32,128]{2,1,0:T(8,128)S(1)}, u32[]{:S(2)}, u32[]{:S(2)}) async-start(f32[64,32,128]{2,1,0:T(8,128)} %bitcast.6), calls=%async_computation.5 | async-start | bytes 2097152 | tf_op jit(solution)/shard_map/all_to_all | solution.py:390
  223.0 1.6 copy-start.15
  224.6 1.6 copy-start.16
  226.2 3.3 %copy-start = (f32[10,256,256]{2,1,0:T(8,128)S(1)}, f32[10,256,256]{2,1,0:T(8,128)}, u32[]{:S(2)}) copy-start(f32[10,256,256]{2,1,0:T(8,128)} %shard_map.41.own_ref) | copy-start | bytes 7864324
  234.0 6.1 %copy-start.9 = (f32[256,1024]{1,0:T(8,128)S(1)}, f32[256,1024]{1,0:T(8,128)}, u32[]{:S(2)}) copy-start(f32[256,1024]{1,0:T(8,128)} %copy-done.8) | copy-start | bytes 3145732
  240.2 1.3 copy-start.3
  241.5 23.8 %copy-start.13 = (bf16[4,256,1024]{2,1,0:T(8,128)(2,1)S(1)}, bf16[4,256,1024]{2,1,0:T(8,128)(2,1)}, u32[]{:S(2)}) copy-start(bf16[4,256,1024]{2,1,0:T(8,128)(2,1)} %get-tuple-element.43.high_ref) | copy-start | bytes 6291460
  241.5 23.8 %copy-start.14 = (bf16[4,256,1024]{2,1,0:T(8,128)(2,1)S(1)}, bf16[4,256,1024]{2,1,0:T(8,128)(2,1)}, u32[]{:S(2)}) copy-start(bf16[4,256,1024]{2,1,0:T(8,128)(2,1)} %get-tuple-element.44.low_ref) | copy-start | bytes 6291460
  (5 other events, 5.2 us)

commit v4 on v3

--- a/solution.py
+++ b/solution.py
@@ -16,7 +16,7 @@
 NCOL = 8
 NB = 256
 GROUP = 4
-PAIRS = [(i, j) for i in range(GROUP) for j in range(i, GROUP)]
+PAIRS = [(i, j) for j in range(GROUP) for i in range(j + 1)]
 
 
 def place_pieces():
@@ -97,11 +97,20 @@
     return jnp.concatenate([value[:NCOL].reshape(NB, 512), value[NCOL:].reshape(NB, 512)], axis=1)
 
 
-def inner_products(w_ref, e_ref, buf_ref, kept_ref, high_ref, low_ref, done):
-    keep = pltpu.make_async_copy(w_ref, kept_ref, done)
+def inner_products(w_ref, e_ref, out_ref, kept_ref, high_ref, low_ref, buf_ref, done):
+    keep = pltpu.make_async_copy(w_ref, kept_ref, done.at[0])
     keep.start()
+    for q in range(NCHIP):
+        buf_ref[q * STEP + GROWS : q * STEP + STEP, :] = e_ref[q]
+    first = PIECES[0, GROUP - 1, 0][0] // GROWS * STEP
+    parts = (slice(0, first), slice(first, NCHIP * STEP))
+    sends = [
+        pltpu.make_async_copy(buf_ref.at[part], out_ref.at[part], done.at[1 + at]) for at, part in enumerate(parts)
+    ]
     for j in range(GROUP):
         high_ref[j], low_ref[j] = split(whole_block(w_ref[:, j]))
+        if j == GROUP - 1:
+            sends[0].start()
         for i in range(j + 1):
             value = dot3((high_ref[i], low_ref[i]), (high_ref[j], low_ref[j]), NT)
             for half in range(2):
@@ -113,9 +122,9 @@
                     start = chip * STEP + offset
                     buf_ref[start : start + take, :] = value[done : done + take, half * 128 : half * 128 + 128]
                     done += take
-    for q in range(NCHIP):
-        buf_ref[q * STEP + GROWS : q * STEP + STEP, :] = e_ref[q]
-    keep.wait()
+    sends[1].start()
+    for copy in (keep, *sends):
+        copy.wait()
 
 
 def gather_rows(ref, step, first, high_ref, low_ref, value_ref=None, columns=8):
@@ -186,16 +195,6 @@
     out_ref[...] = sum_chips(buf_ref, PROWS)
 
 
-def spread_to_chips(part_ref, out_ref, done, beside=None):
-    copies = [pltpu.make_async_copy(part_ref, out_ref.at[q], done.at[q]) for q in range(NCHIP)]
-    for copy in copies:
-        copy.start()
-    if beside is not None:
-        beside()
-    for copy in copies:
-        copy.wait()
-
-
 def spread_rows(part, out_ref):
     def spread(q, carry):
         out_ref[q] = part
@@ -205,15 +204,17 @@
 
 
 def sum_products(buf_ref, out_ref, e_ref, part_ref, done):
+    copies = [pltpu.make_async_copy(buf_ref.at[:, GROWS:, :], e_ref, done.at[NCHIP])]
+    copies[0].start()
     part_ref[...] = sum_chips(buf_ref, GROWS)
-
-    def keep_eigenvectors():
-        e_ref[...] = buf_ref[:, GROWS:, :]
-
-    spread_to_chips(part_ref, out_ref, done, keep_eigenvectors)
-
-
-def spread_found(core_ref, own_ref, sib_ref, out_ref):
+    for q in range(NCHIP):
+        copies.append(pltpu.make_async_copy(part_ref, out_ref.at[q], done.at[q]))
+        copies[-1].start()
+    for copy in copies:
+        copy.wait()
+
+
+def spread_found(core_ref, own_ref, sib_ref, high_ref, low_ref, first_ref, out_ref):
     spread_rows(jnp.where(core_ref[0] == 0, own_ref[...], sib_ref[...]), out_ref)
 
 
@@ -386,6 +387,10 @@
     return pltpu.with_memory_space_constraint(value, pltpu.HBM)
 
 
+def in_vmem(value):
+    return pltpu.with_memory_space_constraint(value, pltpu.VMEM)
+
+
 def exchange(value, axes):
     return lax.all_to_all(value, axes, 0, 0, tiled=True)
 
@@ -421,10 +426,11 @@
     )
     buf, kept = direct(
         inner_products,
-        (f32(NCHIP * STEP, 128), hbm(F32, 2 * NCOL, GROUP, 32, 512)),
+        (hbm(F32, NCHIP * STEP, 128), hbm(F32, 2 * NCOL, GROUP, 32, 512)),
         (mine, pieces),
-        scratch=[pltpu.VMEM((GROUP, NB, 1024), BF16)] * 2 + [pltpu.SemaphoreType.DMA(())],
-        out_specs=(VMEM, HBM),
+        scratch=[pltpu.VMEM((GROUP, NB, 1024), BF16)] * 2
+        + [pltpu.VMEM((NCHIP * STEP, 128), F32), pltpu.SemaphoreType.DMA((3,))],
+        out_specs=(HBM, HBM),
         flops=4 * 10**9,
         size=6 * mega,
     )
@@ -433,11 +439,11 @@
 
     part, spread = run(
         sum_products,
-        (hbm(F32, NCHIP, GROWS, 128), f32(NCHIP, EROWS, 128)),
-        (HBM, whole(NCHIP, EROWS, 128)),
+        (hbm(F32, NCHIP, GROWS, 128), hbm(F32, NCHIP, EROWS, 128)),
+        (HBM, HBM),
         [whole(NCHIP, STEP, 128)],
         (arrived,),
-        scratch=[pltpu.VMEM((GROWS, 128), F32), pltpu.SemaphoreType.DMA((NCHIP,))],
+        scratch=[pltpu.VMEM((GROWS, 128), F32), pltpu.SemaphoreType.DMA((NCHIP + 1,))],
         size=5 * mega,
     )
 
@@ -489,8 +495,8 @@
         spread_found,
         f32(NCHIP, PROWS, 128),
         whole(NCHIP, PROWS, 128),
-        [whole(PROWS, 128), whole(PROWS, 128)],
-        (found, lax.ppermute(found_sib, "core", SWAP)),
+        [whole(PROWS, 128), whole(PROWS, 128), ANY, ANY, ANY],
+        (found, lax.ppermute(found_sib, "core", SWAP), in_vmem(cross_high), in_vmem(cross_low), in_vmem(first)),
         core=core,
         size=mega,
     )
@@ -524,7 +530,7 @@
         flops=2 * 10**9,
         size=7 * mega,
     )
-    arrived = after(middle, after(first_high, exchange(buf.reshape(NCHIP, PROWS, 128), CHIPS), ()), ())
+    arrived = after(middle, after(in_vmem(first_high), exchange(buf.reshape(NCHIP, PROWS, 128), CHIPS), ()), ())
     found = direct(
         solve_own,
         f32(NCHIP, PROWS, 128),

time: 291 us -> 290 us (level)
  local copies, waits for them, and re-layouts: 14.1 us -> 9.35 us
    unnamed x42 -> x34, local copies, waits for them, and re-layouts: 14.1 us -> 9.35 us
where the time goes in v4:
time: 290 us; the launch traced here: 289 us
  blocking collectives  127 us (44%)
  waiting for transfers between devices  71.9 us (25%)
  Pallas kernels  56.3 us (19%)
  starting transfers between devices  24.3 us (8%)
  local copies, waits for them, and re-layouts  9.35 us (3%)
    all_to_all x4, blocking collectives, exchange(): return lax.all_to_all(value, axes, 0, 0, tiled=True)  127 us
    all_to_all x4, waiting for transfers between devices, exchange(): return lax.all_to_all(value, axes, 0, 0, tiled=True)  69.5 us
    pallas_call x15, Pallas kernels, run(): return built(*operands) if core is None else built(core, *operands)  38.7 us
    all_to_all x4, starting transfers between devices, exchange(): return lax.all_to_all(value, axes, 0, 0, tiled=True)  24.2 us
    pallas_call x6, Pallas kernels, direct(): pl.pallas_call(kernel, out_shape=out_shape, in_specs=[VMEM] * len(operand...  17.6 us
    unnamed x34, local copies, waits for them, and re-layouts  9.35 us
  transfers between devices with their start and end apart: 8, of which 6 were waited for; matrix products, arithmetic and copies ran while one was open for 0% of the time, Pallas kernels for 14%

profile of v4, /device:TPU:0, one launch (start us, length us, event | category | flops | bytes accessed | tf_op | source)
XLA Modules:
  0.0 288.7 jit_solution(11418410235757619490)
XLA Ops:
  0.0 2.3 shard_map.28
  2.3 58.9 %all_to_all.40.after_ref.w_ref = f32[16,4,32,512]{3,2,1,0:T(8,128)S(1)} all-to-all(f32[16,4,32,512]{3,2,1,0:T(8,128)S(1)} %shard_map.28), channel_id=1, replica_groups=mesh['y'=4,'xl'=2,'core'=2,'z'=4,'xh'=2] {'core','z','xh'}, dimensions={0} | all-to-all | bytes 8388608 | tf_op jit(solution)/shard_map/all_to_all | solution.py:395
  61.3 5.4 %shard_map.30 = (f32[6656,128]{1,0:T(8,128)}, f32[16,4,32,512]{3,2,1,0:T(8,128)}) custom-call(f32[16,4,32,512]{3,2,1,0:T(8,128)S(1)} %all_to_all.40.after_ref.w_ref, f32[64,32,128]{2,1,0:T(8,128)S(1)} %shard_map.29.e_ref), custom_call_target="tpu_custom_call" | custom-call | flops 4000000000 | bytes 6291456 | tf_op jit(solution)/shard_map/pallas_call | solution.py:375
  66.7 7.0 %all-to-all-start.1 = ((f32[64,104,128]{2,1,0:T(8,128)}), f32[64,104,128]{2,1,0:T(8,128)S(1)}, u32[]{:S(2)}, u32[]{:S(2)}) async-start(f32[64,104,128]{2,1,0:T(8,128)} %bitcast.15), calls=%async_computation.1 | async-start | bytes 6815744 | tf_op jit(solution)/shard_map/all_to_all | solution.py:395
  73.9 42.8 %all-to-all-done.1.buf_ref = f32[64,104,128]{2,1,0:T(8,128)S(1)} async-done(((f32[64,104,128]{2,1,0:T(8,128)}), f32[64,104,128]{2,1,0:T(8,128)S(1)}, u32[]{:S(2)}, u32[]{:S(2)}) %all-to-all-start.1) | async-done | bytes 3407904 | tf_op jit(solution)/shard_map/all_to_all | solution.py:395
  116.7 2.3 shard_map.31
  119.0 6.0 %all-to-all-start.2 = ((f32[64,72,128]{2,1,0:T(8,128)}), f32[64,72,128]{2,1,0:T(8,128)S(1)}, u32[]{:S(2)}, u32[]{:S(2)}) async-start(f32[64,72,128]{2,1,0:T(8,128)} %get-tuple-element.29), calls=%async_computation.2 | async-start | bytes 4718592 | tf_op jit(solution)/shard_map/all_to_all | solution.py:395
  125.1 21.3 %shard_map.32 = (bf16[4,256,1024]{2,1,0:T(8,128)(2,1)}, bf16[4,256,1024]{2,1,0:T(8,128)(2,1)}, bf16[4,256,1024]{2,1,0:T(8,128)(2,1)}, bf16[4,256,1024]{2,1,0:T(8...) custom-call(s32[1]{0:T(128)} %bitcast.core_ref, ...), custom_call_target="tpu_custom_call" | custom-call | flops 10000000000 | bytes 25165824 | tf_op jit(solution)/shard_map/pallas_call | solution.py:371
  146.4 11.1 %all-to-all-done.2.in_ref = f32[64,72,128]{2,1,0:T(8,128)S(1)} async-done(((f32[64,72,128]{2,1,0:T(8,128)}), f32[64,72,128]{2,1,0:T(8,128)S(1)}, u32[]{:S(2)}, u32[]{:S(2)}) %all-to-all-start.2) | async-done | bytes 2359328 | tf_op jit(solution)/shard_map/all_to_all | solution.py:395
  157.5 5.6 %all-to-all-start.3 = ((f32[64,32,128]{2,1,0:T(8,128)}), f32[64,32,128]{2,1,0:T(8,128)S(1)}, u32[]{:S(2)}, u32[]{:S(2)}) async-start(f32[64,32,128]{2,1,0:T(8,128)} %bitcast.14), calls=%async_computation.3 | async-start | bytes 2097152 | tf_op jit(solution)/shard_map/all_to_all | solution.py:395
  163.1 7.9 %shard_map.34 = (f32[10,256,256]{2,1,0:T(8,128)}, bf16[10,256,256]{2,1,0:T(8,128)(2,1)S(1)}, bf16[10,256,256]{2,1,0:T(8,128)(2,1)S(1)}) custom-call(f32[4608,128]{1,0:T(8,128)S(1)} %bitcast.9), custom_call_target="tpu_custom_call" | custom-call | tf_op jit(solution)/shard_map/pallas_call | solution.py:371
  173.2 7.8 %all-to-all-done.3.in_ref = f32[64,32,128]{2,1,0:T(8,128)S(1)} async-done(((f32[64,32,128]{2,1,0:T(8,128)}), f32[64,32,128]{2,1,0:T(8,128)S(1)}, u32[]{:S(2)}, u32[]{:S(2)}) %all-to-all-start.3) | async-done | bytes 1048608 | tf_op jit(solution)/shard_map/all_to_all | solution.py:395
  182.7 1.8 shard_map.38
  185.8 24.0 %all_to_all.41.after_ref = f32[64,32,128]{2,1,0:T(8,128)S(1)} all-to-all(f32[64,32,128]{2,1,0:T(8,128)S(1)} %shard_map.39), channel_id=1, replica_groups=mesh['y'=4,'xl'=2,'core'=2,'z'=4,'xh'=2] {'y','xl','z','xh'}, dimensions={0} | all-to-all | bytes 2097152 | tf_op jit(solution)/shard_map/all_to_all | solution.py:395
  209.8 3.9 %shard_map.43 = f32[2048,128]{1,0:T(8,128)} custom-call(f32[2048,128]{1,0:T(8,128)S(1)} %bitcast.10, bf16[1024,1024]{1,0:T(8,128)(2,1)S(1)} %copy-done.1, bf16[1024,1024]{1,0:T(8,128)(2,1)S(1)} %copy-done.2, f32[256,1024]{1,0:T(8,128)S(1)} %copy-done.9), custom_call_target="tpu_custom_call" | custom-call | flops 2000000000 | bytes 7340032 | tf_op jit(solution)/shard_map/pallas_call | solution.py:375
  213.7 5.4 %all-to-all-start.5 = ((f32[64,32,128]{2,1,0:T(8,128)}), f32[64,32,128]{2,1,0:T(8,128)S(1)}, u32[]{:S(2)}, u32[]{:S(2)}) async-start(f32[64,32,128]{2,1,0:T(8,128)} %bitcast.6), calls=%async_computation.5 | async-start | bytes 2097152 | tf_op jit(solution)/shard_map/all_to_all | solution.py:395
  220.7 1.6 copy-done.15
  223.6 2.3 shard_map.40.after_ref.x_ref
  225.9 3.5 %shard_map.42 = (bf16[10,256,256]{2,1,0:T(8,128)(2,1)S(1)}, bf16[10,256,256]{2,1,0:T(8,128)(2,1)S(1)}) custom-call(s32[1]{0:T(128)} %bitcast.core_ref, f32[10,256,256]{2,1,0:T(8,128)S(1)} %copy-done, f32[10,256,256]{2,1,0:T(8,128)} %collective-permute-done.3.sib_ref), custom_call_target="tpu_custom_call" | custom-call | bytes 8388608 | tf_op jit(solution)/shard_map/pallas_call | solution.py:371
  230.5 7.8 %all-to-all-done.5.in_ref = f32[64,32,128]{2,1,0:T(8,128)S(1)} async-done(((f32[64,32,128]{2,1,0:T(8,128)}), f32[64,32,128]{2,1,0:T(8,128)S(1)}, u32[]{:S(2)}, u32[]{:S(2)}) %all-to-all-start.5) | async-done | bytes 1048608 | tf_op jit(solution)/shard_map/all_to_all | solution.py:395
  239.6 2.0 shard_map.46
  241.6 22.8 %all_to_all.42 = f32[64,32,128]{2,1,0:T(8,128)S(1)} all-to-all(f32[64,32,128]{2,1,0:T(8,128)S(1)} %shard_map.46), channel_id=1, replica_groups=mesh['y'=4,'xl'=2,'core'=2,'z'=4,'xh'=2] {'y','xl','z','xh'}, dimensions={0} | all-to-all | bytes 2097152 | tf_op jit(solution)/shard_map/all_to_all | solution.py:395
  264.4 2.3 shard_map.47
  266.7 20.9 %all_to_all.43.in_ref = f32[16,32,512]{2,1,0:T(8,128)S(1)} all-to-all(f32[16,32,512]{2,1,0:T(8,128)S(1)} %shard_map.47), channel_id=1, replica_groups=mesh['y'=4,'xl'=2,'core'=2,'z'=4,'xh'=2] {'core','z','xh'}, dimensions={0} | all-to-all | bytes 2097152 | tf_op jit(solution)/shard_map/all_to_all | solution.py:395
  (51 shorter events, 11.8 us)
Async XLA Ops:
  2.3 59.0 %copy-start.10 = (f32[4,65536]{1,0:T(4,128)S(1)}, f32[4,65536]{1,0:T(4,128)}, u32[]{:S(2)}) copy-start(f32[4,65536]{1,0:T(4,128)} %e_ref.1) | copy-start | bytes 3145732
  66.7 50.0 %all-to-all-start.1 = ((f32[64,104,128]{2,1,0:T(8,128)}), f32[64,104,128]{2,1,0:T(8,128)S(1)}, u32[]{:S(2)}, u32[]{:S(2)}) async-start(f32[64,104,128]{2,1,0:T(8,128)} %bitcast.15), calls=%async_computation.1 | async-start | bytes 6815744 | tf_op jit(solution)/shard_map/all_to_all | solution.py:395
  73.8 51.3 %collective-permute-start = (f32[16,4,32,512]{3,2,1,0:T(8,128)}, f32[16,4,32,512]{3,2,1,0:T(8,128)}, u32[]{:S(2)}, u32[]{:S(2)}) collective-permute-start(f32[16,4,32,512]{3,2,1,0:T(8,128)} %get-tuple-element.25.mine_ref), channel_id=1, source_target_pairs={{0,8},{8,0},{1,9},{9,1},{2,10},{10,2},{3,11},{11,3},{4,12},{12,4},... | collective-permute-start | bytes 12582920 | tf_op jit(solution)/shard_map/ppermute | solution.py:437
  119.0 6.1 %copy-start.11 = (f32[64,32,128]{2,1,0:T(8,128)S(1)}, f32[64,32,128]{2,1,0:T(8,128)}, u32[]{:S(2)}) copy-start(f32[64,32,128]{2,1,0:T(8,128)} %get-tuple-element.27) | copy-start | bytes 3145732
  119.0 38.4 %all-to-all-start.2 = ((f32[64,72,128]{2,1,0:T(8,128)}), f32[64,72,128]{2,1,0:T(8,128)S(1)}, u32[]{:S(2)}, u32[]{:S(2)}) async-start(f32[64,72,128]{2,1,0:T(8,128)} %get-tuple-element.29), calls=%async_computation.2 | async-start | bytes 4718592 | tf_op jit(solution)/shard_map/all_to_all | solution.py:395
  157.5 23.5 %all-to-all-start.3 = ((f32[64,32,128]{2,1,0:T(8,128)}), f32[64,32,128]{2,1,0:T(8,128)S(1)}, u32[]{:S(2)}, u32[]{:S(2)}) async-start(f32[64,32,128]{2,1,0:T(8,128)} %bitcast.14), calls=%async_computation.3 | async-start | bytes 2097152 | tf_op jit(solution)/shard_map/all_to_all | solution.py:395
  171.0 1.1 copy-start.5
  172.1 1.1 copy-start.7
  181.0 1.4 copy-start.6
  181.0 1.7 copy-start.8
  181.0 4.7 %copy-start.2 = (bf16[1024,1024]{1,0:T(8,128)(2,1)S(1)}, bf16[1024,1024]{1,0:T(8,128)(2,1)}, u32[]{:S(2)}) copy-start(bf16[1024,1024]{1,0:T(8,128)(2,1)} %get-tuple-element.36.low_ref.gl_ref) | copy-start | bytes 6291460
  181.0 4.7 %copy-start.1 = (bf16[1024,1024]{1,0:T(8,128)(2,1)S(1)}, bf16[1024,1024]{1,0:T(8,128)(2,1)}, u32[]{:S(2)}) copy-start(bf16[1024,1024]{1,0:T(8,128)(2,1)} %get-tuple-element.35.high_ref.gh_ref) | copy-start | bytes 6291460
  181.0 4.7 %copy-start.9 = (f32[256,1024]{1,0:T(8,128)S(1)}, f32[256,1024]{1,0:T(8,128)}, u32[]{:S(2)}) copy-start(f32[256,1024]{1,0:T(8,128)} %get-tuple-element.37.first_ref) | copy-start | bytes 3145732
  181.1 1.3 collective-permute-start.1
  184.5 1.2 collective-permute-start.2
  209.8 16.0 %collective-permute-start.3 = (f32[10,256,256]{2,1,0:T(8,128)}, f32[10,256,256]{2,1,0:T(8,128)}, u32[]{:S(2)}, u32[]{:S(2)}) collective-permute-start(f32[10,256,256]{2,1,0:T(8,128)} %shard_map.41.own_ref), channel_id=1, source_target_pairs={{0,8},{8,0},{1,9},{9,1},{2,10},{10,2},{3,11},{11,3},{4,12},{12,4},... | collective-permute-start | bytes 7864328 | tf_op jit(solution)/shard_map/ppermute | solution.py:512
  213.7 24.5 %all-to-all-start.5 = ((f32[64,32,128]{2,1,0:T(8,128)}), f32[64,32,128]{2,1,0:T(8,128)S(1)}, u32[]{:S(2)}, u32[]{:S(2)}) async-start(f32[64,32,128]{2,1,0:T(8,128)} %bitcast.6), calls=%async_computation.5 | async-start | bytes 2097152 | tf_op jit(solution)/shard_map/all_to_all | solution.py:395
  219.2 1.6 copy-start.14
  220.7 1.6 copy-start.15
  222.3 1.2 copy-start.16
  223.6 2.3 copy-start
  238.2 1.3 copy-start.4
  239.6 24.9 %copy-start.12 = (bf16[4,256,1024]{2,1,0:T(8,128)(2,1)S(1)}, bf16[4,256,1024]{2,1,0:T(8,128)(2,1)}, u32[]{:S(2)}) copy-start(bf16[4,256,1024]{2,1,0:T(8,128)(2,1)} %get-tuple-element.43.high_ref) | copy-start | bytes 6291460
  239.6 24.9 %copy-start.13 = (bf16[4,256,1024]{2,1,0:T(8,128)(2,1)S(1)}, bf16[4,256,1024]{2,1,0:T(8,128)(2,1)}, u32[]{:S(2)}) copy-start(bf16[4,256,1024]{2,1,0:T(8,128)(2,1)} %get-tuple-element.44.low_ref) | copy-start | bytes 6291460
  (1 other events, 1.1 us)

commit v5 on v4

--- a/solution.py
+++ b/solution.py
@@ -1,3 +1,5 @@
+import functools
+
 import jax
 import jax.numpy as jnp
 from jax import lax
@@ -17,6 +19,7 @@
 NB = 256
 GROUP = 4
 PAIRS = [(i, j) for j in range(GROUP) for i in range(j + 1)]
+USES = [(i, j) for i in range(GROUP - 1, -1, -1) for j in range(GROUP - 1, i - 1, -1)]
 
 
 def place_pieces():
@@ -191,10 +194,6 @@
     return lax.fori_loop(0, NCHIP, add, jnp.zeros((rows, 128), F32), unroll=8)
 
 
-def sum_projection(buf_ref, out_ref):
-    out_ref[...] = sum_chips(buf_ref, PROWS)
-
-
 def spread_rows(part, out_ref):
     def spread(q, carry):
         out_ref[q] = part
@@ -214,10 +213,6 @@
         copy.wait()
 
 
-def spread_found(core_ref, own_ref, sib_ref, high_ref, low_ref, first_ref, out_ref):
-    spread_rows(jnp.where(core_ref[0] == 0, own_ref[...], sib_ref[...]), out_ref)
-
-
 def block_of(g_ref, i, j):
     halves = []
     for half in range(2):
@@ -229,42 +224,37 @@
     return jnp.concatenate(halves, axis=1)
 
 
-def invert(g_ref, out_ref, high_ref, low_ref):
+def invert(holder, core_ref, own_ref, sib_ref, *refs):
+    high_ref, low_ref, g_ref, held_ref = refs[-4:]
+    g_ref[...] = jnp.where(core_ref[0] == holder, own_ref[...], sib_ref[...])
     row = lax.broadcasted_iota(jnp.int32, (NB, NB), 0)
     col = lax.broadcasted_iota(jnp.int32, (NB, NB), 1)
     apart = row ^ col
-    for index, (i, j) in enumerate(PAIRS):
+    for index, (i, j) in enumerate(USES):
         value = block_of(g_ref, i, j)
-        if i == j:
-            diagonal = jnp.where(row == col, 0.5 * value, 0.0)
-            down = 1.0 / jnp.sum(diagonal, axis=1, keepdims=True)
-            across = 1.0 / jnp.sum(diagonal, axis=0, keepdims=True)
-            beside = jnp.where((apart == 1) & (row < col), value, 0.0)
-            value = jnp.where(row == col, down, 0.0) - down * beside * across
-        out_ref[index] = value
+        if i != j:
+            high_ref[index], low_ref[index] = split(value)
+            continue
+        diagonal = jnp.where(row == col, 0.5 * value, 0.0)
+        down = 1.0 / jnp.sum(diagonal, axis=1, keepdims=True)
+        across = 1.0 / jnp.sum(diagonal, axis=0, keepdims=True)
+        beside = jnp.where((apart == 1) & (row < col), value, 0.0)
+        held_ref[i] = jnp.where(row == col, down, 0.0) - down * beside * across
     size = 2
     while size < NB:
         for i in range(GROUP):
-            index = PAIRS.index((i, i))
             beside = jnp.where((apart >= size) & (apart < 2 * size) & (row < col), block_of(g_ref, i, i), 0.0)
-            value = out_ref[index]
+            value = held_ref[i]
             halves = split(value)
             product = dot3(split(dot3(halves, split(beside), NN)), halves, NN)
-            out_ref[index] = value - product
+            held_ref[i] = value - product
         size *= 2
-    for index in range(len(PAIRS)):
-        high_ref[index], low_ref[index] = split(out_ref[index])
-
-
-def pick_factors(core_ref, own_ref, sib_ref, high_ref, low_ref):
-    high_ref[...], low_ref[...] = split(jnp.where(core_ref[0] == 1, own_ref[...], sib_ref[...]))
-
-
-def solve(rows_of, high_ref, low_ref, keep):
-    def factor(i, j):
-        index = PAIRS.index((i, j))
-        return high_ref[index], low_ref[index]
-
+    for i in range(GROUP):
+        index = USES.index((i, i))
+        high_ref[index], low_ref[index] = split(held_ref[i])
+
+
+def solve(rows_of, factor, keep):
     found = {}
     for b in range(GROUP - 1, -1, -1):
         rest = jnp.concatenate([rows_of(b * 2), rows_of(b * 2 + 1)], axis=1)
@@ -276,18 +266,14 @@
             keep(b * 2 + half, value[:, half * 128 : half * 128 + 128])
 
 
-def solve_both(own_ref, sib_ref, high_ref, low_ref, c_own_ref, c_sib_ref):
-    def rows_of(t):
-        return jnp.concatenate([own_ref[t * 4 : t * 4 + 4, :], sib_ref[t * 4 : t * 4 + 4, :]], axis=0)
-
-    def keep(t, value):
-        c_own_ref[t * 4 : t * 4 + 4, :] = value[0:4]
-        c_sib_ref[t * 4 : t * 4 + 4, :] = value[4:8]
-
-    solve(rows_of, high_ref, low_ref, keep)
-
-
-def solve_own(buf_ref, high_ref, low_ref, out_ref, c_ref):
+def solve_own(buf_ref, high_from, low_from, out_ref, high_ref, low_ref, c_ref, done):
+    parts = (slice(0, 3), slice(3, len(USES)))
+    fetches = []
+    for at, part in enumerate(parts):
+        fetches.append(pltpu.make_async_copy(high_from.at[part], high_ref.at[part], done.at[0, at]))
+        fetches.append(pltpu.make_async_copy(low_from.at[part], low_ref.at[part], done.at[1, at]))
+    for fetch in fetches:
+        fetch.start()
     c_ref[...] = sum_chips(buf_ref, PROWS)
 
     def rows_of(t):
@@ -296,7 +282,14 @@
     def keep(t, value):
         c_ref[t * 4 : t * 4 + 4, :] = value[0:4]
 
-    solve(rows_of, high_ref, low_ref, keep)
+    def factor(i, j):
+        index = USES.index((i, j))
+        if index in (0, 3):
+            for fetch in fetches[0:2] if index == 0 else fetches[2:4]:
+                fetch.wait()
+        return high_ref[index], low_ref[index]
+
+    solve(rows_of, factor, keep)
     spread_rows(c_ref[...], out_ref)
 
 
@@ -371,11 +364,11 @@
     return built(*operands) if core is None else built(core, *operands)
 
 
-def direct(kernel, out_shape, operands, scratch=(), out_specs=None, flops=0, size=0, limit=32):
+def direct(kernel, out_shape, operands, scratch=(), in_specs=None, out_specs=None, flops=0, size=0, limit=32):
     return pl.pallas_call(
         kernel,
         out_shape=out_shape,
-        in_specs=[VMEM] * len(operands),
+        in_specs=[VMEM] * len(operands) if in_specs is None else in_specs,
         out_specs=jax.tree.map(lambda _: VMEM, out_shape) if out_specs is None else out_specs,
         scratch_shapes=list(scratch),
         compiler_params=pltpu.CompilerParams(vmem_limit_bytes=limit * 2**20),
@@ -474,49 +467,42 @@
     gram = after(buf, exchange(part, CHIPS)).reshape(ALLROWS, 128)
 
     count = len(PAIRS)
-    factors, own_high, own_low = run(
-        invert,
-        (hbm(F32, count, NB, NB), bf16(count, NB, NB), bf16(count, NB, NB)),
-        (whole(count, NB, NB),) * 3,
-        [whole(ALLROWS, 128)],
-        (gram,),
-    )
-    arrived = after(factors, exchange(after(gram, buf, (1,)).reshape(NCHIP, PROWS, 128), CHIPS))
-    rows = f32(PROWS, 128)
-    projection = run(sum_projection, rows, whole(PROWS, 128), [whole(NCHIP, PROWS, 128)], (arrived,), size=mega)
-    found, found_sib = direct(
-        solve_both,
-        (rows, rows),
-        (projection, lax.ppermute(projection, "core", SWAP), own_high, own_low),
-        flops=10**8,
-        size=3 * mega,
-    )
-    found = run(
-        spread_found,
-        f32(NCHIP, PROWS, 128),
-        whole(NCHIP, PROWS, 128),
-        [whole(PROWS, 128), whole(PROWS, 128), ANY, ANY, ANY],
-        (found, lax.ppermute(found_sib, "core", SWAP), in_vmem(cross_high), in_vmem(cross_low), in_vmem(first)),
-        core=core,
-        size=mega,
-    )
-    coefficients = exchange(found, CHIPS)
-    factors = after(coefficients, factors, (1,))
-    coefficients = coefficients.reshape(NCHIP * PROWS, 128)
-    square = pl.BlockSpec((2, NB, NB), lambda n, core: (n, 0, 0))
-    first_high, first_low = run(
-        pick_factors,
-        (bf16(count, NB, NB),) * 2,
-        (square,) * 2,
-        [square, square],
-        (factors, lax.ppermute(factors, "core", SWAP)),
-        grid=(count // 2,),
-        core=core,
-        size=8 * mega,
-    )
+    gram_sib = lax.ppermute(gram, "core", SWAP)
+
+    def factors_of(holder, later=()):
+        return run(
+            functools.partial(invert, holder),
+            (hbm(BF16, count, NB, NB),) * 2,
+            (whole(count, NB, NB),) * 2,
+            [whole(ALLROWS, 128)] * 2 + [ANY] * len(later),
+            (gram, gram_sib, *later),
+            scratch=[pltpu.VMEM((ALLROWS, 128), F32), pltpu.VMEM((GROUP, NB, NB), F32)],
+            core=core,
+        )
+
+    def coefficients_of(arrived, high, low):
+        found = direct(
+            solve_own,
+            f32(NCHIP, PROWS, 128),
+            (arrived, in_hbm(high), in_hbm(low)),
+            scratch=[
+                pltpu.VMEM((count, NB, NB), BF16),
+                pltpu.VMEM((count, NB, NB), BF16),
+                pltpu.VMEM((PROWS, 128), F32),
+                pltpu.SemaphoreType.DMA((2, 2)),
+            ],
+            in_specs=[VMEM, HBM, HBM],
+            flops=10**8,
+            size=5 * mega,
+        )
+        return exchange(found, CHIPS).reshape(NCHIP * PROWS, 128)
+
+    high, low = factors_of(0, (in_vmem(cross_high), in_vmem(cross_low), in_vmem(first)))
+    arrived = after(high, exchange(after(gram, buf, (1,)).reshape(NCHIP, PROWS, 128), CHIPS))
+    coefficients = coefficients_of(arrived, high, low)
     buf = direct(
         correct_projection,
-        f32(NCHIP * PROWS, 128),
+        hbm(F32, NCHIP * PROWS, 128),
         (coefficients, cross_high, cross_low, first),
         scratch=rows_pair,
         flops=2 * 10**9,
@@ -530,16 +516,9 @@
         flops=2 * 10**9,
         size=7 * mega,
     )
-    arrived = after(middle, after(in_vmem(first_high), exchange(buf.reshape(NCHIP, PROWS, 128), CHIPS), ()), ())
-    found = direct(
-        solve_own,
-        f32(NCHIP, PROWS, 128),
-        (arrived, first_high, first_low),
-        scratch=[pltpu.VMEM((PROWS, 128), F32)],
-        flops=10**8,
-        size=5 * mega,
-    )
-    coefficients = exchange(found, CHIPS).reshape(NCHIP * PROWS, 128)
+    high, low = factors_of(1)
+    arrived = after(middle, after(high, exchange(buf.reshape(NCHIP, PROWS, 128), CHIPS)), ())
+    coefficients = coefficients_of(arrived, high, low)
     finished = direct(
         update_last,
         f32(2 * NCOL, 32, 512),

time: 290 us -> 288 us (level)
  Pallas kernels: 56.3 us -> 67.2 us
  waiting for transfers between devices: 71.9 us -> 61.8 us
  local copies, waits for them, and re-layouts: 9.35 us -> 6.03 us
    pallas_call x15 -> x12, Pallas kernels: 38.7 us -> 46.8 us  [run(): return built(*operands) if core is None else built(core, *operands)]
    all_to_all x4, waiting for transfers between devices: 69.5 us -> 61.8 us  [exchange(): return lax.all_to_all(value, axes, 0, 0, tiled=True)]
    unnamed x34 -> x30, local copies, waits for them, and re-layouts: 9.35 us -> 6.03 us
  transfers between devices with their start and end apart: 8 -> 6, of which waited for: 6 -> 4; matrix products, arithmetic and copies ran while one was open for 0% -> 0% of each run, Pallas kernels for 14% -> 16%
where the time goes in v5:
time: 288 us; the launch traced here: 287 us
  blocking collectives  127 us (44%)
  Pallas kernels  67.2 us (23%)
  waiting for transfers between devices  61.8 us (21%)
  starting transfers between devices  24.5 us (9%)
  local copies, waits for them, and re-layouts  6.03 us (2%)
    all_to_all x4, blocking collectives, exchange(): return lax.all_to_all(value, axes, 0, 0, tiled=True)  127 us
    all_to_all x4, waiting for transfers between devices, exchange(): return lax.all_to_all(value, axes, 0, 0, tiled=True)  61.8 us
    pallas_call x12, Pallas kernels, run(): return built(*operands) if core is None else built(core, *operands)  46.8 us
    all_to_all x4, starting transfers between devices, exchange(): return lax.all_to_all(value, axes, 0, 0, tiled=True)  24.4 us
    pallas_call x6, Pallas kernels, direct(): pl.pallas_call(kernel, out_shape=out_shape, in_specs=[VMEM] * len(operand...  20.4 us
    unnamed x30, local copies, waits for them, and re-layouts  6.03 us
  transfers between devices with their start and end apart: 6, of which 4 were waited for; matrix products, arithmetic and copies ran while one was open for 0% of the time, Pallas kernels for 16%

profile of v5, /device:TPU:0, one launch (start us, length us, event | category | flops | bytes accessed | tf_op | source)
XLA Modules:
  0.0 286.6 jit_solution(8244532048360705319)
XLA Ops:
  0.0 2.3 shard_map.28
  2.3 58.9 %all_to_all.40.after_ref.w_ref = f32[16,4,32,512]{3,2,1,0:T(8,128)S(1)} all-to-all(f32[16,4,32,512]{3,2,1,0:T(8,128)S(1)} %shard_map.28), channel_id=1, replica_groups=mesh['y'=4,'xl'=2,'core'=2,'z'=4,'xh'=2] {'core','z','xh'}, dimensions={0} | all-to-all | bytes 8388608 | tf_op jit(solution)/shard_map/all_to_all | solution.py:388
  61.3 5.4 %shard_map.30 = (f32[6656,128]{1,0:T(8,128)}, f32[16,4,32,512]{3,2,1,0:T(8,128)}) custom-call(f32[16,4,32,512]{3,2,1,0:T(8,128)S(1)} %all_to_all.40.after_ref.w_ref, f32[64,32,128]{2,1,0:T(8,128)S(1)} %shard_map.29.e_ref), custom_call_target="tpu_custom_call" | custom-call | flops 4000000000 | bytes 6291456 | tf_op jit(solution)/shard_map/pallas_call | solution.py:368
  66.8 7.0 %all-to-all-start.1 = ((f32[64,104,128]{2,1,0:T(8,128)}), f32[64,104,128]{2,1,0:T(8,128)S(1)}, u32[]{:S(2)}, u32[]{:S(2)}) async-start(f32[64,104,128]{2,1,0:T(8,128)} %bitcast.17), calls=%async_computation.1 | async-start | bytes 6815744 | tf_op jit(solution)/shard_map/all_to_all | solution.py:388
  73.9 42.8 %all-to-all-done.1.buf_ref = f32[64,104,128]{2,1,0:T(8,128)S(1)} async-done(((f32[64,104,128]{2,1,0:T(8,128)}), f32[64,104,128]{2,1,0:T(8,128)S(1)}, u32[]{:S(2)}, u32[]{:S(2)}) %all-to-all-start.1) | async-done | bytes 3407904 | tf_op jit(solution)/shard_map/all_to_all | solution.py:388
  116.7 2.3 shard_map.31
  119.0 6.0 %all-to-all-start.2 = ((f32[64,72,128]{2,1,0:T(8,128)}), f32[64,72,128]{2,1,0:T(8,128)S(1)}, u32[]{:S(2)}, u32[]{:S(2)}) async-start(f32[64,72,128]{2,1,0:T(8,128)} %get-tuple-element.26), calls=%async_computation.2 | async-start | bytes 4718592 | tf_op jit(solution)/shard_map/all_to_all | solution.py:388
  125.1 21.3 %shard_map.32 = (bf16[4,256,1024]{2,1,0:T(8,128)(2,1)}, bf16[4,256,1024]{2,1,0:T(8,128)(2,1)}, bf16[4,256,1024]{2,1,0:T(8,128)(2,1)}, bf16[4,256,1024]{2,1,0:T(8...) custom-call(s32[1]{0:T(128)} %bitcast.core_ref, ...), custom_call_target="tpu_custom_call" | custom-call | flops 10000000000 | bytes 25165824 | tf_op jit(solution)/shard_map/pallas_call | solution.py:364
  146.4 11.1 %all-to-all-done.2.in_ref = f32[64,72,128]{2,1,0:T(8,128)S(1)} async-done(((f32[64,72,128]{2,1,0:T(8,128)}), f32[64,72,128]{2,1,0:T(8,128)S(1)}, u32[]{:S(2)}, u32[]{:S(2)}) %all-to-all-start.2) | async-done | bytes 2359328 | tf_op jit(solution)/shard_map/all_to_all | solution.py:388
  157.5 5.6 %all-to-all-start.3 = ((f32[64,32,128]{2,1,0:T(8,128)}), f32[64,32,128]{2,1,0:T(8,128)S(1)}, u32[]{:S(2)}, u32[]{:S(2)}) async-start(f32[64,32,128]{2,1,0:T(8,128)} %bitcast.16), calls=%async_computation.3 | async-start | bytes 2097152 | tf_op jit(solution)/shard_map/all_to_all | solution.py:388
  164.7 1.6 copy-done.2
  167.5 9.7 %shard_map.34 = (bf16[10,256,256]{2,1,0:T(8,128)(2,1)}, bf16[10,256,256]{2,1,0:T(8,128)(2,1)}) custom-call(s32[1]{0:T(128)} %bitcast.core_ref, f32[4608,128]{1,0:T(8,128)S(1)} %bitcast.10, f32[4608,128]{1,0:T(8,128)} %collective-permute-done.1.sib_ref, bf16[1024,1024]{1,0:T(8,128)(2,1)S(1)} %copy-done, bf16[1024,1024]{1,0:T(8,128)(2,1)S(1)} %copy-done.2, ...), custom_call_target="tpu_custom_call" | custom-call | tf_op jit(solution)/shard_map/pallas_call | solution.py:364
  177.3 4.8 %all-to-all-done.3.in_ref = f32[64,32,128]{2,1,0:T(8,128)S(1)} async-done(((f32[64,32,128]{2,1,0:T(8,128)}), f32[64,32,128]{2,1,0:T(8,128)S(1)}, u32[]{:S(2)}, u32[]{:S(2)}) %all-to-all-start.3) | async-done | bytes 1048608 | tf_op jit(solution)/shard_map/all_to_all | solution.py:388
  182.0 3.3 %shard_map.37 = f32[64,32,128]{2,1,0:T(8,128)S(1)} custom-call(f32[64,32,128]{2,1,0:T(8,128)S(1)} %shard_map.36.buf_ref, bf16[10,256,256]{2,1,0:T(8,128)(2,1)} %get-tuple-element.30.after_ref.high_from, bf16[10,256,256]{2,1,0:T(8,128)(2,1)} %get-tuple-element.31.low_from), custom_call_target="tpu_custom_call" | custom-call | flops 100000000 | bytes 5242880 | tf_op jit(solution)/shard_map/pallas_call | solution.py:368
  185.3 23.7 %all_to_all.41 = f32[64,32,128]{2,1,0:T(8,128)S(1)} all-to-all(f32[64,32,128]{2,1,0:T(8,128)S(1)} %shard_map.37), channel_id=1, replica_groups=mesh['y'=4,'xl'=2,'core'=2,'z'=4,'xh'=2] {'y','xl','z','xh'}, dimensions={0} | all-to-all | bytes 2097152 | tf_op jit(solution)/shard_map/all_to_all | solution.py:388
  209.0 3.9 %shard_map.40 = f32[2048,128]{1,0:T(8,128)} custom-call(f32[2048,128]{1,0:T(8,128)S(1)} %bitcast.12, bf16[1024,1024]{1,0:T(8,128)(2,1)S(1)} %copy-done.1, bf16[1024,1024]{1,0:T(8,128)(2,1)S(1)} %copy-done.3, f32[256,1024]{1,0:T(8,128)S(1)} %copy-done.5), custom_call_target="tpu_custom_call" | custom-call | flops 2000000000 | bytes 7340032 | tf_op jit(solution)/shard_map/pallas_call | solution.py:368
  212.9 5.7 %all-to-all-start.5 = ((f32[64,32,128]{2,1,0:T(8,128)}), f32[64,32,128]{2,1,0:T(8,128)S(1)}, u32[]{:S(2)}, u32[]{:S(2)}) async-start(f32[64,32,128]{2,1,0:T(8,128)} %bitcast.18), calls=%async_computation.5 | async-start | bytes 2097152 | tf_op jit(solution)/shard_map/all_to_all | solution.py:388
  218.7 9.9 %shard_map.39 = (bf16[10,256,256]{2,1,0:T(8,128)(2,1)}, bf16[10,256,256]{2,1,0:T(8,128)(2,1)}) custom-call(s32[1]{0:T(128)} %bitcast.core_ref, f32[4608,128]{1,0:T(8,128)S(1)} %bitcast.11, f32[4608,128]{1,0:T(8,128)} %collective-permute-done.1.sib_ref), custom_call_target="tpu_custom_call" | custom-call | tf_op jit(solution)/shard_map/pallas_call | solution.py:364
  230.2 2.3 shard_map.38.after_ref.x_ref
  232.4 3.1 %all-to-all-done.5.in_ref = f32[64,32,128]{2,1,0:T(8,128)S(1)} async-done(((f32[64,32,128]{2,1,0:T(8,128)}), f32[64,32,128]{2,1,0:T(8,128)S(1)}, u32[]{:S(2)}, u32[]{:S(2)}) %all-to-all-start.5) | async-done | bytes 1048608 | tf_op jit(solution)/shard_map/all_to_all | solution.py:388
  235.6 3.3 %shard_map.43 = f32[64,32,128]{2,1,0:T(8,128)S(1)} custom-call(f32[64,32,128]{2,1,0:T(8,128)S(1)} %shard_map.42.buf_ref, bf16[10,256,256]{2,1,0:T(8,128)(2,1)} %get-tuple-element.35.after_ref.high_from, bf16[10,256,256]{2,1,0:T(8,128)(2,1)} %get-tuple-element.36.low_from), custom_call_target="tpu_custom_call" | custom-call | flops 100000000 | bytes 5242880 | tf_op jit(solution)/shard_map/pallas_call | solution.py:368
  238.9 23.4 %all_to_all.42 = f32[64,32,128]{2,1,0:T(8,128)S(1)} all-to-all(f32[64,32,128]{2,1,0:T(8,128)S(1)} %shard_map.43), channel_id=1, replica_groups=mesh['y'=4,'xl'=2,'core'=2,'z'=4,'xh'=2] {'y','xl','z','xh'}, dimensions={0} | all-to-all | bytes 2097152 | tf_op jit(solution)/shard_map/all_to_all | solution.py:388
  262.3 2.3 shard_map.44
  264.6 20.9 %all_to_all.43.in_ref = f32[16,32,512]{2,1,0:T(8,128)S(1)} all-to-all(f32[16,32,512]{2,1,0:T(8,128)S(1)} %shard_map.44), channel_id=1, replica_groups=mesh['y'=4,'xl'=2,'core'=2,'z'=4,'xh'=2] {'core','z','xh'}, dimensions={0} | all-to-all | bytes 2097152 | tf_op jit(solution)/shard_map/all_to_all | solution.py:388
  (40 shorter events, 5.8 us)
Async XLA Ops:
  2.3 59.0 %copy-start.8 = (f32[4,65536]{1,0:T(4,128)S(1)}, f32[4,65536]{1,0:T(4,128)}, u32[]{:S(2)}) copy-start(f32[4,65536]{1,0:T(4,128)} %e_ref.1) | copy-start | bytes 3145732
  66.8 50.0 %all-to-all-start.1 = ((f32[64,104,128]{2,1,0:T(8,128)}), f32[64,104,128]{2,1,0:T(8,128)S(1)}, u32[]{:S(2)}, u32[]{:S(2)}) async-start(f32[64,104,128]{2,1,0:T(8,128)} %bitcast.17), calls=%async_computation.1 | async-start | bytes 6815744 | tf_op jit(solution)/shard_map/all_to_all | solution.py:388
  73.8 51.3 %collective-permute-start = (f32[16,4,32,512]{3,2,1,0:T(8,128)}, f32[16,4,32,512]{3,2,1,0:T(8,128)}, u32[]{:S(2)}, u32[]{:S(2)}) collective-permute-start(f32[16,4,32,512]{3,2,1,0:T(8,128)} %get-tuple-element.22.mine_ref), channel_id=1, source_target_pairs={{0,8},{8,0},{1,9},{9,1},{2,10},{10,2},{3,11},{11,3},{4,12},{12,4},... | collective-permute-start | bytes 12582920 | tf_op jit(solution)/shard_map/ppermute | solution.py:430
  119.0 6.1 %copy-start.9 = (f32[64,32,128]{2,1,0:T(8,128)S(1)}, f32[64,32,128]{2,1,0:T(8,128)}, u32[]{:S(2)}) copy-start(f32[64,32,128]{2,1,0:T(8,128)} %get-tuple-element.24) | copy-start | bytes 3145732
  119.0 38.4 %all-to-all-start.2 = ((f32[64,72,128]{2,1,0:T(8,128)}), f32[64,72,128]{2,1,0:T(8,128)S(1)}, u32[]{:S(2)}, u32[]{:S(2)}) async-start(f32[64,72,128]{2,1,0:T(8,128)} %get-tuple-element.26), calls=%async_computation.2 | async-start | bytes 4718592 | tf_op jit(solution)/shard_map/all_to_all | solution.py:388
  157.5 5.6 %collective-permute-start.1 = (f32[4608,128]{1,0:T(8,128)S(1)}, f32[4608,128]{1,0:T(8,128)}, u32[]{:S(2)}, u32[]{:S(2)}) collective-permute-start(f32[4608,128]{1,0:T(8,128)S(1)} %bitcast.8), channel_id=1, source_target_pairs={{0,8},{8,0},{1,9},{9,1},{2,10},{10,2},{3,11},{11,3},{4,12},{12,4},... | collective-permute-start | bytes 7077896 | tf_op jit(solution)/shard_map/ppermute | solution.py:470
  157.5 24.6 %all-to-all-start.3 = ((f32[64,32,128]{2,1,0:T(8,128)}), f32[64,32,128]{2,1,0:T(8,128)S(1)}, u32[]{:S(2)}, u32[]{:S(2)}) async-start(f32[64,32,128]{2,1,0:T(8,128)} %bitcast.16), calls=%async_computation.3 | async-start | bytes 2097152 | tf_op jit(solution)/shard_map/all_to_all | solution.py:388
  163.1 1.6 copy-start
  164.7 1.6 copy-start.2
  166.3 1.2 copy-start.4
  182.0 27.0 %copy-start.1 = (bf16[1024,1024]{1,0:T(8,128)(2,1)S(1)}, bf16[1024,1024]{1,0:T(8,128)(2,1)}, u32[]{:S(2)}) copy-start(bf16[1024,1024]{1,0:T(8,128)(2,1)} %get-tuple-element.27.refs_0_.gh_ref) | copy-start | bytes 6291460
  182.0 27.0 %copy-start.3 = (bf16[1024,1024]{1,0:T(8,128)(2,1)S(1)}, bf16[1024,1024]{1,0:T(8,128)(2,1)}, u32[]{:S(2)}) copy-start(bf16[1024,1024]{1,0:T(8,128)(2,1)} %get-tuple-element.28.refs_1_.gl_ref) | copy-start | bytes 6291460
  182.0 27.0 %copy-start.5 = (f32[256,1024]{1,0:T(8,128)S(1)}, f32[256,1024]{1,0:T(8,128)}, u32[]{:S(2)}) copy-start(f32[256,1024]{1,0:T(8,128)} %get-tuple-element.29.refs_2_.first_ref) | copy-start | bytes 3145732
  209.0 3.9 %copy-start.6 = (f32[64,32,128]{2,1,0:T(8,128)}, f32[64,32,128]{2,1,0:T(8,128)S(1)}, u32[]{:S(2)}) copy-start(f32[64,32,128]{2,1,0:T(8,128)S(1)} %all_to_all.41) | copy-start | bytes 3145732
  212.9 22.7 %all-to-all-start.5 = ((f32[64,32,128]{2,1,0:T(8,128)}), f32[64,32,128]{2,1,0:T(8,128)S(1)}, u32[]{:S(2)}, u32[]{:S(2)}) async-start(f32[64,32,128]{2,1,0:T(8,128)} %bitcast.18), calls=%async_computation.5 | async-start | bytes 2097152 | tf_op jit(solution)/shard_map/all_to_all | solution.py:388
  218.6 9.9 %copy-start.7 = (f32[64,32,128]{2,1,0:T(8,128)S(1)}, f32[64,32,128]{2,1,0:T(8,128)}, u32[]{:S(2)}) copy-start(f32[64,32,128]{2,1,0:T(8,128)} %copy-done.6) | copy-start | bytes 3145732
  218.6 9.9 %copy-start.12 = (bf16[4,256,1024]{2,1,0:T(8,128)(2,1)S(1)}, bf16[4,256,1024]{2,1,0:T(8,128)(2,1)}, u32[]{:S(2)}) copy-start(bf16[4,256,1024]{2,1,0:T(8,128)(2,1)} %get-tuple-element.32.high_ref) | copy-start | bytes 6291460
  218.6 9.9 %copy-start.14 = (f32[256,1024]{1,0:T(8,128)S(1)}, f32[256,1024]{1,0:T(8,128)}, u32[]{:S(2)}) copy-start(f32[256,1024]{1,0:T(8,128)} %get-tuple-element.34.x_ref) | copy-start | bytes 3145732
  228.6 1.6 copy-start.13
  235.6 26.7 %copy-start.10 = (bf16[4,256,1024]{2,1,0:T(8,128)(2,1)S(1)}, bf16[4,256,1024]{2,1,0:T(8,128)(2,1)}, u32[]{:S(2)}) copy-start(bf16[4,256,1024]{2,1,0:T(8,128)(2,1)} %get-tuple-element.37.high_ref) | copy-start | bytes 6291460
  235.6 26.7 %copy-start.11 = (bf16[4,256,1024]{2,1,0:T(8,128)(2,1)S(1)}, bf16[4,256,1024]{2,1,0:T(8,128)(2,1)}, u32[]{:S(2)}) copy-start(bf16[4,256,1024]{2,1,0:T(8,128)(2,1)} %get-tuple-element.38.low_ref) | copy-start | bytes 6291460

commit v6 on v5

--- a/solution.py
+++ b/solution.py
@@ -103,12 +103,13 @@
 def inner_products(w_ref, e_ref, out_ref, kept_ref, high_ref, low_ref, buf_ref, done):
     keep = pltpu.make_async_copy(w_ref, kept_ref, done.at[0])
     keep.start()
-    for q in range(NCHIP):
-        buf_ref[q * STEP + GROWS : q * STEP + STEP, :] = e_ref[q]
-    first = PIECES[0, GROUP - 1, 0][0] // GROWS * STEP
-    parts = (slice(0, first), slice(first, NCHIP * STEP))
+    pieces = pltpu.make_async_copy(e_ref, out_ref.at[:, GROWS:, :], done.at[3])
+    pieces.start()
+    first = PIECES[0, GROUP - 1, 0][0] // GROWS
+    parts = (slice(0, first), slice(first, NCHIP))
     sends = [
-        pltpu.make_async_copy(buf_ref.at[part], out_ref.at[part], done.at[1 + at]) for at, part in enumerate(parts)
+        pltpu.make_async_copy(buf_ref.at[part], out_ref.at[part, :GROWS, :], done.at[1 + at])
+        for at, part in enumerate(parts)
     ]
     for j in range(GROUP):
         high_ref[j], low_ref[j] = split(whole_block(w_ref[:, j]))
@@ -118,15 +119,14 @@
             value = dot3((high_ref[i], low_ref[i]), (high_ref[j], low_ref[j]), NT)
             for half in range(2):
                 at, rows = PIECES[i, j, half]
-                done = 0
-                while done < rows:
-                    chip, offset = divmod(at + done, GROWS)
-                    take = min(rows - done, GROWS - offset)
-                    start = chip * STEP + offset
-                    buf_ref[start : start + take, :] = value[done : done + take, half * 128 : half * 128 + 128]
-                    done += take
+                at_row = 0
+                while at_row < rows:
+                    chip, offset = divmod(at + at_row, GROWS)
+                    take = min(rows - at_row, GROWS - offset)
+                    buf_ref[chip, offset : offset + take, :] = value[at_row : at_row + take, half * 128 : half * 128 + 128]
+                    at_row += take
     sends[1].start()
-    for copy in (keep, *sends):
+    for copy in (keep, pieces, *sends):
         copy.wait()
 
 
@@ -419,16 +419,16 @@
     )
     buf, kept = direct(
         inner_products,
-        (hbm(F32, NCHIP * STEP, 128), hbm(F32, 2 * NCOL, GROUP, 32, 512)),
+        (hbm(F32, NCHIP, STEP, 128), hbm(F32, 2 * NCOL, GROUP, 32, 512)),
         (mine, pieces),
         scratch=[pltpu.VMEM((GROUP, NB, 1024), BF16)] * 2
-        + [pltpu.VMEM((NCHIP * STEP, 128), F32), pltpu.SemaphoreType.DMA((3,))],
+        + [pltpu.VMEM((NCHIP, GROWS, 128), F32), pltpu.SemaphoreType.DMA((4,))],
         out_specs=(HBM, HBM),
         flops=4 * 10**9,
         size=6 * mega,
     )
     other = lax.ppermute(kept, "core", SWAP)
-    arrived = exchange(buf.reshape(NCHIP, STEP, 128), CHIPS)
+    arrived = exchange(buf, CHIPS)
 
     part, spread = run(
         sum_products,

time: 288 us -> 287 us (level)
  no operation moved by 1% of the time
where the time goes in v6:
time: 287 us
  blocking collectives  127 us (44%)
  Pallas kernels  67.1 us (23%)
  waiting for transfers between devices  61.8 us (22%)
  starting transfers between devices  24.5 us (9%)
  local copies, waits for them, and re-layouts  6.03 us (2%)
    all_to_all x4, blocking collectives, exchange(): return lax.all_to_all(value, axes, 0, 0, tiled=True)  127 us
    all_to_all x4, waiting for transfers between devices, exchange(): return lax.all_to_all(value, axes, 0, 0, tiled=True)  61.8 us
    pallas_call x12, Pallas kernels, run(): return built(*operands) if core is None else built(core, *operands)  46.8 us
    all_to_all x4, starting transfers between devices, exchange(): return lax.all_to_all(value, axes, 0, 0, tiled=True)  24.4 us
    pallas_call x6, Pallas kernels, direct(): pl.pallas_call(kernel, out_shape=out_shape, in_specs=[VMEM] * len(operand...  20.3 us
    unnamed x30, local copies, waits for them, and re-layouts  6.03 us
  transfers between devices with their start and end apart: 6, of which 4 were waited for; matrix products, arithmetic and copies ran while one was open for 0% of the time, Pallas kernels for 16%

profile of v6, /device:TPU:0, one launch (start us, length us, event | category | flops | bytes accessed | tf_op | source)
XLA Modules:
  0.0 286.5 jit_solution(4453053477523339007)
XLA Ops:
  0.0 2.3 shard_map.28
  2.3 58.9 %all_to_all.40.after_ref.w_ref = f32[16,4,32,512]{3,2,1,0:T(8,128)S(1)} all-to-all(f32[16,4,32,512]{3,2,1,0:T(8,128)S(1)} %shard_map.28), channel_id=1, replica_groups=mesh['y'=4,'xl'=2,'core'=2,'z'=4,'xh'=2] {'core','z','xh'}, dimensions={0} | all-to-all | bytes 8388608 | tf_op jit(solution)/shard_map/all_to_all | solution.py:388
  61.3 5.3 %shard_map.30 = (f32[64,104,128]{2,1,0:T(8,128)}, f32[16,4,32,512]{3,2,1,0:T(8,128)}) custom-call(f32[16,4,32,512]{3,2,1,0:T(8,128)S(1)} %all_to_all.40.after_ref.w_ref, f32[64,32,128]{2,1,0:T(8,128)S(1)} %shard_map.29.e_ref), custom_call_target="tpu_custom_call" | custom-call | flops 4000000000 | bytes 6291456 | tf_op jit(solution)/shard_map/pallas_call | solution.py:368
  66.6 7.0 %all-to-all-start.1 = ((f32[64,104,128]{2,1,0:T(8,128)}), f32[64,104,128]{2,1,0:T(8,128)S(1)}, u32[]{:S(2)}, u32[]{:S(2)}) async-start(f32[64,104,128]{2,1,0:T(8,128)} %get-tuple-element.23), calls=%async_computation.1 | async-start | bytes 6815744 | tf_op jit(solution)/shard_map/all_to_all | solution.py:388
  73.8 42.8 %all-to-all-done.1.buf_ref = f32[64,104,128]{2,1,0:T(8,128)S(1)} async-done(((f32[64,104,128]{2,1,0:T(8,128)}), f32[64,104,128]{2,1,0:T(8,128)S(1)}, u32[]{:S(2)}, u32[]{:S(2)}) %all-to-all-start.1) | async-done | bytes 3407904 | tf_op jit(solution)/shard_map/all_to_all | solution.py:388
  116.6 2.3 shard_map.31
  118.9 6.0 %all-to-all-start.2 = ((f32[64,72,128]{2,1,0:T(8,128)}), f32[64,72,128]{2,1,0:T(8,128)S(1)}, u32[]{:S(2)}, u32[]{:S(2)}) async-start(f32[64,72,128]{2,1,0:T(8,128)} %get-tuple-element.26), calls=%async_computation.2 | async-start | bytes 4718592 | tf_op jit(solution)/shard_map/all_to_all | solution.py:388
  125.0 21.3 %shard_map.32 = (bf16[4,256,1024]{2,1,0:T(8,128)(2,1)}, bf16[4,256,1024]{2,1,0:T(8,128)(2,1)}, bf16[4,256,1024]{2,1,0:T(8,128)(2,1)}, bf16[4,256,1024]{2,1,0:T(8...) custom-call(s32[1]{0:T(128)} %bitcast.core_ref, ...), custom_call_target="tpu_custom_call" | custom-call | flops 10000000000 | bytes 25165824 | tf_op jit(solution)/shard_map/pallas_call | solution.py:364
  146.3 11.1 %all-to-all-done.2.in_ref = f32[64,72,128]{2,1,0:T(8,128)S(1)} async-done(((f32[64,72,128]{2,1,0:T(8,128)}), f32[64,72,128]{2,1,0:T(8,128)S(1)}, u32[]{:S(2)}, u32[]{:S(2)}) %all-to-all-start.2) | async-done | bytes 2359328 | tf_op jit(solution)/shard_map/all_to_all | solution.py:388
  157.4 5.6 %all-to-all-start.3 = ((f32[64,32,128]{2,1,0:T(8,128)}), f32[64,32,128]{2,1,0:T(8,128)S(1)}, u32[]{:S(2)}, u32[]{:S(2)}) async-start(f32[64,32,128]{2,1,0:T(8,128)} %bitcast.15), calls=%async_computation.3 | async-start | bytes 2097152 | tf_op jit(solution)/shard_map/all_to_all | solution.py:388
  164.6 1.6 copy-done.2
  167.4 9.7 %shard_map.34 = (bf16[10,256,256]{2,1,0:T(8,128)(2,1)}, bf16[10,256,256]{2,1,0:T(8,128)(2,1)}) custom-call(s32[1]{0:T(128)} %bitcast.core_ref, f32[4608,128]{1,0:T(8,128)S(1)} %bitcast.9, f32[4608,128]{1,0:T(8,128)} %collective-permute-done.1.sib_ref, bf16[1024,1024]{1,0:T(8,128)(2,1)S(1)} %copy-done, bf16[1024,1024]{1,0:T(8,128)(2,1)S(1)} %copy-done.2, ...), custom_call_target="tpu_custom_call" | custom-call | tf_op jit(solution)/shard_map/pallas_call | solution.py:364
  177.2 4.8 %all-to-all-done.3.in_ref = f32[64,32,128]{2,1,0:T(8,128)S(1)} async-done(((f32[64,32,128]{2,1,0:T(8,128)}), f32[64,32,128]{2,1,0:T(8,128)S(1)}, u32[]{:S(2)}, u32[]{:S(2)}) %all-to-all-start.3) | async-done | bytes 1048608 | tf_op jit(solution)/shard_map/all_to_all | solution.py:388
  181.9 3.3 %shard_map.37 = f32[64,32,128]{2,1,0:T(8,128)S(1)} custom-call(f32[64,32,128]{2,1,0:T(8,128)S(1)} %shard_map.36.buf_ref, bf16[10,256,256]{2,1,0:T(8,128)(2,1)} %get-tuple-element.30.after_ref.high_from, bf16[10,256,256]{2,1,0:T(8,128)(2,1)} %get-tuple-element.31.low_from), custom_call_target="tpu_custom_call" | custom-call | flops 100000000 | bytes 5242880 | tf_op jit(solution)/shard_map/pallas_call | solution.py:368
  185.2 23.7 %all_to_all.41 = f32[64,32,128]{2,1,0:T(8,128)S(1)} all-to-all(f32[64,32,128]{2,1,0:T(8,128)S(1)} %shard_map.37), channel_id=1, replica_groups=mesh['y'=4,'xl'=2,'core'=2,'z'=4,'xh'=2] {'y','xl','z','xh'}, dimensions={0} | all-to-all | bytes 2097152 | tf_op jit(solution)/shard_map/all_to_all | solution.py:388
  208.9 3.9 %shard_map.40 = f32[2048,128]{1,0:T(8,128)} custom-call(f32[2048,128]{1,0:T(8,128)S(1)} %bitcast.11, bf16[1024,1024]{1,0:T(8,128)(2,1)S(1)} %copy-done.1, bf16[1024,1024]{1,0:T(8,128)(2,1)S(1)} %copy-done.3, f32[256,1024]{1,0:T(8,128)S(1)} %copy-done.5), custom_call_target="tpu_custom_call" | custom-call | flops 2000000000 | bytes 7340032 | tf_op jit(solution)/shard_map/pallas_call | solution.py:368
  212.8 5.7 %all-to-all-start.5 = ((f32[64,32,128]{2,1,0:T(8,128)}), f32[64,32,128]{2,1,0:T(8,128)S(1)}, u32[]{:S(2)}, u32[]{:S(2)}) async-start(f32[64,32,128]{2,1,0:T(8,128)} %bitcast.16), calls=%async_computation.5 | async-start | bytes 2097152 | tf_op jit(solution)/shard_map/all_to_all | solution.py:388
  218.5 9.9 %shard_map.39 = (bf16[10,256,256]{2,1,0:T(8,128)(2,1)}, bf16[10,256,256]{2,1,0:T(8,128)(2,1)}) custom-call(s32[1]{0:T(128)} %bitcast.core_ref, f32[4608,128]{1,0:T(8,128)S(1)} %bitcast.10, f32[4608,128]{1,0:T(8,128)} %collective-permute-done.1.sib_ref), custom_call_target="tpu_custom_call" | custom-call | tf_op jit(solution)/shard_map/pallas_call | solution.py:364
  230.0 2.3 shard_map.38.after_ref.x_ref
  232.3 3.2 %all-to-all-done.5.in_ref = f32[64,32,128]{2,1,0:T(8,128)S(1)} async-done(((f32[64,32,128]{2,1,0:T(8,128)}), f32[64,32,128]{2,1,0:T(8,128)S(1)}, u32[]{:S(2)}, u32[]{:S(2)}) %all-to-all-start.5) | async-done | bytes 1048608 | tf_op jit(solution)/shard_map/all_to_all | solution.py:388
  235.5 3.3 %shard_map.43 = f32[64,32,128]{2,1,0:T(8,128)S(1)} custom-call(f32[64,32,128]{2,1,0:T(8,128)S(1)} %shard_map.42.buf_ref, bf16[10,256,256]{2,1,0:T(8,128)(2,1)} %get-tuple-element.35.after_ref.high_from, bf16[10,256,256]{2,1,0:T(8,128)(2,1)} %get-tuple-element.36.low_from), custom_call_target="tpu_custom_call" | custom-call | flops 100000000 | bytes 5242880 | tf_op jit(solution)/shard_map/pallas_call | solution.py:368
  238.8 23.4 %all_to_all.42 = f32[64,32,128]{2,1,0:T(8,128)S(1)} all-to-all(f32[64,32,128]{2,1,0:T(8,128)S(1)} %shard_map.43), channel_id=1, replica_groups=mesh['y'=4,'xl'=2,'core'=2,'z'=4,'xh'=2] {'y','xl','z','xh'}, dimensions={0} | all-to-all | bytes 2097152 | tf_op jit(solution)/shard_map/all_to_all | solution.py:388
  262.2 2.3 shard_map.44
  264.5 20.9 %all_to_all.43.in_ref = f32[16,32,512]{2,1,0:T(8,128)S(1)} all-to-all(f32[16,32,512]{2,1,0:T(8,128)S(1)} %shard_map.44), channel_id=1, replica_groups=mesh['y'=4,'xl'=2,'core'=2,'z'=4,'xh'=2] {'core','z','xh'}, dimensions={0} | all-to-all | bytes 2097152 | tf_op jit(solution)/shard_map/all_to_all | solution.py:388
  (40 shorter events, 5.8 us)
Async XLA Ops:
  2.3 59.0 %copy-start.8 = (f32[4,65536]{1,0:T(4,128)S(1)}, f32[4,65536]{1,0:T(4,128)}, u32[]{:S(2)}) copy-start(f32[4,65536]{1,0:T(4,128)} %e_ref.1) | copy-start | bytes 3145732
  66.6 50.0 %all-to-all-start.1 = ((f32[64,104,128]{2,1,0:T(8,128)}), f32[64,104,128]{2,1,0:T(8,128)S(1)}, u32[]{:S(2)}, u32[]{:S(2)}) async-start(f32[64,104,128]{2,1,0:T(8,128)} %get-tuple-element.23), calls=%async_computation.1 | async-start | bytes 6815744 | tf_op jit(solution)/shard_map/all_to_all | solution.py:388
  73.7 51.3 %collective-permute-start = (f32[16,4,32,512]{3,2,1,0:T(8,128)}, f32[16,4,32,512]{3,2,1,0:T(8,128)}, u32[]{:S(2)}, u32[]{:S(2)}) collective-permute-start(f32[16,4,32,512]{3,2,1,0:T(8,128)} %get-tuple-element.22.mine_ref), channel_id=1, source_target_pairs={{0,8},{8,0},{1,9},{9,1},{2,10},{10,2},{3,11},{11,3},{4,12},{12,4},... | collective-permute-start | bytes 12582920 | tf_op jit(solution)/shard_map/ppermute | solution.py:430
  118.9 6.1 %copy-start.9 = (f32[64,32,128]{2,1,0:T(8,128)S(1)}, f32[64,32,128]{2,1,0:T(8,128)}, u32[]{:S(2)}) copy-start(f32[64,32,128]{2,1,0:T(8,128)} %get-tuple-element.24) | copy-start | bytes 3145732
  118.9 38.4 %all-to-all-start.2 = ((f32[64,72,128]{2,1,0:T(8,128)}), f32[64,72,128]{2,1,0:T(8,128)S(1)}, u32[]{:S(2)}, u32[]{:S(2)}) async-start(f32[64,72,128]{2,1,0:T(8,128)} %get-tuple-element.26), calls=%async_computation.2 | async-start | bytes 4718592 | tf_op jit(solution)/shard_map/all_to_all | solution.py:388
  157.4 5.6 %collective-permute-start.1 = (f32[4608,128]{1,0:T(8,128)S(1)}, f32[4608,128]{1,0:T(8,128)}, u32[]{:S(2)}, u32[]{:S(2)}) collective-permute-start(f32[4608,128]{1,0:T(8,128)S(1)} %bitcast.7), channel_id=1, source_target_pairs={{0,8},{8,0},{1,9},{9,1},{2,10},{10,2},{3,11},{11,3},{4,12},{12,4},... | collective-permute-start | bytes 7077896 | tf_op jit(solution)/shard_map/ppermute | solution.py:470
  157.4 24.6 %all-to-all-start.3 = ((f32[64,32,128]{2,1,0:T(8,128)}), f32[64,32,128]{2,1,0:T(8,128)S(1)}, u32[]{:S(2)}, u32[]{:S(2)}) async-start(f32[64,32,128]{2,1,0:T(8,128)} %bitcast.15), calls=%async_computation.3 | async-start | bytes 2097152 | tf_op jit(solution)/shard_map/all_to_all | solution.py:388
  163.0 1.6 copy-start
  164.6 1.6 copy-start.2
  166.2 1.2 copy-start.4
  181.9 27.0 %copy-start.1 = (bf16[1024,1024]{1,0:T(8,128)(2,1)S(1)}, bf16[1024,1024]{1,0:T(8,128)(2,1)}, u32[]{:S(2)}) copy-start(bf16[1024,1024]{1,0:T(8,128)(2,1)} %get-tuple-element.27.refs_0_.gh_ref) | copy-start | bytes 6291460
  181.9 27.0 %copy-start.3 = (bf16[1024,1024]{1,0:T(8,128)(2,1)S(1)}, bf16[1024,1024]{1,0:T(8,128)(2,1)}, u32[]{:S(2)}) copy-start(bf16[1024,1024]{1,0:T(8,128)(2,1)} %get-tuple-element.28.refs_1_.gl_ref) | copy-start | bytes 6291460
  181.9 27.0 %copy-start.5 = (f32[256,1024]{1,0:T(8,128)S(1)}, f32[256,1024]{1,0:T(8,128)}, u32[]{:S(2)}) copy-start(f32[256,1024]{1,0:T(8,128)} %get-tuple-element.29.refs_2_.first_ref) | copy-start | bytes 3145732
  208.9 3.9 %copy-start.6 = (f32[64,32,128]{2,1,0:T(8,128)}, f32[64,32,128]{2,1,0:T(8,128)S(1)}, u32[]{:S(2)}) copy-start(f32[64,32,128]{2,1,0:T(8,128)S(1)} %all_to_all.41) | copy-start | bytes 3145732
  212.8 22.7 %all-to-all-start.5 = ((f32[64,32,128]{2,1,0:T(8,128)}), f32[64,32,128]{2,1,0:T(8,128)S(1)}, u32[]{:S(2)}, u32[]{:S(2)}) async-start(f32[64,32,128]{2,1,0:T(8,128)} %bitcast.16), calls=%async_computation.5 | async-start | bytes 2097152 | tf_op jit(solution)/shard_map/all_to_all | solution.py:388
  218.5 9.9 %copy-start.7 = (f32[64,32,128]{2,1,0:T(8,128)S(1)}, f32[64,32,128]{2,1,0:T(8,128)}, u32[]{:S(2)}) copy-start(f32[64,32,128]{2,1,0:T(8,128)} %copy-done.6) | copy-start | bytes 3145732
  218.5 9.9 %copy-start.12 = (bf16[4,256,1024]{2,1,0:T(8,128)(2,1)S(1)}, bf16[4,256,1024]{2,1,0:T(8,128)(2,1)}, u32[]{:S(2)}) copy-start(bf16[4,256,1024]{2,1,0:T(8,128)(2,1)} %get-tuple-element.32.high_ref) | copy-start | bytes 6291460
  218.5 9.9 %copy-start.14 = (f32[256,1024]{1,0:T(8,128)S(1)}, f32[256,1024]{1,0:T(8,128)}, u32[]{:S(2)}) copy-start(f32[256,1024]{1,0:T(8,128)} %get-tuple-element.34.x_ref) | copy-start | bytes 3145732
  228.4 1.6 copy-start.13
  235.5 26.7 %copy-start.10 = (bf16[4,256,1024]{2,1,0:T(8,128)(2,1)S(1)}, bf16[4,256,1024]{2,1,0:T(8,128)(2,1)}, u32[]{:S(2)}) copy-start(bf16[4,256,1024]{2,1,0:T(8,128)(2,1)} %get-tuple-element.37.high_ref) | copy-start | bytes 6291460
  235.5 26.7 %copy-start.11 = (bf16[4,256,1024]{2,1,0:T(8,128)(2,1)S(1)}, bf16[4,256,1024]{2,1,0:T(8,128)(2,1)}, u32[]{:S(2)}) copy-start(bf16[4,256,1024]{2,1,0:T(8,128)(2,1)} %get-tuple-element.38.low_ref) | copy-start | bytes 6291460
